TPU v7x, 128 devices: a whole 4x4x4 slice. The times are simulated.
128 devices in a mesh: tensor: 4 (over y), dp: 32 (over z, x, core).
Axes of the slice: x: 4, y: 4, z: 4, core: 2. Of those that a mesh axis runs over, the one named last changes fastest.
Arguments:
- gradients: bfloat16 [32, 512, 128, 128], P('dp', 'tensor')
- residual: bfloat16 [32, 512, 128, 128], P('dp', 'tensor'), may hold values from -1.5 to 1.5
- momentum: bfloat16 [512, 128, 128], P('tensor'), may hold values from -6 to 6
- bitmap: int32 [32, 512], P('dp', 'tensor'), may hold values from 0 to 1, as said below
- starts: int32 [4, 32], replicated, may hold values from 0 to 127, as said below
Outputs:
- new_residual: bfloat16 [32, 512, 128, 128], P('dp', 'tensor')
- new_momentum: bfloat16 [512, 128, 128], P('tensor')
Inputs may be any that keep to these rules, and one draw needn't show every extreme that they name: `bitmap`: in each tile shard one bucket of 7 tiles is selected by every replica; the other tiles are selected at random. `starts`: row k holds the first local tile of each of the 32 buckets of tile shard k, rising from 0; a bucket ends where the next begins, the last at 128; every bucket holds 1 to 7 tiles, and one in each row holds exactly 7.
All inputs are finite; a program needn't handle non-finite values.
Results may differ from a plain program's by a relative error of at most 0.015.
Values may be sent and summed in bfloat16 or wider, within the bound.
No kernel may reach another device: no remote copies, remote signals or barrier semaphores. Data moves between devices by JAX's collectives and lax.ppermute only.
A program may use at most 128 MiB of HBM per device.

v0:
```python
import jax
import jax.numpy as jnp
from jax import lax
from jax.sharding import PartitionSpec as P

MOMENTUM = 0.9
CLIP_LEVEL = 3.0
EPSILON = 1e-06


def bucket_table(starts, tile_count):
    ends = jnp.concatenate(
        [starts[:, 1:], jnp.full((starts.shape[0], 1), tile_count, jnp.int32)], axis=1
    )
    return ends - starts


def shards(gradients, residual, momentum, bitmap, starts):
    buckets = lax.axis_size("dp")
    tile_count = gradients.shape[1]
    tile_size = gradients.shape[2]
    accumulated = gradients[0].astype(jnp.float32) + residual[0].astype(jnp.float32)
    selected = bitmap[0][:, None, None] > 0
    rounded = accumulated.astype(jnp.bfloat16)
    zero_tiles = jnp.zeros_like(rounded)
    new_residual = jnp.where(selected, zero_tiles, rounded)[None]
    outgoing = jnp.where(selected, rounded, zero_tiles)
    bucket_sizes = bucket_table(starts, tile_count)
    bucket_tiles = jnp.sum(bucket_sizes, axis=0)
    shard_index = lax.axis_index("tensor")
    my_starts = lax.dynamic_index_in_dim(starts, shard_index, 0, keepdims=False)
    my_sizes = lax.dynamic_index_in_dim(bucket_sizes, shard_index, 0, keepdims=False)
    local_tiles = jnp.arange(tile_count, dtype=jnp.int32)
    owner_of = jnp.sum((local_tiles[:, None] >= my_starts[None, :]).astype(jnp.int32), axis=1) - 1
    membership = owner_of[:, None] == jnp.arange(buckets, dtype=jnp.int32)[None, :]
    entries = float(tile_size * tile_size)
    capacity = 2 * tile_count // buckets - 1
    slot_index = jnp.arange(capacity, dtype=jnp.int32)
    source_rows = jnp.minimum(my_starts[:, None] + slot_index[None, :], tile_count - 1)
    slot_valid = slot_index[None, :] < my_sizes[:, None]
    packed_tiles = jnp.take(outgoing, source_rows.reshape(-1), axis=0).reshape(
        buckets, capacity, tile_size, tile_size
    )
    packed_tiles = jnp.where(
        slot_valid[:, :, None, None], packed_tiles, jnp.zeros_like(packed_tiles)
    )
    total_tiles = jnp.sum(
        lax.all_to_all(packed_tiles, "dp", split_axis=0, concat_axis=0, tiled=True),
        axis=0,
        dtype=jnp.float32,
    )
    slot_squares = jnp.sum(total_tiles * total_tiles, axis=(1, 2))
    my_bucket = lax.axis_index("dp")
    total_squares = lax.psum(jnp.sum(slot_squares), "tensor")
    bucket_count = lax.dynamic_index_in_dim(bucket_tiles, my_bucket, 0, keepdims=False).astype(
        jnp.float32
    )
    bucket_rms = jnp.sqrt(total_squares / (bucket_count * entries) + EPSILON)
    clip_factor = jnp.minimum(1.0, CLIP_LEVEL / bucket_rms)
    update_tiles = (total_tiles * clip_factor).astype(jnp.bfloat16)
    returned = lax.all_gather(update_tiles, "dp", axis=0, tiled=True)
    offset = jnp.sum(jnp.where(membership, my_starts[None, :], 0), axis=1)
    update_all = jnp.take(returned, owner_of * capacity + local_tiles - offset, axis=0)
    new_momentum = (
        MOMENTUM * momentum.astype(jnp.float32) + update_all.astype(jnp.float32)
    ).astype(jnp.bfloat16)
    return (new_residual, new_momentum)


def solution(mesh):
    return jax.shard_map(
        shards,
        mesh=mesh,
        in_specs=(
            P("dp", "tensor", None, None),
            P("dp", "tensor", None, None),
            P("tensor", None, None),
            P("dp", "tensor"),
            P(),
        ),
        out_specs=(P("dp", "tensor", None, None), P("tensor", None, None)),
        check_vma=False,
    )
```

profile of v0, /device:TPU:1, one launch (start us, length us, event | category | flops | bytes accessed | tf_op | source)
XLA Modules:
  0.0 219.2 jit_solution(5811669039541042357)
XLA Ops:
  7.2 0.8 slice.3
  7.9 0.7 fusion.1
  8.6 0.7 dynamic-slice_bitcast_fusion
  9.3 0.1 add_minimum_fusion
  9.4 0.1 compare_and_fusion
  9.5 0.1 min.22
  9.6 0.7 compare_bitcast_fusion
  10.3 0.1 iota_compare_fusion
  10.3 6.1 %bitcast_select_fusion = bf16[128,128,128]{2,1,0:T(8,128)(2,1)} fusion(pred[128]{0:T(512)(128)(4,1)S(1)} %compare_bitcast_fusion, bf16[1,128,128,128]{3,2,1,0:T(8,128)(2,1)} %param.6, bf16[1,128,128,128]{3,2,1,0:T(8,128)(2,1)} %param.5), kind=kLoop, calls=%fused_computation.6 | loop fusion | flops 10485760 | bytes 12583040 | tf_op jit(solution)/shard_map/jit(_where)/select_n | solution.py:27
  16.5 10.6 %gather_fusion = bf16[224,128,128]{2,1,0:T(8,128)(2,1)} fusion(bf16[128,128,128]{2,1,0:T(8,128)(2,1)} %bitcast_select_fusion, s32[1024]{0:T(1024)S(1)} %pad_clamp_fusion.1), kind=kCustom, calls=%fused_computation | custom fusion | bytes 14680960 | tf_op jit(solution)/shard_map/jit(_take)/gather | solution.py:41
  27.1 6.8 %select_select_fusion = bf16[32,7,128,128]{3,2,1,0:T(8,128)(2,1)} fusion(bf16[32,7,128,128]{3,2,1,0:T(8,128)(2,1)} %bitcast.21, pred[32,7]{1,0:T(8,128)(4,1)S(1)} %compare_and_fusion, pred[32,7]{1,0:T(8,128)(4,1)S(1)} %iota_compare_fusion), kind=kLoop, calls=%fused_computation.5 | loop fusion | flops 7340032 | bytes 14680512 | tf_op jit(solution)/shard_map/jit(_where)/select_n | solution.py:44
  33.9 9.5 %all-to-all-start = ((bf16[32,7,128,128]{3,2,1,0:T(8,128)(2,1)}), bf16[32,7,128,128]{3,2,1,0:T(8,128)(2,1)}, u32[]{:S(2)}, u32[]{:S(2)}) async-start(bf16[32,7,128,128]{3,2,1,0:T(8,128)(2,1)} %select_select_fusion), calls=%async_computation | async-start | bytes 14680064 | tf_op jit(solution)/shard_map/all_to_all | solution.py:48
  43.5 0.6 dynamic_slice.13
  44.7 85.5 %all-to-all-done = bf16[32,7,128,128]{3,2,1,0:T(8,128)(2,1)} async-done(((bf16[32,7,128,128]{3,2,1,0:T(8,128)(2,1)}), bf16[32,7,128,128]{3,2,1,0:T(8,128)(2,1)}, u32[]{:S(2)}, u32[]{:S(2)}) %all-to-all-start) | async-done | bytes 7340064 | tf_op jit(solution)/shard_map/all_to_all | solution.py:48
  130.2 4.9 %convert_reduce_fusion = f32[7,128,128]{2,1,0:T(8,128)S(1)} fusion(bf16[32,7,128,128]{3,2,1,0:T(8,128)(2,1)} %all-to-all-done), kind=kLoop, calls=%fused_computation.2 | loop fusion | flops 7225344 | bytes 7798784 | tf_op jit(solution)/shard_map/reduce_sum | solution.py:47
  135.1 0.7 multiply_reduce_fusion
  135.8 9.3 %psum.7 = f32[]{:T(128)} all-reduce(f32[]{:T(128)} %multiply_reduce_fusion), channel_id=1, replica_groups=mesh['tensor'=4,'dp'=32] {'tensor'}, use_global_device_ids=true, to_apply=%region_4.5 | all-reduce | flops 1 | bytes 8 | tf_op jit(solution)/shard_map/psum | solution.py:54
  145.8 0.7 multiply_convert_fusion
  146.6 0.1 convert_reduce_fusion.1
  146.7 0.1 select_reduce_fusion
  146.8 6.2 %broadcast_select_fusion = bf16[1,128,128,128]{3,2,1,0:T(8,128)(2,1)} fusion(pred[128]{0:T(512)(128)(4,1)S(1)} %compare_bitcast_fusion, bf16[1,128,128,128]{3,2,1,0:T(8,128)(2,1)} %param.6, bf16[1,128,128,128]{3,2,1,0:T(8,128)(2,1)} %param.5), kind=kLoop, calls=%fused_computation.7 | loop fusion | flops 10485760 | bytes 12583040 | tf_op jit(solution)/shard_map/jit(_where)/select_n | solution.py:26
  153.0 46.8 %all-gather.2.cloned.1.call-done = bf16[224,128,128]{2,1,0:T(8,128)(2,1)} async-done(((bf16[7,128,128]{2,1,0:T(8,128)(2,1)}), bf16[224,128,128]{2,1,0:T(8,128)(2,1)}) %all-gather.2.cloned.1.call-update) | async-done | bytes 7340048 | tf_op jit(solution)/shard_map/all_gather | solution.py:61
  199.8 6.2 %gather_fusion.1 = bf16[128,128,128]{2,1,0:T(8,128)(2,1)} fusion(bf16[224,128,128]{2,1,0:T(8,128)(2,1)} %all-gather.2.cloned.1.call-done, s32[1024]{0:T(1024)S(1)} %pad_clamp_fusion), kind=kCustom, calls=%fused_computation.1 | custom fusion | bytes 8389120 | tf_op jit(solution)/shard_map/jit(_take)/gather | solution.py:63
  206.0 6.4 %add_convert_fusion = bf16[128,128,128]{2,1,0:T(8,128)(2,1)} fusion(bf16[128,128,128]{2,1,0:T(8,128)(2,1)} %param.7, bf16[128,128,128]{2,1,0:T(8,128)(2,1)} %gather_fusion.1, pred[128]{0:T(512)(128)(4,1)S(1)} %compare_and_fusion.1), kind=kLoop, calls=%fused_computation.3 | loop fusion | flops 12582912 | bytes 12583040 | tf_op jit(solution)/shard_map/convert_element_type | solution.py:66
  (8 shorter events, 0.1 us)
Async XLA Ops:
  33.9 96.3 %all-to-all-start = ((bf16[32,7,128,128]{3,2,1,0:T(8,128)(2,1)}), bf16[32,7,128,128]{3,2,1,0:T(8,128)(2,1)}, u32[]{:S(2)}, u32[]{:S(2)}) async-start(bf16[32,7,128,128]{3,2,1,0:T(8,128)(2,1)} %select_select_fusion), calls=%async_computation | async-start | bytes 14680064 | tf_op jit(solution)/shard_map/all_to_all | solution.py:48
  43.4 156.4 %all-gather.2.cloned.1.call-start = ((), (), s32[]{:S(2)}) async-start(), calls=%async_computation.1 | async-start | bytes 7569408 | tf_op jit(solution)/shard_map/all_gather | solution.py:61
Sparse Core Ops, SparseCore 0:
  146.7 53.0 all-gather.1
where the time goes:
time: 220 us; the launch traced here: 219 us
  waiting for transfers between devices  132 us (60%)
  other arithmetic  33.6 us (15%)
  local copies, waits for them, and re-layouts  18.9 us (9%)
  between operations  15.4 us (7%)
  starting transfers between devices  9.52 us (4%)
  blocking collectives  9.33 us (4%)
    all_to_all x1, waiting for transfers between devices, shards(): lax.all_to_all(packed_tiles, 'dp', split_axis=0, concat_axis=0, tiled=True)  85.5 us
    all_gather x1, waiting for transfers between devices, shards(): returned = lax.all_gather(update_tiles, 'dp', axis=0, tiled=True)  46.8 us
    gather x1, local copies, waits for them, and re-layouts, shards(): jnp.take(outgoing, source_rows.reshape(-1), axis=0)  10.6 us
    all_to_all x1, starting transfers between devices, shards(): lax.all_to_all(packed_tiles, 'dp', split_axis=0, concat_axis=0, tiled=True)  9.48 us
    psum x1, blocking collectives, shards(): total_squares = lax.psum(jnp.sum(slot_squares), 'tensor')  9.33 us
    select_n x1, other arithmetic, shards(): jnp.where(slot_valid[:, :, None, None], packed_tiles, jnp.zeros_like(pack...  6.81 us
    convert_element_type x1, other arithmetic, shards(): new_momentum = (MOMENTUM * momentum.astype(jnp.float32) + update_all.asty...  6.36 us
    gather x1, local copies, waits for them, and re-layouts, shards(): jnp.take(returned, owner_of * capacity + local_tiles - offset, axis=0)  6.18 us
  transfers between devices with their start and end apart: 2, of which 2 were waited for; matrix products, arithmetic and copies ran while one was open for 3% of the time, Pallas kernels for 0%

commit v1 on v0

v1 whole, which is shorter than its diff:
```python
import functools

import jax
import jax.numpy as jnp
from jax import lax
from jax.experimental import pallas as pl
from jax.experimental.pallas import tpu as pltpu
from jax.sharding import PartitionSpec as P

MOMENTUM = 0.9
CLIP_LEVEL = 3.0
EPSILON = 1e-06
STREAMS = 2
BLOCK = 8
SHIFTS = (1, 3, 2, 0)
BF16 = jnp.bfloat16
F32 = jnp.float32


def dp_index(z, x, core):
    return (z * 4 + x) * 2 + core


def each_dp():
    return [(d, d // 8, (d // 2) % 4, d % 2) for d in range(32)]


def swap_core():
    return [(d, d ^ 1) for d in range(32)]


def shift_first(k):
    pairs = []
    for d, z, x, core in each_dp():
        to = dp_index(z, (x + k) % 4, core) if core == 0 else dp_index((z + k) % 4, x, core)
        pairs.append((d, to))
    return pairs


def swap_second(mask):
    pairs = []
    for d, z, x, core in each_dp():
        to = dp_index(z ^ mask, x, core) if core == 0 else dp_index(z, x ^ mask, core)
        pairs.append((d, to))
    return pairs


def shift_tensor(k):
    return [(i, (i + k) % 4) for i in range(4)]


def tile_block(index_map):
    return pl.BlockSpec((BLOCK, 128, 128), index_map)


def blocks_shape(count):
    return jax.ShapeDtypeStruct((count * BLOCK, 128, 128), BF16)


def params():
    return pltpu.CompilerParams(vmem_limit_bytes=40 * 1024 * 1024)


def rounded_tile(g_ref, r_ref, t):
    return (g_ref[t].astype(F32) + r_ref[t].astype(F32)).astype(BF16)


def outgoing_kernel(index_ref, bitmap_ref, g_ref, r_ref, out_ref):
    first = index_ref[pl.program_id(0)] * BLOCK
    for t in range(BLOCK):
        value = rounded_tile(g_ref, r_ref, t)
        out_ref[t] = jnp.where(bitmap_ref[first + t] > 0, value, jnp.zeros_like(value))


def outgoing_blocks(index, bitmap, gradients, residual):
    count = index.shape[0]
    return pl.pallas_call(
        outgoing_kernel,
        grid_spec=pltpu.PrefetchScalarGridSpec(
            num_scalar_prefetch=2,
            grid=(count,),
            in_specs=[tile_block(lambda i, index, bitmap: (index[i], 0, 0))] * 2,
            out_specs=tile_block(lambda i, index, bitmap: (i, 0, 0)),
        ),
        out_shape=blocks_shape(count),
        compiler_params=params(),
        cost_estimate=pl.CostEstimate(
            flops=count * BLOCK * 16384, bytes_accessed=count * BLOCK * 98304, transcendentals=0
        ),
    )(index, bitmap, gradients, residual)


def residual_kernel(bitmap_ref, g_ref, r_ref, out_ref):
    tiles = out_ref.shape[0]
    first = pl.program_id(0) * tiles
    for t in range(tiles):
        value = rounded_tile(g_ref, r_ref, t)
        out_ref[t] = jnp.where(bitmap_ref[first + t] > 0, jnp.zeros_like(value), value)


def left_over(bitmap, gradients, residual):
    spec = pl.BlockSpec((16, 128, 128), lambda i, bitmap: (i, 0, 0))
    return pl.pallas_call(
        residual_kernel,
        grid_spec=pltpu.PrefetchScalarGridSpec(
            num_scalar_prefetch=1, grid=(8,), in_specs=[spec] * 2, out_specs=spec
        ),
        out_shape=blocks_shape(16),
        compiler_params=params(),
        cost_estimate=pl.CostEstimate(flops=2**21, bytes_accessed=3 * 2**22, transcendentals=0),
    )(bitmap, gradients, residual)


def pair_kernel(a_ref, b_ref, *out_refs):
    for k, out_ref in enumerate(out_refs):

        @pl.when(pl.program_id(0) == k)
        def _():
            out_ref[...] = (a_ref[...].astype(F32) + b_ref[...].astype(F32)).astype(BF16)


def pair_sums(a, b):
    count = a.shape[0] // BLOCK
    return pl.pallas_call(
        pair_kernel,
        grid=(count,),
        in_specs=[tile_block(lambda i: (i, 0, 0))] * 2,
        out_specs=[tile_block(lambda i: (0, 0, 0))] * count,
        out_shape=[blocks_shape(1)] * count,
        compiler_params=params(),
        cost_estimate=pl.CostEstimate(
            flops=count * BLOCK * 16384, bytes_accessed=count * BLOCK * 98304, transcendentals=0
        ),
    )(a, b)


def sum_kernel(*refs):
    out_ref = refs[-1]
    for t in range(BLOCK):
        total = refs[0][t].astype(F32)
        for ref in refs[1:-1]:
            total = total + ref[t].astype(F32)
        out_ref[t] = total.astype(BF16)


def block_sum(*blocks):
    spec = tile_block(lambda: (0, 0, 0))
    return pl.pallas_call(
        sum_kernel,
        in_specs=[spec] * len(blocks),
        out_specs=spec,
        out_shape=blocks_shape(1),
        compiler_params=params(),
        cost_estimate=pl.CostEstimate(
            flops=BLOCK * 65536, bytes_accessed=(1 + len(blocks)) * BLOCK * 32768, transcendentals=0
        ),
    )(*blocks)


def last_sum_kernel(first_ref, table_ref, a_ref, b_ref, out_ref, row_ref):
    lo, hi = table_ref[0:1, :], table_ref[1:2, :]
    row = jnp.zeros((1, 128), F32)
    for t in range(BLOCK):
        total = a_ref[t].astype(F32) + b_ref[t].astype(F32)
        out_ref[t] = total.astype(BF16)
        square = jnp.sum(jnp.sum(total * total, axis=0, keepdims=True), axis=1, keepdims=True)
        tile = first_ref[0] + t
        row = row + jnp.where((lo <= tile) & (tile < hi), square, 0.0)
    row_ref[...] = jnp.broadcast_to(row, (8, 128))


def last_sum(first, table, a, b):
    spec = tile_block(lambda i, first: (0, 0, 0))
    small = pl.BlockSpec((8, 128), lambda i, first: (0, 0))
    return pl.pallas_call(
        last_sum_kernel,
        grid_spec=pltpu.PrefetchScalarGridSpec(
            num_scalar_prefetch=1,
            grid=(1,),
            in_specs=[small, spec, spec],
            out_specs=[spec, small],
        ),
        out_shape=[blocks_shape(1), jax.ShapeDtypeStruct((8, 128), F32)],
        compiler_params=params(),
        cost_estimate=pl.CostEstimate(
            flops=BLOCK * 65536, bytes_accessed=3 * BLOCK * 32768, transcendentals=0
        ),
    )(first, table, a, b)


def final_kernel(index_ref, table_ref, mine_ref, other_ref, m_ref, *refs):
    block_refs, out_ref, factor_ref = refs[:-2], refs[-2], refs[-1]
    step = pl.program_id(0)

    @pl.when(step == 0)
    def _():
        lo, hi, count = table_ref[0:1, :], table_ref[1:2, :], table_ref[2:3, :]
        squares = mine_ref[0:1, :] + other_ref[0:1, :]
        rms = jnp.sqrt(squares / (count.astype(F32) * 16384.0) + EPSILON)
        clip = jnp.minimum(1.0, CLIP_LEVEL / rms)
        tile = lax.broadcasted_iota(jnp.int32, (128, 128), 0)
        chosen = jnp.where((lo <= tile) & (tile < hi), clip, 0.0)
        factor_ref[...] = jnp.broadcast_to(jnp.sum(chosen, axis=1, keepdims=True), (128, 128))

    first = index_ref[step] * BLOCK
    for k, block_ref in enumerate(block_refs):

        @pl.when(step == k)
        def _():
            for t in range(BLOCK):
                factor = factor_ref[pl.ds(first + t, 1), :]
                update = (block_ref[t].astype(F32) * factor).astype(BF16)
                out_ref[t] = (MOMENTUM * m_ref[t].astype(F32) + update.astype(F32)).astype(BF16)


def finish(index, table, mine, other, momentum, blocks):
    small = pl.BlockSpec((8, 128), lambda i, index: (0, 0))
    moved = tile_block(lambda i, index: (index[i], 0, 0))
    return pl.pallas_call(
        final_kernel,
        grid_spec=pltpu.PrefetchScalarGridSpec(
            num_scalar_prefetch=1,
            grid=(len(blocks),),
            in_specs=[small] * 3
            + [moved]
            + [tile_block(lambda i, index: (0, 0, 0))] * len(blocks),
            out_specs=moved,
            scratch_shapes=[pltpu.VMEM((128, 128), F32)],
        ),
        out_shape=blocks_shape(16),
        compiler_params=params(),
        cost_estimate=pl.CostEstimate(flops=2**23, bytes_accessed=3 * 2**22, transcendentals=0),
    )(index, table, mine, other, momentum, *blocks)


def row_sum(own, by_shift):
    r1, r2, r3 = by_shift
    return (own + r2) + (r1 + r3)


def shards(gradients, residual, momentum, bitmap, starts):
    gradients, residual, bitmap = gradients[0], residual[0], bitmap[0]
    dp = lax.axis_index("dp")
    z, x, core = dp // 8, (dp // 2) % 4, dp % 2
    mine = jnp.where(core == 0, x, z)
    theirs = jnp.where(core == 0, z, x)
    shifts = jnp.array(SHIFTS, jnp.int32)
    mine_to = core * 8 + ((mine + shifts) % 4) * 2
    theirs_to = (1 - core) * 8 + ((theirs + shifts) % 4) * 2
    mine_from = core * 8 + ((mine - shifts) % 4) * 2
    theirs_from = (1 - core) * 8 + ((theirs - shifts) % 4) * 2

    ends = jnp.concatenate([starts[:, 1:], jnp.full((4, 1), 128, jnp.int32)], axis=1)
    shard = lax.axis_index("tensor")
    lo = lax.dynamic_slice_in_dim(starts, shard, 1, 0)
    hi = lax.dynamic_slice_in_dim(ends, shard, 1, 0)
    count = jnp.sum(ends - starts, axis=0, keepdims=True)
    table = jnp.concatenate([lo, hi, count, jnp.zeros((5, 32), jnp.int32)], axis=0)
    table = jnp.pad(table, ((0, 0), (0, 96)), constant_values=128)

    sent = []
    for s in range(STREAMS):
        blocks = outgoing_blocks(theirs_to + s, bitmap, gradients, residual)
        sent.append(lax.ppermute(blocks, "dp", swap_core()))
    kept, arrived = [], []
    for s in range(STREAMS):
        own = outgoing_blocks(mine_to + s, bitmap, gradients, residual)
        parts = pair_sums(own, sent[s])
        arrived.append([lax.ppermute(parts[i], "dp", shift_first(SHIFTS[i])) for i in range(3)])
        kept.append(parts[3])
    new_residual = left_over(bitmap, gradients, residual)

    full, rows = [], []
    for s in range(STREAMS):
        part = block_sum(kept[s], *arrived[s])
        masks = (1, 3) if s == 0 else (3, 1)
        part = block_sum(part, lax.ppermute(part, "dp", swap_second(masks[0])))
        first = ((core * 8 + mine * 2 + s) * BLOCK).reshape(1)
        block, row = last_sum(first, table, part, lax.ppermute(part, "dp", swap_second(masks[1])))
        full.append(block)
        rows.append(row)

    gathered = []
    for s in range(STREAMS):
        gathered.append([lax.ppermute(full[s], "dp", shift_first(SHIFTS[i])) for i in range(3)])
        gathered[-1].append(full[s])
    row = rows[0] + rows[1]
    row = row_sum(row, [lax.ppermute(row, "tensor", shift_tensor(k)) for k in (1, 2, 3)])
    row = row_sum(row, [lax.ppermute(row, "dp", shift_first(k)) for k in (1, 2, 3)])
    other = lax.ppermute(row, "dp", swap_core())

    blocks, index = [], []
    for s in range(STREAMS):
        for i in range(4):
            blocks.append(gathered[s][i])
            index.append(mine_from[i] + s)
            blocks.append(lax.ppermute(gathered[s][i], "dp", swap_core()))
            index.append(theirs_from[i] + s)
    new_momentum = finish(jnp.stack(index), table, row, other, momentum, blocks)
    return (new_residual[None], new_momentum)


def solution(mesh):
    return jax.shard_map(
        shards,
        mesh=mesh,
        in_specs=(
            P("dp", "tensor", None, None),
            P("dp", "tensor", None, None),
            P("tensor", None, None),
            P("dp", "tensor"),
            P(),
        ),
        out_specs=(P("dp", "tensor", None, None), P("tensor", None, None)),
        check_vma=False,
    )
```

time: 220 us -> 116 us (0.53)
  waiting for transfers between devices: 132 us -> 32.9 us
  other arithmetic: 33.6 us -> 0.81 us
  starting transfers between devices: 9.52 us -> 40.9 us
  Pallas kernels: 0 us -> 19 us
  between operations: 15.4 us -> 5.95 us
  blocking collectives: 9.33 us -> 0 us
  local copies, waits for them, and re-layouts: 18.9 us -> 16 us
    all_to_all x1 -> x0, waiting for transfers between devices: 85.5 us -> none  [shards(): lax.all_to_all(packed_tiles, 'dp', split_axis=0, concat_axis=0, tiled=True)]
    all_gather x1 -> x0, waiting for transfers between devices: 46.8 us -> none  [shards(): returned = lax.all_gather(update_tiles, 'dp', axis=0, tiled=True)]
    ppermute x0 -> x33, starting transfers between devices: none -> 40.9 us  [the longest x6 9.05 us: shards(): lax.ppermute(parts[i], 'dp', shift_first(SHIFTS[i]))]
    ppermute x0 -> x33, waiting for transfers between devices: none -> 32.9 us  [the longest x3 11.7 us: shards(): lax.ppermute(row, 'dp', shift_first(k))]
    select_n x5 -> x0, other arithmetic: 19.1 us -> none  [the longest x1 6.81 us: shards(): jnp.where(slot_valid[:, :, None, None], packed_tiles, jnp.zeros_like(pack...]
    pallas_call x0 -> x14, Pallas kernels: none -> 19 us  [the longest x1 8.98 us: finish(): pl.pallas_call(final_kernel, grid_spec=pltpu.PrefetchScalarGridSpec(num_s...]
    gather x2 -> x0, local copies, waits for them, and re-layouts: 16.8 us -> none  [the longest x1 10.6 us: shards(): jnp.take(outgoing, source_rows.reshape(-1), axis=0)]
    all_to_all x1 -> x0, starting transfers between devices: 9.48 us -> none  [shards(): lax.all_to_all(packed_tiles, 'dp', split_axis=0, concat_axis=0, tiled=True)]
  transfers between devices with their start and end apart: 2 -> 33, of which waited for: 2 -> 15; matrix products, arithmetic and copies ran while one was open for 3% -> 6% of each run, Pallas kernels for 0% -> 8%
where the time goes in v1:
time: 116 us; the launch traced here: 115 us
  starting transfers between devices  40.9 us (35%)
  waiting for transfers between devices  32.9 us (28%)
  Pallas kernels  19 us (16%)
  local copies, waits for them, and re-layouts  16 us (14%)
  between operations  5.95 us (5%)
    ppermute x3, waiting for transfers between devices, shards(): lax.ppermute(row, 'dp', shift_first(k))  11.7 us
    unnamed x18, local copies, waits for them, and re-layouts  9.42 us
    ppermute x6, starting transfers between devices, shards(): lax.ppermute(parts[i], 'dp', shift_first(SHIFTS[i]))  9.05 us
    pallas_call x1, Pallas kernels, finish(): pl.pallas_call(final_kernel, grid_spec=pltpu.PrefetchScalarGridSpec(num_s...  8.98 us
    ppermute x8, starting transfers between devices, shards(): blocks.append(lax.ppermute(gathered[s][i], 'dp', swap_core()))  8.27 us
    ppermute x6, starting transfers between devices, shards(): lax.ppermute(full[s], 'dp', shift_first(SHIFTS[i]))  8.2 us
    ppermute x6, waiting for transfers between devices, shards(): lax.ppermute(parts[i], 'dp', shift_first(SHIFTS[i]))  6.54 us
    another operation x1, local copies, waits for them, and re-layouts, shards(): new_momentum = finish(jnp.stack(index), table, row, other, momentum, blocks)  5.12 us
  transfers between devices with their start and end apart: 33, of which 15 were waited for; matrix products, arithmetic and copies ran while one was open for 6% of the time, Pallas kernels for 8%

profile of v1, /device:TPU:1, one launch (start us, length us, event | category | flops | bytes accessed | tf_op | source)
XLA Modules:
  0.0 115.5 jit_solution(12727655690139808748)
XLA Ops:
  1.4 2.2 %copy-done = bf16[1,128,128,128]{3,2,1,0:T(8,128)(2,1)S(1)} copy-done((bf16[1,128,128,128]{3,2,1,0:T(8,128)(2,1)S(1)}, bf16[1,128,128,128]{3,2,1,0:T(8,128)(2,1)}, u32[]{:S(2)}) %copy-start) | copy-done | bytes 4194328
  3.6 2.2 %copy-done.3 = bf16[1,128,128,128]{3,2,1,0:T(8,128)(2,1)S(1)} copy-done((bf16[1,128,128,128]{3,2,1,0:T(8,128)(2,1)S(1)}, bf16[1,128,128,128]{3,2,1,0:T(8,128)(2,1)}, u32[]{:S(2)}) %copy-start.3) | copy-done | bytes 4194328
  14.3 2.8 %collective-permute-start.2 = (bf16[8,128,128]{2,1,0:T(8,128)(2,1)S(1)}, bf16[8,128,128]{2,1,0:T(8,128)(2,1)S(1)}, u32[]{:S(2)}, u32[]{:S(2)}) collective-permute-start(bf16[8,128,128]{2,1,0:T(8,128)(2,1)S(1)} %get-tuple-element.16), channel_id=1, source_target_pairs={{0,6},{1,25},{2,0},{3,27},{4,2},{5,29},{6,4},{7,31},{8,14},{9,1},{... | collective-permute-start | bytes 786440 | tf_op jit(solution)/shard_map/ppermute | solution.py:269
  19.0 1.9 %collective-permute-start.8 = (bf16[8,128,128]{2,1,0:T(8,128)(2,1)S(1)}, bf16[8,128,128]{2,1,0:T(8,128)(2,1)S(1)}, u32[]{:S(2)}, u32[]{:S(2)}) collective-permute-start(bf16[8,128,128]{2,1,0:T(8,128)(2,1)S(1)} %get-tuple-element.21), channel_id=1, source_target_pairs={{0,6},{1,25},{2,0},{3,27},{4,2},{5,29},{6,4},{7,31},{8,14},{9,1},{... | collective-permute-start | bytes 786440 | tf_op jit(solution)/shard_map/ppermute | solution.py:269
  26.9 1.9 %collective-permute-done.8.refs_2_ = bf16[8,128,128]{2,1,0:T(8,128)(2,1)S(1)} collective-permute-done((bf16[8,128,128]{2,1,0:T(8,128)(2,1)S(1)}, bf16[8,128,128]{2,1,0:T(8,128)(2,1)S(1)}, u32[]{:S(2)}, u32[]{:S(2)}) %collective-permute-start.8) | collective-permute-done | bytes 262176 | tf_op jit(solution)/shard_map/ppermute | solution.py:269
  29.9 2.6 %collective-permute-start.10 = (bf16[8,128,128]{2,1,0:T(8,128)(2,1)S(1)}, bf16[8,128,128]{2,1,0:T(8,128)(2,1)S(1)}, u32[]{:S(2)}, u32[]{:S(2)}) collective-permute-start(bf16[8,128,128]{2,1,0:T(8,128)(2,1)S(1)} %shard_map.87.refs_0_), channel_id=1, source_target_pairs={{0,24},{1,7},{2,26},{3,5},{4,28},{5,3},{6,30},{7,1},{8,16},{9,15},... | collective-permute-start | bytes 786440 | tf_op jit(solution)/shard_map/ppermute | solution.py:277
  32.9 3.5 %collective-permute-done.10.refs_1_ = bf16[8,128,128]{2,1,0:T(8,128)(2,1)S(1)} collective-permute-done((bf16[8,128,128]{2,1,0:T(8,128)(2,1)S(1)}, bf16[8,128,128]{2,1,0:T(8,128)(2,1)S(1)}, u32[]{:S(2)}, u32[]{:S(2)}) %collective-permute-start.10) | collective-permute-done | bytes 262176 | tf_op jit(solution)/shard_map/ppermute | solution.py:277
  36.8 2.7 %collective-permute-done.5.b_ref = bf16[8,128,128]{2,1,0:T(8,128)(2,1)S(1)} collective-permute-done((bf16[8,128,128]{2,1,0:T(8,128)(2,1)S(1)}, bf16[8,128,128]{2,1,0:T(8,128)(2,1)S(1)}, u32[]{:S(2)}, u32[]{:S(2)}) %collective-permute-start.5) | collective-permute-done | bytes 262176 | tf_op jit(solution)/shard_map/ppermute | solution.py:279
  39.7 2.4 %collective-permute-done.11.b_ref = bf16[8,128,128]{2,1,0:T(8,128)(2,1)S(1)} collective-permute-done((bf16[8,128,128]{2,1,0:T(8,128)(2,1)S(1)}, bf16[8,128,128]{2,1,0:T(8,128)(2,1)S(1)}, u32[]{:S(2)}, u32[]{:S(2)}) %collective-permute-start.11) | collective-permute-done | bytes 262176 | tf_op jit(solution)/shard_map/ppermute | solution.py:279
  42.3 2.8 %collective-permute-start.14 = (f32[8,128]{1,0:T(8,128)S(1)}, f32[8,128]{1,0:T(8,128)S(1)}, u32[]{:S(2)}, u32[]{:S(2)}) collective-permute-start(f32[8,128]{1,0:T(8,128)S(1)} %add.156), channel_id=1, source_target_pairs={{0,96},{32,0},{64,32},{96,64},{1,97},{33,1},{65,33},{97,65},{2,98}... | collective-permute-start | bytes 12296 | tf_op jit(solution)/shard_map/ppermute | solution.py:288
  46.7 5.6 %collective-permute-start.25 = (bf16[8,128,128]{2,1,0:T(8,128)(2,1)S(1)}, bf16[8,128,128]{2,1,0:T(8,128)(2,1)S(1)}, u32[]{:S(2)}, u32[]{:S(2)}) collective-permute-start(bf16[8,128,128]{2,1,0:T(8,128)(2,1)S(1)} %get-tuple-element.24.refs_6_), channel_id=1, source_target_pairs={{0,1},{1,0},{2,3},{3,2},{4,5},{5,4},{6,7},{7,6},{8,9},{9,8},{10,11... | collective-permute-start | bytes 786440 | tf_op jit(solution)/shard_map/ppermute | solution.py:297
  52.3 2.9 %collective-permute-start.23 = (bf16[8,128,128]{2,1,0:T(8,128)(2,1)S(1)}, bf16[8,128,128]{2,1,0:T(8,128)(2,1)S(1)}, u32[]{:S(2)}, u32[]{:S(2)}) collective-permute-start(bf16[8,128,128]{2,1,0:T(8,128)(2,1)S(1)} %get-tuple-element.24.refs_6_), channel_id=1, source_target_pairs={{0,4},{1,17},{2,6},{3,19},{4,0},{5,21},{6,2},{7,23},{8,12},{9,25},... | collective-permute-start | bytes 786440 | tf_op jit(solution)/shard_map/ppermute | solution.py:285
  58.2 4.5 %collective-permute-done.17 = f32[8,128]{1,0:T(8,128)S(1)} collective-permute-done((f32[8,128]{1,0:T(8,128)S(1)}, f32[8,128]{1,0:T(8,128)S(1)}, u32[]{:S(2)}, u32[]{:S(2)}) %collective-permute-start.17) | collective-permute-done | bytes 4128 | tf_op jit(solution)/shard_map/ppermute | solution.py:289
  63.0 3.5 %collective-permute-done.16 = f32[8,128]{1,0:T(8,128)S(1)} collective-permute-done((f32[8,128]{1,0:T(8,128)S(1)}, f32[8,128]{1,0:T(8,128)S(1)}, u32[]{:S(2)}, u32[]{:S(2)}) %collective-permute-start.16) | collective-permute-done | bytes 4128 | tf_op jit(solution)/shard_map/ppermute | solution.py:289
  66.7 3.7 %collective-permute-done.15 = f32[8,128]{1,0:T(8,128)S(1)} collective-permute-done((f32[8,128]{1,0:T(8,128)S(1)}, f32[8,128]{1,0:T(8,128)S(1)}, u32[]{:S(2)}, u32[]{:S(2)}) %collective-permute-start.15) | collective-permute-done | bytes 4128 | tf_op jit(solution)/shard_map/ppermute | solution.py:289
  70.4 3.1 %collective-permute-start.18 = (f32[8,128]{1,0:T(8,128)S(1)}, f32[8,128]{1,0:T(8,128)S(1)}, u32[]{:S(2)}, u32[]{:S(2)}) collective-permute-start(f32[8,128]{1,0:T(8,128)S(1)} %add_add_fusion.1.mine_ref), channel_id=1, source_target_pairs={{0,1},{1,0},{2,3},{3,2},{4,5},{5,4},{6,7},{7,6},{8,9},{9,8},{10,11... | collective-permute-start | bytes 12296 | tf_op jit(solution)/shard_map/ppermute | solution.py:290
  74.7 2.4 %collective-permute-start.30 = (bf16[8,128,128]{2,1,0:T(8,128)(2,1)S(1)}, bf16[8,128,128]{2,1,0:T(8,128)(2,1)S(1)}, u32[]{:S(2)}, u32[]{:S(2)}) collective-permute-start(bf16[8,128,128]{2,1,0:T(8,128)(2,1)S(1)} %get-tuple-element.25.refs_14_), channel_id=1, source_target_pairs={{0,4},{1,17},{2,6},{3,19},{4,0},{5,21},{6,2},{7,23},{8,12},{9,25},... | collective-permute-start | bytes 786440 | tf_op jit(solution)/shard_map/ppermute | solution.py:285
  79.1 2.6 %collective-permute-done.30.refs_12_ = bf16[8,128,128]{2,1,0:T(8,128)(2,1)S(1)} collective-permute-done((bf16[8,128,128]{2,1,0:T(8,128)(2,1)S(1)}, bf16[8,128,128]{2,1,0:T(8,128)(2,1)S(1)}, u32[]{:S(2)}, u32[]{:S(2)}) %collective-permute-start.30) | collective-permute-done | bytes 262176 | tf_op jit(solution)/shard_map/ppermute | solution.py:285
  82.8 2.4 %collective-permute-done.28.refs_10_ = bf16[8,128,128]{2,1,0:T(8,128)(2,1)S(1)} collective-permute-done((bf16[8,128,128]{2,1,0:T(8,128)(2,1)S(1)}, bf16[8,128,128]{2,1,0:T(8,128)(2,1)S(1)}, u32[]{:S(2)}, u32[]{:S(2)}) %collective-permute-start.28) | collective-permute-done | bytes 262176 | tf_op jit(solution)/shard_map/ppermute | solution.py:285
  92.3 5.1 %stack.2.index_ref = s32[16]{0:T(128)S(1)} concatenate(s32[1]{0:T(128)} %get-tuple-element.39, s32[1]{0:T(128)} %get-tuple-element.35, s32[1]{0:T(128)} %get-tuple-element.38, s32[1]{0:T(128)} %get-tuple-element.34, s32[1]{0:T(128)} %get-tuple-element.37, s32[1]{0:T(128)} %get-tuple-element.33, s32[1]{0:T(128)} %get-tuple-element.36, s32[1]{0:T(128)} %get-tuple-element.32, ...), dimensions={0} | concatenate | bytes 128 | tf_op jit(solution)/shard_map/stack | solution.py:299
  97.4 2.2 %copy-done.2 = bf16[1,128,128,128]{3,2,1,0:T(8,128)(2,1)S(1)} copy-done((bf16[1,128,128,128]{3,2,1,0:T(8,128)(2,1)S(1)}, bf16[1,128,128,128]{3,2,1,0:T(8,128)(2,1)}, u32[]{:S(2)}) %copy-start.2) | copy-done | bytes 4194328
  99.6 2.2 %copy-done.4 = bf16[1,128,128,128]{3,2,1,0:T(8,128)(2,1)S(1)} copy-done((bf16[1,128,128,128]{3,2,1,0:T(8,128)(2,1)S(1)}, bf16[1,128,128,128]{3,2,1,0:T(8,128)(2,1)}, u32[]{:S(2)}) %copy-start.4) | copy-done | bytes 4194328
  101.8 4.6 %shard_map.77 = bf16[128,128,128]{2,1,0:T(8,128)(2,1)} custom-call(s32[128]{0:T(128)S(1)} %bitcast.21, bf16[128,128,128]{2,1,0:T(8,128)(2,1)S(1)} %bitcast.11, bf16[128,128,128]{2,1,0:T(8,128)(2,1)S(1)} %bitcast.16), custom_call_target="tpu_custom_call" | custom-call | flops 2097152 | bytes 12582912 | tf_op jit(solution)/shard_map/pallas_call | solution.py:103
  106.5 9.0 %shard_map.90 = bf16[128,128,128]{2,1,0:T(8,128)(2,1)} custom-call(s32[16]{0:T(128)S(1)} %stack.2.index_ref, s32[8,128]{1,0:T(8,128)S(1)} %pad.5.table_ref, f32[8,128]{1,0:T(8,128)S(1)} %add_add_fusion.1.mine_ref, f32[8,128]{1,0:T(8,128)S(1)} %collective-permute-done.18.other_ref, bf16[128,128,128]{2,1,0:T(8,128)(2,1)S(1)} %copy-done.5, ...), custom_call_target="tpu_custom_call" | custom-call | flops 8388608 | bytes 12582912 | tf_op jit(solution)/shard_map/pallas_call | solution.py:219
  (88 shorter events, 30.8 us)
Async XLA Ops:
  9.9 8.0 %collective-permute-start.6 = (bf16[32,128,128]{2,1,0:T(8,128)(2,1)S(1)}, bf16[32,128,128]{2,1,0:T(8,128)(2,1)S(1)}, u32[]{:S(2)}, u32[]{:S(2)}) collective-permute-start(bf16[32,128,128]{2,1,0:T(8,128)(2,1)S(1)} %shard_map.85), channel_id=1, source_target_pairs={{0,1},{1,0},{2,3},{3,2},{4,5},{5,4},{6,7},{7,6},{8,9},{9,8},{10,11... | collective-permute-start | bytes 3145736 | tf_op jit(solution)/shard_map/ppermute | solution.py:264
  11.5 9.4 %collective-permute-start.1 = (bf16[8,128,128]{2,1,0:T(8,128)(2,1)S(1)}, bf16[8,128,128]{2,1,0:T(8,128)(2,1)S(1)}, u32[]{:S(2)}, u32[]{:S(2)}) collective-permute-start(bf16[8,128,128]{2,1,0:T(8,128)(2,1)S(1)} %get-tuple-element.15), channel_id=1, source_target_pairs={{0,2},{1,9},{2,4},{3,11},{4,6},{5,13},{6,0},{7,15},{8,10},{9,17},{... | collective-permute-start | bytes 786440 | tf_op jit(solution)/shard_map/ppermute | solution.py:269
  14.3 8.9 %collective-permute-start.2 = (bf16[8,128,128]{2,1,0:T(8,128)(2,1)S(1)}, bf16[8,128,128]{2,1,0:T(8,128)(2,1)S(1)}, u32[]{:S(2)}, u32[]{:S(2)}) collective-permute-start(bf16[8,128,128]{2,1,0:T(8,128)(2,1)S(1)} %get-tuple-element.16), channel_id=1, source_target_pairs={{0,6},{1,25},{2,0},{3,27},{4,2},{5,29},{6,4},{7,31},{8,14},{9,1},{... | collective-permute-start | bytes 786440 | tf_op jit(solution)/shard_map/ppermute | solution.py:269
  17.1 7.0 %collective-permute-start.3 = (bf16[8,128,128]{2,1,0:T(8,128)(2,1)S(1)}, bf16[8,128,128]{2,1,0:T(8,128)(2,1)S(1)}, u32[]{:S(2)}, u32[]{:S(2)}) collective-permute-start(bf16[8,128,128]{2,1,0:T(8,128)(2,1)S(1)} %get-tuple-element.17), channel_id=1, source_target_pairs={{0,4},{1,17},{2,6},{3,19},{4,0},{5,21},{6,2},{7,23},{8,12},{9,25},... | collective-permute-start | bytes 786440 | tf_op jit(solution)/shard_map/ppermute | solution.py:269
  18.2 8.7 %collective-permute-start.7 = (bf16[8,128,128]{2,1,0:T(8,128)(2,1)S(1)}, bf16[8,128,128]{2,1,0:T(8,128)(2,1)S(1)}, u32[]{:S(2)}, u32[]{:S(2)}) collective-permute-start(bf16[8,128,128]{2,1,0:T(8,128)(2,1)S(1)} %get-tuple-element.20), channel_id=1, source_target_pairs={{0,2},{1,9},{2,4},{3,11},{4,6},{5,13},{6,0},{7,15},{8,10},{9,17},{... | collective-permute-start | bytes 786440 | tf_op jit(solution)/shard_map/ppermute | solution.py:269
  19.0 9.8 %collective-permute-start.8 = (bf16[8,128,128]{2,1,0:T(8,128)(2,1)S(1)}, bf16[8,128,128]{2,1,0:T(8,128)(2,1)S(1)}, u32[]{:S(2)}, u32[]{:S(2)}) collective-permute-start(bf16[8,128,128]{2,1,0:T(8,128)(2,1)S(1)} %get-tuple-element.21), channel_id=1, source_target_pairs={{0,6},{1,25},{2,0},{3,27},{4,2},{5,29},{6,4},{7,31},{8,14},{9,1},{... | collective-permute-start | bytes 786440 | tf_op jit(solution)/shard_map/ppermute | solution.py:269
  20.9 8.8 %collective-permute-start.9 = (bf16[8,128,128]{2,1,0:T(8,128)(2,1)S(1)}, bf16[8,128,128]{2,1,0:T(8,128)(2,1)S(1)}, u32[]{:S(2)}, u32[]{:S(2)}) collective-permute-start(bf16[8,128,128]{2,1,0:T(8,128)(2,1)S(1)} %get-tuple-element.22), channel_id=1, source_target_pairs={{0,4},{1,17},{2,6},{3,19},{4,0},{5,21},{6,2},{7,23},{8,12},{9,25},... | collective-permute-start | bytes 786440 | tf_op jit(solution)/shard_map/ppermute | solution.py:269
  24.2 8.4 %collective-permute-start.4 = (bf16[8,128,128]{2,1,0:T(8,128)(2,1)S(1)}, bf16[8,128,128]{2,1,0:T(8,128)(2,1)S(1)}, u32[]{:S(2)}, u32[]{:S(2)}) collective-permute-start(bf16[8,128,128]{2,1,0:T(8,128)(2,1)S(1)} %shard_map.81.refs_0_), channel_id=1, source_target_pairs={{0,8},{1,3},{2,10},{3,1},{4,12},{5,7},{6,14},{7,5},{8,0},{9,11},{1... | collective-permute-start | bytes 786440 | tf_op jit(solution)/shard_map/ppermute | solution.py:277
  42.3 12.9 %collective-permute-start.14 = (f32[8,128]{1,0:T(8,128)S(1)}, f32[8,128]{1,0:T(8,128)S(1)}, u32[]{:S(2)}, u32[]{:S(2)}) collective-permute-start(f32[8,128]{1,0:T(8,128)S(1)} %add.156), channel_id=1, source_target_pairs={{0,96},{32,0},{64,32},{96,64},{1,97},{33,1},{65,33},{97,65},{2,98}... | collective-permute-start | bytes 12296 | tf_op jit(solution)/shard_map/ppermute | solution.py:288
  45.1 10.4 %collective-permute-start.13 = (f32[8,128]{1,0:T(8,128)S(1)}, f32[8,128]{1,0:T(8,128)S(1)}, u32[]{:S(2)}, u32[]{:S(2)}) collective-permute-start(f32[8,128]{1,0:T(8,128)S(1)} %add.156), channel_id=1, source_target_pairs={{0,32},{32,64},{64,96},{96,0},{1,33},{33,65},{65,97},{97,1},{2,34}... | collective-permute-start | bytes 12296 | tf_op jit(solution)/shard_map/ppermute | solution.py:288
  45.1 11.6 %collective-permute-start.12 = (f32[8,128]{1,0:T(8,128)S(1)}, f32[8,128]{1,0:T(8,128)S(1)}, u32[]{:S(2)}, u32[]{:S(2)}) collective-permute-start(f32[8,128]{1,0:T(8,128)S(1)} %add.156), channel_id=1, source_target_pairs={{0,64},{32,96},{64,0},{96,32},{1,65},{33,97},{65,1},{97,33},{2,66}... | collective-permute-start | bytes 12296 | tf_op jit(solution)/shard_map/ppermute | solution.py:288
  46.7 28.0 %collective-permute-start.25 = (bf16[8,128,128]{2,1,0:T(8,128)(2,1)S(1)}, bf16[8,128,128]{2,1,0:T(8,128)(2,1)S(1)}, u32[]{:S(2)}, u32[]{:S(2)}) collective-permute-start(bf16[8,128,128]{2,1,0:T(8,128)(2,1)S(1)} %get-tuple-element.24.refs_6_), channel_id=1, source_target_pairs={{0,1},{1,0},{2,3},{3,2},{4,5},{5,4},{6,7},{7,6},{8,9},{9,8},{10,11... | collective-permute-start | bytes 786440 | tf_op jit(solution)/shard_map/ppermute | solution.py:297
  52.3 24.8 %collective-permute-start.23 = (bf16[8,128,128]{2,1,0:T(8,128)(2,1)S(1)}, bf16[8,128,128]{2,1,0:T(8,128)(2,1)S(1)}, u32[]{:S(2)}, u32[]{:S(2)}) collective-permute-start(bf16[8,128,128]{2,1,0:T(8,128)(2,1)S(1)} %get-tuple-element.24.refs_6_), channel_id=1, source_target_pairs={{0,4},{1,17},{2,6},{3,19},{4,0},{5,21},{6,2},{7,23},{8,12},{9,25},... | collective-permute-start | bytes 786440 | tf_op jit(solution)/shard_map/ppermute | solution.py:285
  55.2 22.6 %collective-permute-start.21 = (bf16[8,128,128]{2,1,0:T(8,128)(2,1)S(1)}, bf16[8,128,128]{2,1,0:T(8,128)(2,1)S(1)}, u32[]{:S(2)}, u32[]{:S(2)}) collective-permute-start(bf16[8,128,128]{2,1,0:T(8,128)(2,1)S(1)} %get-tuple-element.24.refs_6_), channel_id=1, source_target_pairs={{0,6},{1,25},{2,0},{3,27},{4,2},{5,29},{6,4},{7,31},{8,14},{9,1},{... | collective-permute-start | bytes 786440 | tf_op jit(solution)/shard_map/ppermute | solution.py:285
  55.5 23.1 %collective-permute-start.19 = (bf16[8,128,128]{2,1,0:T(8,128)(2,1)S(1)}, bf16[8,128,128]{2,1,0:T(8,128)(2,1)S(1)}, u32[]{:S(2)}, u32[]{:S(2)}) collective-permute-start(bf16[8,128,128]{2,1,0:T(8,128)(2,1)S(1)} %get-tuple-element.24.refs_6_), channel_id=1, source_target_pairs={{0,2},{1,9},{2,4},{3,11},{4,6},{5,13},{6,0},{7,15},{8,10},{9,17},{... | collective-permute-start | bytes 786440 | tf_op jit(solution)/shard_map/ppermute | solution.py:285
  74.7 7.0 %collective-permute-start.30 = (bf16[8,128,128]{2,1,0:T(8,128)(2,1)S(1)}, bf16[8,128,128]{2,1,0:T(8,128)(2,1)S(1)}, u32[]{:S(2)}, u32[]{:S(2)}) collective-permute-start(bf16[8,128,128]{2,1,0:T(8,128)(2,1)S(1)} %get-tuple-element.25.refs_14_), channel_id=1, source_target_pairs={{0,4},{1,17},{2,6},{3,19},{4,0},{5,21},{6,2},{7,23},{8,12},{9,25},... | collective-permute-start | bytes 786440 | tf_op jit(solution)/shard_map/ppermute | solution.py:285
  77.1 8.0 %collective-permute-start.28 = (bf16[8,128,128]{2,1,0:T(8,128)(2,1)S(1)}, bf16[8,128,128]{2,1,0:T(8,128)(2,1)S(1)}, u32[]{:S(2)}, u32[]{:S(2)}) collective-permute-start(bf16[8,128,128]{2,1,0:T(8,128)(2,1)S(1)} %get-tuple-element.25.refs_14_), channel_id=1, source_target_pairs={{0,6},{1,25},{2,0},{3,27},{4,2},{5,29},{6,4},{7,31},{8,14},{9,1},{... | collective-permute-start | bytes 786440 | tf_op jit(solution)/shard_map/ppermute | solution.py:285
  77.7 7.4 %collective-permute-start.26 = (bf16[8,128,128]{2,1,0:T(8,128)(2,1)S(1)}, bf16[8,128,128]{2,1,0:T(8,128)(2,1)S(1)}, u32[]{:S(2)}, u32[]{:S(2)}) collective-permute-start(bf16[8,128,128]{2,1,0:T(8,128)(2,1)S(1)} %get-tuple-element.25.refs_14_), channel_id=1, source_target_pairs={{0,2},{1,9},{2,4},{3,11},{4,6},{5,13},{6,0},{7,15},{8,10},{9,17},{... | collective-permute-start | bytes 786440 | tf_op jit(solution)/shard_map/ppermute | solution.py:285
  78.6 7.4 %collective-permute-start.24 = (bf16[8,128,128]{2,1,0:T(8,128)(2,1)S(1)}, bf16[8,128,128]{2,1,0:T(8,128)(2,1)S(1)}, u32[]{:S(2)}, u32[]{:S(2)}) collective-permute-start(bf16[8,128,128]{2,1,0:T(8,128)(2,1)S(1)} %collective-permute-done.23.refs_4_), channel_id=1, source_target_pairs={{0,1},{1,0},{2,3},{3,2},{4,5},{5,4},{6,7},{7,6},{8,9},{9,8},{10,11... | collective-permute-start | bytes 786440 | tf_op jit(solution)/shard_map/ppermute | solution.py:297
  78.6 27.8 %collective-permute-start.22 = (bf16[8,128,128]{2,1,0:T(8,128)(2,1)S(1)}, bf16[8,128,128]{2,1,0:T(8,128)(2,1)S(1)}, u32[]{:S(2)}, u32[]{:S(2)}) collective-permute-start(bf16[8,128,128]{2,1,0:T(8,128)(2,1)S(1)} %collective-permute-done.21.refs_2_), channel_id=1, source_target_pairs={{0,1},{1,0},{2,3},{3,2},{4,5},{5,4},{6,7},{7,6},{8,9},{9,8},{10,11... | collective-permute-start | bytes 786440 | tf_op jit(solution)/shard_map/ppermute | solution.py:297
  81.7 24.7 %collective-permute-start.20 = (bf16[8,128,128]{2,1,0:T(8,128)(2,1)S(1)}, bf16[8,128,128]{2,1,0:T(8,128)(2,1)S(1)}, u32[]{:S(2)}, u32[]{:S(2)}) collective-permute-start(bf16[8,128,128]{2,1,0:T(8,128)(2,1)S(1)} %collective-permute-done.19.refs_0_), channel_id=1, source_target_pairs={{0,1},{1,0},{2,3},{3,2},{4,5},{5,4},{6,7},{7,6},{8,9},{9,8},{10,11... | collective-permute-start | bytes 786440 | tf_op jit(solution)/shard_map/ppermute | solution.py:297
  85.1 21.3 %collective-permute-start.31 = (bf16[8,128,128]{2,1,0:T(8,128)(2,1)S(1)}, bf16[8,128,128]{2,1,0:T(8,128)(2,1)}, u32[]{:S(2)}, u32[]{:S(2)}) collective-permute-start(bf16[8,128,128]{2,1,0:T(8,128)(2,1)S(1)} %collective-permute-done.30.refs_12_), channel_id=1, source_target_pairs={{0,1},{1,0},{2,3},{3,2},{4,5},{5,4},{6,7},{7,6},{8,9},{9,8},{10,11... | collective-permute-start | bytes 786440 | tf_op jit(solution)/shard_map/ppermute | solution.py:297
  85.2 21.3 %collective-permute-start.29 = (bf16[8,128,128]{2,1,0:T(8,128)(2,1)S(1)}, bf16[8,128,128]{2,1,0:T(8,128)(2,1)}, u32[]{:S(2)}, u32[]{:S(2)}) collective-permute-start(bf16[8,128,128]{2,1,0:T(8,128)(2,1)S(1)} %collective-permute-done.28.refs_10_), channel_id=1, source_target_pairs={{0,1},{1,0},{2,3},{3,2},{4,5},{5,4},{6,7},{7,6},{8,9},{9,8},{10,11... | collective-permute-start | bytes 786440 | tf_op jit(solution)/shard_map/ppermute | solution.py:297
  86.0 20.5 %collective-permute-start.27 = (bf16[8,128,128]{2,1,0:T(8,128)(2,1)S(1)}, bf16[8,128,128]{2,1,0:T(8,128)(2,1)}, u32[]{:S(2)}, u32[]{:S(2)}) collective-permute-start(bf16[8,128,128]{2,1,0:T(8,128)(2,1)S(1)} %collective-permute-done.26.refs_8_), channel_id=1, source_target_pairs={{0,1},{1,0},{2,3},{3,2},{4,5},{5,4},{6,7},{7,6},{8,9},{9,8},{10,11... | collective-permute-start | bytes 786440 | tf_op jit(solution)/shard_map/ppermute | solution.py:297
  (18 other events, 163.4 us)

commit v2 on v0

v2 whole, which is shorter than its diff:
```python
import functools

import jax
import jax.numpy as jnp
from jax import lax
from jax.experimental import pallas as pl
from jax.experimental.pallas import tpu as pltpu
from jax.sharding import PartitionSpec as P

MOMENTUM = 0.9
CLIP_LEVEL = 3.0
EPSILON = 1e-06
BF16 = jnp.bfloat16
F32 = jnp.float32
HALF = 8
BLOCK = 16
GROUPS = ((2, 1), (3, 0))
RETURNED = (0, 1, 3, 2)
MIB = 2**20


def dp_index(z, x, core):
    return (z * 4 + x) * 2 + core


def each_dp():
    return [(d, d // 8, (d // 2) % 4, d % 2) for d in range(32)]


def swap_core():
    return [(d, d ^ 1) for d in range(32)]


def along(axis, move):
    pairs = []
    for d, z, x, core in each_dp():
        on_x = (core == 0) == (axis == 0)
        to = dp_index(z, move(x), core) if on_x else dp_index(move(z), x, core)
        pairs.append((d, to))
    return pairs


def shift_first(k):
    return along(0, lambda p: (p + k) % 4)


def swap_first(mask):
    return along(0, lambda p: p ^ mask)


def swap_second(mask):
    return along(1, lambda p: p ^ mask)


def swap_tensor(mask):
    return [(i, i ^ mask) for i in range(4)]


def after(array, earlier):
    return lax.optimization_barrier((array, earlier))[0]


def send(array, pairs, axis="dp"):
    return lax.ppermute(array, axis, pairs)


def places():
    dp = lax.axis_index("dp")
    z, x, core = lax.div(dp, 8), lax.rem(lax.div(dp, 2), 4), lax.rem(dp, 2)
    return core, jnp.where(core == 0, x, z), jnp.where(core == 0, z, x)


def block_of(side, shift):
    core, mine, theirs = places()
    if side:
        core, mine = 1 - core, theirs
    return core * 4 + lax.rem(mine + shift + 4, 4)


def spec_of(tiles, index_map):
    return pl.BlockSpec((tiles, 128, 128), index_map)


def tiles_shape(count):
    return jax.ShapeDtypeStruct((count, 128, 128), BF16)


def params(mib=40):
    return pltpu.CompilerParams(vmem_limit_bytes=mib * MIB)


def cost(tiles_read_or_written):
    return pl.CostEstimate(
        flops=tiles_read_or_written * 16384,
        bytes_accessed=tiles_read_or_written * 32768,
        transcendentals=0,
    )


def outgoing_kernel(side, shifts, bitmap_hbm, g_hbm, r_hbm, out_ref, bitmap, g_ref, r_ref, sems):
    firsts = [block_of(side, k) * BLOCK + h * HALF for k in shifts for h in range(2)]
    chosen = pltpu.make_async_copy(bitmap_hbm, bitmap, sems.at[0, 0])
    chosen.start()
    copies = []
    for i, first in enumerate(firsts):
        rows, place = pl.ds(first, HALF), pl.ds(i * HALF, HALF)
        for j, (source, target) in enumerate(((g_hbm, g_ref), (r_hbm, r_ref))):
            copy = pltpu.make_async_copy(source.at[rows], target.at[place], sems.at[i + 1, j])
            copy.start()
            copies.append(copy)
    chosen.wait()
    for i, first in enumerate(firsts):
        copies[2 * i].wait()
        copies[2 * i + 1].wait()
        for t in range(HALF):
            place = i * HALF + t
            value = (g_ref[place].astype(F32) + r_ref[place].astype(F32)).astype(BF16)
            out_ref[place] = jnp.where(bitmap[0, first + t] > 0, value, jnp.zeros_like(value))


def outgoing(side, shifts, bitmap, gradients, residual):
    tiles = len(shifts) * BLOCK
    return pl.pallas_call(
        functools.partial(outgoing_kernel, side, shifts),
        in_specs=[pl.BlockSpec(memory_space=pl.ANY)] * 3,
        out_specs=pl.BlockSpec(memory_space=pltpu.VMEM),
        out_shape=tiles_shape(tiles),
        scratch_shapes=[
            pltpu.SMEM((1, 128), jnp.int32),
            pltpu.VMEM((tiles, 128, 128), BF16),
            pltpu.VMEM((tiles, 128, 128), BF16),
            pltpu.SemaphoreType.DMA((2 * len(shifts) + 1, 2)),
        ],
        compiler_params=params(),
        cost_estimate=cost(3 * tiles),
    )(bitmap, gradients, residual)


def left_kernel(after_ref, bitmap_ref, g_ref, r_ref, out_ref, token_ref):
    first = pl.program_id(0) * BLOCK
    for t in range(BLOCK):
        value = (g_ref[t].astype(F32) + r_ref[t].astype(F32)).astype(BF16)
        out_ref[t] = jnp.where(bitmap_ref[0, first + t] > 0, jnp.zeros_like(value), value)
    token_ref[...] = jnp.zeros_like(token_ref)


def left_over(after, bitmap, gradients, residual):
    block = spec_of(BLOCK, lambda i: (i, 0, 0))
    return pl.pallas_call(
        left_kernel,
        grid=(8,),
        in_specs=[
            pl.BlockSpec(memory_space=pl.ANY),
            pl.BlockSpec(memory_space=pltpu.SMEM),
            block,
            block,
        ],
        out_specs=[block, pl.BlockSpec((8, 128), lambda i: (0, 0))],
        out_shape=[tiles_shape(128), jax.ShapeDtypeStruct((8, 128), F32)],
        compiler_params=params(),
        cost_estimate=cost(3 * 128),
    )(after, bitmap, gradients, residual)


def pair_kernel(a_ref, b_ref, *out_refs):
    for k, out_ref in enumerate(out_refs):

        @pl.when(pl.program_id(0) == k)
        def _():
            out_ref[...] = (a_ref[...].astype(F32) + b_ref[...].astype(F32)).astype(BF16)


def pair_sums(a, b):
    count = a.shape[0] // BLOCK
    return pl.pallas_call(
        pair_kernel,
        grid=(count,),
        in_specs=[spec_of(BLOCK, lambda i: (i, 0, 0))] * 2,
        out_specs=[spec_of(BLOCK, lambda i: (0, 0, 0))] * count,
        out_shape=[tiles_shape(BLOCK)] * count,
        compiler_params=params(),
        cost_estimate=cost(3 * count * BLOCK),
    )(a, b)


def total_kernel(after_ref, r0, r1, r2, r3, low_ref, high_ref):
    for t in range(BLOCK):
        total = (r0[t].astype(F32) + r2[t].astype(F32)) + (r1[t].astype(F32) + r3[t].astype(F32))
        out_ref = low_ref if t < HALF else high_ref
        out_ref[t % HALF] = total.astype(BF16)


def block_total(after, *blocks):
    return pl.pallas_call(
        total_kernel,
        in_specs=[pl.BlockSpec(memory_space=pl.ANY)] + [spec_of(BLOCK, lambda: (0, 0, 0))] * 4,
        out_specs=[spec_of(HALF, lambda: (0, 0, 0))] * 2,
        out_shape=[tiles_shape(HALF)] * 2,
        compiler_params=params(),
        cost_estimate=cost(5 * BLOCK),
    )(after, *blocks)


def halves_kernel(a0, a1, b0, b1, low_ref, high_ref):
    for t in range(HALF):
        low_ref[t] = (a0[t].astype(F32) + a1[t].astype(F32)).astype(BF16)
        high_ref[t] = (b0[t].astype(F32) + b1[t].astype(F32)).astype(BF16)


def halves_sum(*halves):
    return pl.pallas_call(
        halves_kernel,
        in_specs=[spec_of(HALF, lambda: (0, 0, 0))] * 4,
        out_specs=[spec_of(HALF, lambda: (0, 0, 0))] * 2,
        out_shape=[tiles_shape(HALF)] * 2,
        compiler_params=params(),
        cost_estimate=cost(6 * HALF),
    )(*halves)


def last_kernel(lo_ref, hi_ref, a0, a1, b0, b1, out_ref, row_ref):
    shard = lax.axis_index("tensor")
    lo, hi = lo_ref[pl.ds(shard, 1), :], hi_ref[pl.ds(shard, 1), :]
    first = block_of(0, 0) * BLOCK
    row = jnp.zeros((1, 128), F32)
    for t in range(BLOCK):
        left, right = (a0, a1) if t < HALF else (b0, b1)
        total = left[t % HALF].astype(F32) + right[t % HALF].astype(F32)
        out_ref[t] = total.astype(BF16)
        square = jnp.sum(jnp.sum(total * total, axis=0, keepdims=True), axis=1, keepdims=True)
        row = row + jnp.where((lo <= first + t) & (first + t < hi), square, 0.0)
    row_ref[...] = jnp.broadcast_to(row, (8, 128))


def last_sum(lo, hi, *halves):
    return pl.pallas_call(
        last_kernel,
        out_shape=[tiles_shape(BLOCK), jax.ShapeDtypeStruct((8, 128), F32)],
        compiler_params=params(),
        cost_estimate=cost(6 * HALF),
    )(lo, hi, *halves)


def final_kernel(lo_ref, hi_ref, mine_ref, other_ref, m_ref, *refs):
    blocks, (out_ref, factor_ref, ready_ref, sems) = refs[:8], refs[8:]
    shard = lax.axis_index("tensor")
    lo, hi = lo_ref[pl.ds(shard, 1), :], hi_ref[pl.ds(shard, 1), :]
    count = jnp.sum((hi_ref[...] - lo_ref[...]).astype(F32), axis=0, keepdims=True)
    squares = mine_ref[0:1, :] + other_ref[0:1, :]
    rms = jnp.sqrt(squares / (jnp.maximum(count, 1.0) * 16384.0) + EPSILON)
    clip = jnp.minimum(1.0, CLIP_LEVEL / rms)
    tile = lax.broadcasted_iota(jnp.int32, (128, 128), 0)
    chosen = jnp.where((lo <= tile) & (tile < hi), clip, 0.0)
    factor_ref[...] = jnp.broadcast_to(jnp.sum(chosen, axis=1, keepdims=True), (128, 128))

    copies = []
    for k, block in enumerate(blocks):
        first = block_of(k % 2, -RETURNED[k // 2]) * BLOCK

        def one_tile(t, carry):
            factor = factor_ref[pl.ds(first + t, 1), :]
            update = block[t].astype(F32) * factor
            new = MOMENTUM * m_ref[first + t].astype(F32) + update
            ready_ref[k * BLOCK + t] = new.astype(BF16)
            return carry

        lax.fori_loop(0, BLOCK, one_tile, 0, unroll=4)
        copies.append(
            pltpu.make_async_copy(
                ready_ref.at[pl.ds(k * BLOCK, BLOCK)],
                out_ref.at[pl.ds(first, BLOCK)],
                sems.at[k],
            )
        )
        copies[-1].start()
    for copy in copies:
        copy.wait()


def finish(lo, hi, mine, other, momentum, blocks):
    whole = pl.BlockSpec(memory_space=pltpu.VMEM)
    return pl.pallas_call(
        final_kernel,
        in_specs=[whole] * (5 + len(blocks)),
        out_specs=pl.BlockSpec(memory_space=pl.ANY),
        scratch_shapes=[
            pltpu.VMEM((128, 128), F32),
            pltpu.VMEM((128, 128, 128), BF16),
            pltpu.SemaphoreType.DMA((8,)),
        ],
        out_shape=tiles_shape(128),
        compiler_params=params(20),
        cost_estimate=cost(3 * 128),
    )(lo, hi, mine, other, momentum, *blocks)


def shards(gradients, residual, momentum, bitmap, starts):
    gradients, residual = gradients[0], residual[0]
    lo = jnp.pad(starts, ((0, 0), (0, 96)), constant_values=128)
    hi = jnp.pad(starts[:, 1:], ((0, 0), (0, 97)), constant_values=128)

    gradients = pltpu.with_memory_space_constraint(gradients, pltpu.HBM)
    residual = pltpu.with_memory_space_constraint(residual, pltpu.HBM)
    bitmap = pltpu.with_memory_space_constraint(bitmap, pltpu.HBM)
    arrays = (bitmap, gradients, residual)
    swapped = [send(outgoing(1, shifts, *arrays), swap_core()) for shifts in GROUPS]
    kept = [outgoing(0, shifts, *arrays) for shifts in GROUPS]
    first = pair_sums(kept[0], swapped[0])
    by_two = send(first[0], shift_first(2))
    by_one = send(first[1], shift_first(1))
    second = pair_sums(kept[1], swapped[1])
    by_three = send(second[0], shift_first(3))
    left, token = left_over(second[0], *arrays)

    low, high = block_total(token, second[1], by_one, by_two, by_three)
    low, high = halves_sum(low, send(low, swap_second(1)), high, send(high, swap_second(3)))
    full, row = last_sum(lo, hi, low, send(low, swap_second(3)), high, send(high, swap_second(1)))

    returned = {2: send(full, shift_first(2))}
    row = row + send(row, swap_tensor(1), "tensor")
    full = after(full, row)
    returned[1] = send(full, shift_first(1))
    row = row + send(row, swap_tensor(3), "tensor")
    full = after(full, row)
    returned[3] = send(full, shift_first(3))
    for mask in (1, 3):
        row = row + send(row, swap_first(mask))
    other = send(row, swap_core())

    blocks = [full, send(full, swap_core())]
    for k in RETURNED[1:]:
        blocks += [returned[k], send(after(returned[k], row), swap_core())]
    return (left[None], finish(lo, hi, row, other, momentum, blocks))


def solution(mesh):
    return jax.shard_map(
        shards,
        mesh=mesh,
        in_specs=(
            P("dp", "tensor", None, None),
            P("dp", "tensor", None, None),
            P("tensor", None, None),
            P("dp", "tensor"),
            P(),
        ),
        out_specs=(P("dp", "tensor", None, None), P("tensor", None, None)),
        check_vma=False,
    )
```

time: 220 us -> 79.7 us (0.36)
  waiting for transfers between devices: 132 us -> 30.4 us
  other arithmetic: 33.6 us -> 0.01 us
  starting transfers between devices: 9.52 us -> 29.4 us
  local copies, waits for them, and re-layouts: 18.9 us -> 0.09 us
  Pallas kernels: 0 us -> 18.7 us
  between operations: 15.4 us -> 0.76 us
  blocking collectives: 9.33 us -> 0 us
    all_to_all x1 -> x0, waiting for transfers between devices: 85.5 us -> none  [shards(): lax.all_to_all(packed_tiles, 'dp', split_axis=0, concat_axis=0, tiled=True)]
    all_gather x1 -> x0, waiting for transfers between devices: 46.8 us -> none  [shards(): returned = lax.all_gather(update_tiles, 'dp', axis=0, tiled=True)]
    ppermute x0 -> x21, waiting for transfers between devices: none -> 30.4 us  [send(): return lax.ppermute(array, axis, pairs)]
    ppermute x0 -> x21, starting transfers between devices: none -> 29.4 us  [send(): return lax.ppermute(array, axis, pairs)]
    select_n x5 -> x0, other arithmetic: 19.1 us -> none  [the longest x1 6.81 us: shards(): jnp.where(slot_valid[:, :, None, None], packed_tiles, jnp.zeros_like(pack...]
    pallas_call x0 -> x11, Pallas kernels: none -> 18.7 us  [the longest x1 8.05 us: left_over(): pl.pallas_call(left_kernel, grid=(8,), in_specs=[pl.BlockSpec(memory_spac...]
    gather x2 -> x0, local copies, waits for them, and re-layouts: 16.8 us -> none  [the longest x1 10.6 us: shards(): jnp.take(outgoing, source_rows.reshape(-1), axis=0)]
    all_to_all x1 -> x0, starting transfers between devices: 9.48 us -> none  [shards(): lax.all_to_all(packed_tiles, 'dp', split_axis=0, concat_axis=0, tiled=True)]
  transfers between devices with their start and end apart: 2 -> 21, of which waited for: 2 -> 10; matrix products, arithmetic and copies ran while one was open for 3% -> 0% of each run, Pallas kernels for 0% -> 17%
where the time goes in v2:
time: 79.7 us; the launch traced here: 79.3 us
  waiting for transfers between devices  30.4 us (38%)
  starting transfers between devices  29.4 us (37%)
  Pallas kernels  18.7 us (23%)
    ppermute x21, waiting for transfers between devices, send(): return lax.ppermute(array, axis, pairs)  30.4 us
    ppermute x21, starting transfers between devices, send(): return lax.ppermute(array, axis, pairs)  29.4 us
    pallas_call x1, Pallas kernels, left_over(): pl.pallas_call(left_kernel, grid=(8,), in_specs=[pl.BlockSpec(memory_spac...  8.05 us
    pallas_call x4, Pallas kernels, outgoing(): pl.pallas_call(functools.partial(outgoing_kernel, side, shifts), in_specs...  6.76 us
    pallas_call x1, Pallas kernels, finish(): pl.pallas_call(final_kernel, in_specs=[whole] * (5 + len(blocks)), out_sp...  2.67 us
  transfers between devices with their start and end apart: 21, of which 10 were waited for; matrix products, arithmetic and copies ran while one was open for 0% of the time, Pallas kernels for 17%

profile of v2, /device:TPU:1, one launch (start us, length us, event | category | flops | bytes accessed | tf_op | source)
XLA Modules:
  0.0 79.3 jit_solution(12378096407310017614)
XLA Ops:
  0.6 1.7 %shard_map.69 = bf16[32,128,128]{2,1,0:T(8,128)(2,1)S(1)} custom-call(s32[1,128]{1,0:T(1,128)} %bitmap_hbm.7, bf16[128,128,128]{2,1,0:T(8,128)(2,1)} %bitcast.3, bf16[128,128,128]{2,1,0:T(8,128)(2,1)} %bitcast.8), custom_call_target="tpu_custom_call" | custom-call | flops 1572864 | bytes 3145728 | tf_op jit(solution)/shard_map/pallas_call | solution.py:123
  2.3 1.5 %collective-permute-start = (bf16[32,128,128]{2,1,0:T(8,128)(2,1)S(1)}, bf16[32,128,128]{2,1,0:T(8,128)(2,1)S(1)}, u32[]{:S(2)}, u32[]{:S(2)}) collective-permute-start(bf16[32,128,128]{2,1,0:T(8,128)(2,1)S(1)} %shard_map.69), channel_id=1, source_target_pairs={{0,1},{1,0},{2,3},{3,2},{4,5},{5,4},{6,7},{7,6},{8,9},{9,8},{10,11... | collective-permute-start | bytes 3145736 | tf_op jit(solution)/shard_map/ppermute | solution.py:64
  3.8 1.7 %shard_map.73 = bf16[32,128,128]{2,1,0:T(8,128)(2,1)S(1)} custom-call(s32[1,128]{1,0:T(1,128)} %bitmap_hbm.7, bf16[128,128,128]{2,1,0:T(8,128)(2,1)} %bitcast.4, bf16[128,128,128]{2,1,0:T(8,128)(2,1)} %bitcast.9), custom_call_target="tpu_custom_call" | custom-call | flops 1572864 | bytes 3145728 | tf_op jit(solution)/shard_map/pallas_call | solution.py:123
  5.6 1.7 %shard_map.72.a_ref = bf16[32,128,128]{2,1,0:T(8,128)(2,1)S(1)} custom-call(s32[1,128]{1,0:T(1,128)} %bitmap_hbm.7, bf16[128,128,128]{2,1,0:T(8,128)(2,1)} %bitcast.5, bf16[128,128,128]{2,1,0:T(8,128)(2,1)} %bitcast.10), custom_call_target="tpu_custom_call" | custom-call | flops 1572864 | bytes 3145728 | tf_op jit(solution)/shard_map/pallas_call | solution.py:123
  7.3 1.7 %shard_map.68.a_ref = bf16[32,128,128]{2,1,0:T(8,128)(2,1)S(1)} custom-call(s32[1,128]{1,0:T(1,128)} %bitmap_hbm.7, bf16[128,128,128]{2,1,0:T(8,128)(2,1)} %bitcast.6, bf16[128,128,128]{2,1,0:T(8,128)(2,1)} %bitcast.11), custom_call_target="tpu_custom_call" | custom-call | flops 1572864 | bytes 3145728 | tf_op jit(solution)/shard_map/pallas_call | solution.py:123
  9.4 3.9 %collective-permute-start.4 = (bf16[16,128,128]{2,1,0:T(8,128)(2,1)S(1)}, bf16[16,128,128]{2,1,0:T(8,128)(2,1)S(1)}, u32[]{:S(2)}, u32[]{:S(2)}) collective-permute-start(bf16[16,128,128]{2,1,0:T(8,128)(2,1)S(1)} %get-tuple-element.19.after_ref), channel_id=1, source_target_pairs={{0,6},{1,25},{2,0},{3,27},{4,2},{5,29},{6,4},{7,31},{8,14},{9,1},{... | collective-permute-start | bytes 1572872 | tf_op jit(solution)/shard_map/ppermute | solution.py:64
  14.9 8.1 %shard_map.71 = (bf16[128,128,128]{2,1,0:T(8,128)(2,1)}, f32[8,128]{1,0:T(8,128)S(1)}) custom-call(bf16[16,128,128]{2,1,0:T(8,128)(2,1)S(1)} %get-tuple-element.19.after_ref, s32[1,128]{1,0:T(1,128)} %bitmap_hbm.7, bf16[128,128,128]{2,1,0:T(8,128)(2,1)} %bitcast.7, bf16[128,128,128]{2,1,0:T(8,128)(2,1)} %bitcast.12), custom_call_target="tpu_custom_call" | custom-call | flops 6291456 | bytes 12582912 | tf_op jit(solution)/shard_map/pallas_call | solution.py:149
  23.0 2.0 %collective-permute-done.4.r3 = bf16[16,128,128]{2,1,0:T(8,128)(2,1)S(1)} collective-permute-done((bf16[16,128,128]{2,1,0:T(8,128)(2,1)S(1)}, bf16[16,128,128]{2,1,0:T(8,128)(2,1)S(1)}, u32[]{:S(2)}, u32[]{:S(2)}) %collective-permute-start.4) | collective-permute-done | bytes 524320 | tf_op jit(solution)/shard_map/ppermute | solution.py:64
  25.0 3.7 %collective-permute-done.2.r1 = bf16[16,128,128]{2,1,0:T(8,128)(2,1)S(1)} collective-permute-done((bf16[16,128,128]{2,1,0:T(8,128)(2,1)S(1)}, bf16[16,128,128]{2,1,0:T(8,128)(2,1)S(1)}, u32[]{:S(2)}, u32[]{:S(2)}) %collective-permute-start.2) | collective-permute-done | bytes 524320 | tf_op jit(solution)/shard_map/ppermute | solution.py:64
  30.1 1.8 %collective-permute-start.6 = (bf16[8,128,128]{2,1,0:T(8,128)(2,1)S(1)}, bf16[8,128,128]{2,1,0:T(8,128)(2,1)S(1)}, u32[]{:S(2)}, u32[]{:S(2)}) collective-permute-start(bf16[8,128,128]{2,1,0:T(8,128)(2,1)S(1)} %get-tuple-element.26.b0), channel_id=1, source_target_pairs={{0,24},{1,7},{2,26},{3,5},{4,28},{5,3},{6,30},{7,1},{8,16},{9,15},... | collective-permute-start | bytes 786440 | tf_op jit(solution)/shard_map/ppermute | solution.py:64
  31.9 2.7 %collective-permute-done.5.a1 = bf16[8,128,128]{2,1,0:T(8,128)(2,1)S(1)} collective-permute-done((bf16[8,128,128]{2,1,0:T(8,128)(2,1)S(1)}, bf16[8,128,128]{2,1,0:T(8,128)(2,1)S(1)}, u32[]{:S(2)}, u32[]{:S(2)}) %collective-permute-start.5) | collective-permute-done | bytes 262176 | tf_op jit(solution)/shard_map/ppermute | solution.py:64
  34.6 2.2 %collective-permute-done.6.b1 = bf16[8,128,128]{2,1,0:T(8,128)(2,1)S(1)} collective-permute-done((bf16[8,128,128]{2,1,0:T(8,128)(2,1)S(1)}, bf16[8,128,128]{2,1,0:T(8,128)(2,1)S(1)}, u32[]{:S(2)}, u32[]{:S(2)}) %collective-permute-start.6) | collective-permute-done | bytes 262176 | tf_op jit(solution)/shard_map/ppermute | solution.py:64
  36.9 1.6 %collective-permute-start.7 = (bf16[8,128,128]{2,1,0:T(8,128)(2,1)S(1)}, bf16[8,128,128]{2,1,0:T(8,128)(2,1)S(1)}, u32[]{:S(2)}, u32[]{:S(2)}) collective-permute-start(bf16[8,128,128]{2,1,0:T(8,128)(2,1)S(1)} %get-tuple-element.27.a0), channel_id=1, source_target_pairs={{0,24},{1,7},{2,26},{3,5},{4,28},{5,3},{6,30},{7,1},{8,16},{9,15},... | collective-permute-start | bytes 786440 | tf_op jit(solution)/shard_map/ppermute | solution.py:64
  38.6 5.1 %collective-permute-done.7.a1 = bf16[8,128,128]{2,1,0:T(8,128)(2,1)S(1)} collective-permute-done((bf16[8,128,128]{2,1,0:T(8,128)(2,1)S(1)}, bf16[8,128,128]{2,1,0:T(8,128)(2,1)S(1)}, u32[]{:S(2)}, u32[]{:S(2)}) %collective-permute-start.7) | collective-permute-done | bytes 262176 | tf_op jit(solution)/shard_map/ppermute | solution.py:64
  44.3 1.4 %collective-permute-start.9 = (f32[8,128]{1,0:T(8,128)S(1)}, f32[8,128]{1,0:T(8,128)S(1)}, u32[]{:S(2)}, u32[]{:S(2)}) collective-permute-start(f32[8,128]{1,0:T(8,128)S(1)} %get-tuple-element.29), channel_id=1, source_target_pairs={{0,32},{32,0},{64,96},{96,64},{1,33},{33,1},{65,97},{97,65},{2,34}... | collective-permute-start | bytes 12296 | tf_op jit(solution)/shard_map/ppermute | solution.py:64
  45.7 1.5 %collective-permute-done.9 = f32[8,128]{1,0:T(8,128)S(1)} collective-permute-done((f32[8,128]{1,0:T(8,128)S(1)}, f32[8,128]{1,0:T(8,128)S(1)}, u32[]{:S(2)}, u32[]{:S(2)}) %collective-permute-start.9) | collective-permute-done | bytes 4128 | tf_op jit(solution)/shard_map/ppermute | solution.py:64
  47.1 2.7 %collective-permute-start.10 = (f32[8,128]{1,0:T(8,128)S(1)}, f32[8,128]{1,0:T(8,128)S(1)}, u32[]{:S(2)}, u32[]{:S(2)}) collective-permute-start(f32[8,128]{1,0:T(8,128)S(1)} %add.16), channel_id=1, source_target_pairs={{0,96},{32,64},{64,32},{96,0},{1,97},{33,65},{65,33},{97,1},{2,98}... | collective-permute-start | bytes 12296 | tf_op jit(solution)/shard_map/ppermute | solution.py:64
  50.9 2.1 %collective-permute-start.17 = (bf16[16,128,128]{2,1,0:T(8,128)(2,1)S(1)}, bf16[16,128,128]{2,1,0:T(8,128)(2,1)S(1)}, u32[]{:S(2)}, u32[]{:S(2)}) collective-permute-start(bf16[16,128,128]{2,1,0:T(8,128)(2,1)S(1)} %get-tuple-element.32.refs_0_), channel_id=1, source_target_pairs={{0,6},{1,25},{2,0},{3,27},{4,2},{5,29},{6,4},{7,31},{8,14},{9,1},{... | collective-permute-start | bytes 1572872 | tf_op jit(solution)/shard_map/ppermute | solution.py:64
  53.0 9.8 %collective-permute-done.11 = f32[8,128]{1,0:T(8,128)S(1)} collective-permute-done((f32[8,128]{1,0:T(8,128)S(1)}, f32[8,128]{1,0:T(8,128)S(1)}, u32[]{:S(2)}, u32[]{:S(2)}) %collective-permute-start.11) | collective-permute-done | bytes 4128 | tf_op jit(solution)/shard_map/ppermute | solution.py:64
  62.8 2.9 %collective-permute-start.12 = (f32[8,128]{1,0:T(8,128)S(1)}, f32[8,128]{1,0:T(8,128)S(1)}, u32[]{:S(2)}, u32[]{:S(2)}) collective-permute-start(f32[8,128]{1,0:T(8,128)S(1)} %add.18), channel_id=1, source_target_pairs={{0,6},{1,25},{2,4},{3,27},{4,2},{5,29},{6,0},{7,31},{8,14},{9,17},... | collective-permute-start | bytes 12296 | tf_op jit(solution)/shard_map/ppermute | solution.py:64
  65.7 6.3 %collective-permute-start.14 = (bf16[16,128,128]{2,1,0:T(8,128)(2,1)S(1)}, bf16[16,128,128]{2,1,0:T(8,128)(2,1)S(1)}, u32[]{:S(2)}, u32[]{:S(2)}) collective-permute-start(bf16[16,128,128]{2,1,0:T(8,128)(2,1)S(1)} %get-tuple-element.32.refs_0_), channel_id=1, source_target_pairs={{0,1},{1,0},{2,3},{3,2},{4,5},{5,4},{6,7},{7,6},{8,9},{9,8},{10,11... | collective-permute-start | bytes 1572872 | tf_op jit(solution)/shard_map/ppermute | solution.py:64
  72.0 1.6 %collective-permute-start.20 = (bf16[16,128,128]{2,1,0:T(8,128)(2,1)S(1)}, bf16[16,128,128]{2,1,0:T(8,128)(2,1)S(1)}, u32[]{:S(2)}, u32[]{:S(2)}) collective-permute-start(bf16[16,128,128]{2,1,0:T(8,128)(2,1)S(1)} %collective-permute-done.19.refs_6_), channel_id=1, source_target_pairs={{0,1},{1,0},{2,3},{3,2},{4,5},{5,4},{6,7},{7,6},{8,9},{9,8},{10,11... | collective-permute-start | bytes 1572872 | tf_op jit(solution)/shard_map/ppermute | solution.py:64
  74.2 2.4 %collective-permute-done.13.other_ref = f32[8,128]{1,0:T(8,128)S(1)} collective-permute-done((f32[8,128]{1,0:T(8,128)S(1)}, f32[8,128]{1,0:T(8,128)S(1)}, u32[]{:S(2)}, u32[]{:S(2)}) %collective-permute-start.13) | collective-permute-done | bytes 4128 | tf_op jit(solution)/shard_map/ppermute | solution.py:64
  76.6 2.7 %shard_map.78 = bf16[128,128,128]{2,1,0:T(8,128)(2,1)} custom-call(s32[4,128]{1,0:T(4,128)S(1)} %pad.8.lo_ref, s32[4,128]{1,0:T(4,128)S(1)} %pad.9.hi_ref, f32[8,128]{1,0:T(8,128)S(1)} %add.19.mine_ref, f32[8,128]{1,0:T(8,128)S(1)} %collective-permute-done.13.other_ref, bf16[128,128,128]{2,1,0:T(8,128)(2,1)S(1)} %copy-done, ...), custom_call_target="tpu_custom_call" | custom-call | flops 6291456 | bytes 12582912 | tf_op jit(solution)/shard_map/pallas_call | solution.py:282
  (40 shorter events, 5.8 us)
Async XLA Ops:
  2.3 6.7 %collective-permute-start = (bf16[32,128,128]{2,1,0:T(8,128)(2,1)S(1)}, bf16[32,128,128]{2,1,0:T(8,128)(2,1)S(1)}, u32[]{:S(2)}, u32[]{:S(2)}) collective-permute-start(bf16[32,128,128]{2,1,0:T(8,128)(2,1)S(1)} %shard_map.69), channel_id=1, source_target_pairs={{0,1},{1,0},{2,3},{3,2},{4,5},{5,4},{6,7},{7,6},{8,9},{9,8},{10,11... | collective-permute-start | bytes 3145736 | tf_op jit(solution)/shard_map/ppermute | solution.py:64
  5.5 7.8 %collective-permute-start.1 = (bf16[32,128,128]{2,1,0:T(8,128)(2,1)S(1)}, bf16[32,128,128]{2,1,0:T(8,128)(2,1)S(1)}, u32[]{:S(2)}, u32[]{:S(2)}) collective-permute-start(bf16[32,128,128]{2,1,0:T(8,128)(2,1)S(1)} %shard_map.73), channel_id=1, source_target_pairs={{0,1},{1,0},{2,3},{3,2},{4,5},{5,4},{6,7},{7,6},{8,9},{9,8},{10,11... | collective-permute-start | bytes 3145736 | tf_op jit(solution)/shard_map/ppermute | solution.py:64
  9.4 15.7 %collective-permute-start.4 = (bf16[16,128,128]{2,1,0:T(8,128)(2,1)S(1)}, bf16[16,128,128]{2,1,0:T(8,128)(2,1)S(1)}, u32[]{:S(2)}, u32[]{:S(2)}) collective-permute-start(bf16[16,128,128]{2,1,0:T(8,128)(2,1)S(1)} %get-tuple-element.19.after_ref), channel_id=1, source_target_pairs={{0,6},{1,25},{2,0},{3,27},{4,2},{5,29},{6,4},{7,31},{8,14},{9,1},{... | collective-permute-start | bytes 1572872 | tf_op jit(solution)/shard_map/ppermute | solution.py:64
  13.6 15.1 %collective-permute-start.2 = (bf16[16,128,128]{2,1,0:T(8,128)(2,1)S(1)}, bf16[16,128,128]{2,1,0:T(8,128)(2,1)S(1)}, u32[]{:S(2)}, u32[]{:S(2)}) collective-permute-start(bf16[16,128,128]{2,1,0:T(8,128)(2,1)S(1)} %get-tuple-element.23), channel_id=1, source_target_pairs={{0,2},{1,9},{2,4},{3,11},{4,6},{5,13},{6,0},{7,15},{8,10},{9,17},{... | collective-permute-start | bytes 1572872 | tf_op jit(solution)/shard_map/ppermute | solution.py:64
  13.6 24.9 %copy-start.1 = (s32[4,32]{1,0:T(4,128)S(1)}, s32[4,32]{1,0:T(4,128)}, u32[]{:S(2)}) copy-start(s32[4,32]{1,0:T(4,128)} %param.9) | copy-start | bytes 1540
  13.7 15.0 %collective-permute-start.3 = (bf16[16,128,128]{2,1,0:T(8,128)(2,1)S(1)}, bf16[16,128,128]{2,1,0:T(8,128)(2,1)S(1)}, u32[]{:S(2)}, u32[]{:S(2)}) collective-permute-start(bf16[16,128,128]{2,1,0:T(8,128)(2,1)S(1)} %get-tuple-element.24), channel_id=1, source_target_pairs={{0,4},{1,17},{2,6},{3,19},{4,0},{5,21},{6,2},{7,23},{8,12},{9,25},... | collective-permute-start | bytes 1572872 | tf_op jit(solution)/shard_map/ppermute | solution.py:64
  23.0 53.6 %copy-start = (bf16[128,128,128]{2,1,0:T(8,128)(2,1)S(1)}, bf16[128,128,128]{2,1,0:T(8,128)(2,1)}, u32[]{:S(2)}) copy-start(bf16[128,128,128]{2,1,0:T(8,128)(2,1)} %m_ref.1) | copy-start | bytes 12582916
  29.0 5.6 %collective-permute-start.5 = (bf16[8,128,128]{2,1,0:T(8,128)(2,1)S(1)}, bf16[8,128,128]{2,1,0:T(8,128)(2,1)S(1)}, u32[]{:S(2)}, u32[]{:S(2)}) collective-permute-start(bf16[8,128,128]{2,1,0:T(8,128)(2,1)S(1)} %get-tuple-element.25.a0), channel_id=1, source_target_pairs={{0,8},{1,3},{2,10},{3,1},{4,12},{5,7},{6,14},{7,5},{8,0},{9,11},{1... | collective-permute-start | bytes 786440 | tf_op jit(solution)/shard_map/ppermute | solution.py:64
  30.1 6.7 %collective-permute-start.6 = (bf16[8,128,128]{2,1,0:T(8,128)(2,1)S(1)}, bf16[8,128,128]{2,1,0:T(8,128)(2,1)S(1)}, u32[]{:S(2)}, u32[]{:S(2)}) collective-permute-start(bf16[8,128,128]{2,1,0:T(8,128)(2,1)S(1)} %get-tuple-element.26.b0), channel_id=1, source_target_pairs={{0,24},{1,7},{2,26},{3,5},{4,28},{5,3},{6,30},{7,1},{8,16},{9,15},... | collective-permute-start | bytes 786440 | tf_op jit(solution)/shard_map/ppermute | solution.py:64
  36.9 6.8 %collective-permute-start.7 = (bf16[8,128,128]{2,1,0:T(8,128)(2,1)S(1)}, bf16[8,128,128]{2,1,0:T(8,128)(2,1)S(1)}, u32[]{:S(2)}, u32[]{:S(2)}) collective-permute-start(bf16[8,128,128]{2,1,0:T(8,128)(2,1)S(1)} %get-tuple-element.27.a0), channel_id=1, source_target_pairs={{0,24},{1,7},{2,26},{3,5},{4,28},{5,3},{6,30},{7,1},{8,16},{9,15},... | collective-permute-start | bytes 786440 | tf_op jit(solution)/shard_map/ppermute | solution.py:64
  38.5 5.5 %collective-permute-start.8 = (bf16[8,128,128]{2,1,0:T(8,128)(2,1)S(1)}, bf16[8,128,128]{2,1,0:T(8,128)(2,1)S(1)}, u32[]{:S(2)}, u32[]{:S(2)}) collective-permute-start(bf16[8,128,128]{2,1,0:T(8,128)(2,1)S(1)} %get-tuple-element.28.b0), channel_id=1, source_target_pairs={{0,8},{1,3},{2,10},{3,1},{4,12},{5,7},{6,14},{7,5},{8,0},{9,11},{1... | collective-permute-start | bytes 786440 | tf_op jit(solution)/shard_map/ppermute | solution.py:64
  44.3 2.8 %collective-permute-start.9 = (f32[8,128]{1,0:T(8,128)S(1)}, f32[8,128]{1,0:T(8,128)S(1)}, u32[]{:S(2)}, u32[]{:S(2)}) collective-permute-start(f32[8,128]{1,0:T(8,128)S(1)} %get-tuple-element.29), channel_id=1, source_target_pairs={{0,32},{32,0},{64,96},{96,64},{1,33},{33,1},{65,97},{97,65},{2,34}... | collective-permute-start | bytes 12296 | tf_op jit(solution)/shard_map/ppermute | solution.py:64
  47.1 3.7 %collective-permute-start.10 = (f32[8,128]{1,0:T(8,128)S(1)}, f32[8,128]{1,0:T(8,128)S(1)}, u32[]{:S(2)}, u32[]{:S(2)}) collective-permute-start(f32[8,128]{1,0:T(8,128)S(1)} %add.16), channel_id=1, source_target_pairs={{0,96},{32,64},{64,32},{96,0},{1,97},{33,65},{65,33},{97,1},{2,98}... | collective-permute-start | bytes 12296 | tf_op jit(solution)/shard_map/ppermute | solution.py:64
  49.9 22.1 %collective-permute-start.19 = (bf16[16,128,128]{2,1,0:T(8,128)(2,1)S(1)}, bf16[16,128,128]{2,1,0:T(8,128)(2,1)S(1)}, u32[]{:S(2)}, u32[]{:S(2)}) collective-permute-start(bf16[16,128,128]{2,1,0:T(8,128)(2,1)S(1)} %get-tuple-element.32.refs_0_), channel_id=1, source_target_pairs={{0,4},{1,17},{2,6},{3,19},{4,0},{5,21},{6,2},{7,23},{8,12},{9,25},... | collective-permute-start | bytes 1572872 | tf_op jit(solution)/shard_map/ppermute | solution.py:64
  50.3 23.3 %collective-permute-start.15 = (bf16[16,128,128]{2,1,0:T(8,128)(2,1)S(1)}, bf16[16,128,128]{2,1,0:T(8,128)(2,1)S(1)}, u32[]{:S(2)}, u32[]{:S(2)}) collective-permute-start(bf16[16,128,128]{2,1,0:T(8,128)(2,1)S(1)} %get-tuple-element.32.refs_0_), channel_id=1, source_target_pairs={{0,2},{1,9},{2,4},{3,11},{4,6},{5,13},{6,0},{7,15},{8,10},{9,17},{... | collective-permute-start | bytes 1572872 | tf_op jit(solution)/shard_map/ppermute | solution.py:64
  50.9 22.8 %collective-permute-start.17 = (bf16[16,128,128]{2,1,0:T(8,128)(2,1)S(1)}, bf16[16,128,128]{2,1,0:T(8,128)(2,1)S(1)}, u32[]{:S(2)}, u32[]{:S(2)}) collective-permute-start(bf16[16,128,128]{2,1,0:T(8,128)(2,1)S(1)} %get-tuple-element.32.refs_0_), channel_id=1, source_target_pairs={{0,6},{1,25},{2,0},{3,27},{4,2},{5,29},{6,4},{7,31},{8,14},{9,1},{... | collective-permute-start | bytes 1572872 | tf_op jit(solution)/shard_map/ppermute | solution.py:64
  53.0 9.8 %collective-permute-start.11 = (f32[8,128]{1,0:T(8,128)S(1)}, f32[8,128]{1,0:T(8,128)S(1)}, u32[]{:S(2)}, u32[]{:S(2)}) collective-permute-start(f32[8,128]{1,0:T(8,128)S(1)} %add.17), channel_id=1, source_target_pairs={{0,2},{1,9},{2,0},{3,11},{4,6},{5,13},{6,4},{7,15},{8,10},{9,1},{1... | collective-permute-start | bytes 12296 | tf_op jit(solution)/shard_map/ppermute | solution.py:64
  62.8 9.2 %collective-permute-start.12 = (f32[8,128]{1,0:T(8,128)S(1)}, f32[8,128]{1,0:T(8,128)S(1)}, u32[]{:S(2)}, u32[]{:S(2)}) collective-permute-start(f32[8,128]{1,0:T(8,128)S(1)} %add.18), channel_id=1, source_target_pairs={{0,6},{1,25},{2,4},{3,27},{4,2},{5,29},{6,0},{7,31},{8,14},{9,17},... | collective-permute-start | bytes 12296 | tf_op jit(solution)/shard_map/ppermute | solution.py:64
  65.7 10.9 %collective-permute-start.14 = (bf16[16,128,128]{2,1,0:T(8,128)(2,1)S(1)}, bf16[16,128,128]{2,1,0:T(8,128)(2,1)S(1)}, u32[]{:S(2)}, u32[]{:S(2)}) collective-permute-start(bf16[16,128,128]{2,1,0:T(8,128)(2,1)S(1)} %get-tuple-element.32.refs_0_), channel_id=1, source_target_pairs={{0,1},{1,0},{2,3},{3,2},{4,5},{5,4},{6,7},{7,6},{8,9},{9,8},{10,11... | collective-permute-start | bytes 1572872 | tf_op jit(solution)/shard_map/ppermute | solution.py:64
  72.0 4.6 %collective-permute-start.20 = (bf16[16,128,128]{2,1,0:T(8,128)(2,1)S(1)}, bf16[16,128,128]{2,1,0:T(8,128)(2,1)S(1)}, u32[]{:S(2)}, u32[]{:S(2)}) collective-permute-start(bf16[16,128,128]{2,1,0:T(8,128)(2,1)S(1)} %collective-permute-done.19.refs_6_), channel_id=1, source_target_pairs={{0,1},{1,0},{2,3},{3,2},{4,5},{5,4},{6,7},{7,6},{8,9},{9,8},{10,11... | collective-permute-start | bytes 1572872 | tf_op jit(solution)/shard_map/ppermute | solution.py:64
  73.6 3.0 %collective-permute-start.16 = (bf16[16,128,128]{2,1,0:T(8,128)(2,1)S(1)}, bf16[16,128,128]{2,1,0:T(8,128)(2,1)S(1)}, u32[]{:S(2)}, u32[]{:S(2)}) collective-permute-start(bf16[16,128,128]{2,1,0:T(8,128)(2,1)S(1)} %collective-permute-done.15.refs_2_), channel_id=1, source_target_pairs={{0,1},{1,0},{2,3},{3,2},{4,5},{5,4},{6,7},{7,6},{8,9},{9,8},{10,11... | collective-permute-start | bytes 1572872 | tf_op jit(solution)/shard_map/ppermute | solution.py:64
  73.7 3.0 %collective-permute-start.18 = (bf16[16,128,128]{2,1,0:T(8,128)(2,1)S(1)}, bf16[16,128,128]{2,1,0:T(8,128)(2,1)S(1)}, u32[]{:S(2)}, u32[]{:S(2)}) collective-permute-start(bf16[16,128,128]{2,1,0:T(8,128)(2,1)S(1)} %collective-permute-done.17.refs_4_), channel_id=1, source_target_pairs={{0,1},{1,0},{2,3},{3,2},{4,5},{5,4},{6,7},{7,6},{8,9},{9,8},{10,11... | collective-permute-start | bytes 1572872 | tf_op jit(solution)/shard_map/ppermute | solution.py:64
  74.1 2.5 %collective-permute-start.13 = (f32[8,128]{1,0:T(8,128)S(1)}, f32[8,128]{1,0:T(8,128)S(1)}, u32[]{:S(2)}, u32[]{:S(2)}) collective-permute-start(f32[8,128]{1,0:T(8,128)S(1)} %add.19.mine_ref), channel_id=1, source_target_pairs={{0,1},{1,0},{2,3},{3,2},{4,5},{5,4},{6,7},{7,6},{8,9},{9,8},{10,11... | collective-permute-start | bytes 12296 | tf_op jit(solution)/shard_map/ppermute | solution.py:64

commit v3 on v2

--- a/solution.py
+++ b/solution.py
@@ -14,6 +14,8 @@
 F32 = jnp.float32
 HALF = 8
 BLOCK = 16
+ROWS = 16
+CHAIN = 3
 GROUPS = ((2, 1), (3, 0))
 RETURNED = (0, 1, 3, 2)
 MIB = 2**20
@@ -44,10 +46,6 @@
     return along(0, lambda p: (p + k) % 4)
 
 
-def swap_first(mask):
-    return along(0, lambda p: p ^ mask)
-
-
 def swap_second(mask):
     return along(1, lambda p: p ^ mask)
 
@@ -97,7 +95,10 @@
     )
 
 
-def outgoing_kernel(side, shifts, bitmap_hbm, g_hbm, r_hbm, out_ref, bitmap, g_ref, r_ref, sems):
+def outgoing_kernel(side, shifts, outs_count, bitmap_hbm, g_hbm, r_hbm, *refs):
+    given, outs, (bitmap, g_ref, r_ref, sems) = refs[:-5], refs[-5:-4], refs[-4:]
+    if outs_count > 1:
+        given, outs = refs[:1], refs[1:-4]
     firsts = [block_of(side, k) * BLOCK + h * HALF for k in shifts for h in range(2)]
     chosen = pltpu.make_async_copy(bitmap_hbm, bitmap, sems.at[0, 0])
     chosen.start()
@@ -114,17 +115,24 @@
         copies[2 * i + 1].wait()
         for t in range(HALF):
             place = i * HALF + t
-            value = (g_ref[place].astype(F32) + r_ref[place].astype(F32)).astype(BF16)
-            out_ref[place] = jnp.where(bitmap[0, first + t] > 0, value, jnp.zeros_like(value))
-
-
-def outgoing(side, shifts, bitmap, gradients, residual):
+            value = g_ref[place] + r_ref[place]
+            value = jnp.where(bitmap[0, first + t] > 0, value, jnp.zeros_like(value))
+            if given:
+                value = value + given[0][place]
+                outs[place // BLOCK][place % BLOCK] = value
+            else:
+                outs[0][place] = value
+
+
+def outgoing(side, shifts, bitmap, gradients, residual, *swapped):
     tiles = len(shifts) * BLOCK
-    return pl.pallas_call(
-        functools.partial(outgoing_kernel, side, shifts),
-        in_specs=[pl.BlockSpec(memory_space=pl.ANY)] * 3,
-        out_specs=pl.BlockSpec(memory_space=pltpu.VMEM),
-        out_shape=tiles_shape(tiles),
+    vmem = pl.BlockSpec(memory_space=pltpu.VMEM)
+    shapes = [tiles_shape(BLOCK)] * len(shifts) if swapped else [tiles_shape(tiles)]
+    return pl.pallas_call(
+        functools.partial(outgoing_kernel, side, shifts, len(shapes)),
+        in_specs=[pl.BlockSpec(memory_space=pl.ANY)] * 3 + [vmem] * len(swapped),
+        out_specs=[vmem] * len(shapes),
+        out_shape=shapes,
         scratch_shapes=[
             pltpu.SMEM((1, 128), jnp.int32),
             pltpu.VMEM((tiles, 128, 128), BF16),
@@ -133,13 +141,13 @@
         ],
         compiler_params=params(),
         cost_estimate=cost(3 * tiles),
-    )(bitmap, gradients, residual)
+    )(bitmap, gradients, residual, *swapped)
 
 
 def left_kernel(after_ref, bitmap_ref, g_ref, r_ref, out_ref, token_ref):
     first = pl.program_id(0) * BLOCK
     for t in range(BLOCK):
-        value = (g_ref[t].astype(F32) + r_ref[t].astype(F32)).astype(BF16)
+        value = g_ref[t] + r_ref[t]
         out_ref[t] = jnp.where(bitmap_ref[0, first + t] > 0, jnp.zeros_like(value), value)
     token_ref[...] = jnp.zeros_like(token_ref)
 
@@ -167,7 +175,7 @@
 
         @pl.when(pl.program_id(0) == k)
         def _():
-            out_ref[...] = (a_ref[...].astype(F32) + b_ref[...].astype(F32)).astype(BF16)
+            out_ref[...] = a_ref[...] + b_ref[...]
 
 
 def pair_sums(a, b):
@@ -203,8 +211,8 @@
 
 def halves_kernel(a0, a1, b0, b1, low_ref, high_ref):
     for t in range(HALF):
-        low_ref[t] = (a0[t].astype(F32) + a1[t].astype(F32)).astype(BF16)
-        high_ref[t] = (b0[t].astype(F32) + b1[t].astype(F32)).astype(BF16)
+        low_ref[t] = a0[t] + a1[t]
+        high_ref[t] = b0[t] + b1[t]
 
 
 def halves_sum(*halves):
@@ -218,7 +226,11 @@
     )(*halves)
 
 
-def last_kernel(lo_ref, hi_ref, a0, a1, b0, b1, out_ref, row_ref):
+def put_tile(ref, t, value):
+    ref[pl.ds(t * 128, 128), :] = value
+
+
+def last_kernel(lo_ref, hi_ref, a0, a1, b0, b1, plain_ref, full_ref, row_ref):
     shard = lax.axis_index("tensor")
     lo, hi = lo_ref[pl.ds(shard, 1), :], hi_ref[pl.ds(shard, 1), :]
     first = block_of(0, 0) * BLOCK
@@ -226,23 +238,79 @@
     for t in range(BLOCK):
         left, right = (a0, a1) if t < HALF else (b0, b1)
         total = left[t % HALF].astype(F32) + right[t % HALF].astype(F32)
-        out_ref[t] = total.astype(BF16)
+        put_tile(plain_ref, t, total.astype(BF16))
+        put_tile(full_ref, t, total.astype(BF16))
         square = jnp.sum(jnp.sum(total * total, axis=0, keepdims=True), axis=1, keepdims=True)
         row = row + jnp.where((lo <= first + t) & (first + t < hi), square, 0.0)
     row_ref[...] = jnp.broadcast_to(row, (8, 128))
 
 
+def flat_shape(tiles, rows):
+    return jax.ShapeDtypeStruct((tiles * 128 + rows, 128), BF16)
+
+
 def last_sum(lo, hi, *halves):
     return pl.pallas_call(
         last_kernel,
-        out_shape=[tiles_shape(BLOCK), jax.ShapeDtypeStruct((8, 128), F32)],
+        out_shape=[
+            flat_shape(BLOCK, 0),
+            flat_shape(BLOCK, ROWS),
+            jax.ShapeDtypeStruct((8, 128), F32),
+        ],
         compiler_params=params(),
         cost_estimate=cost(6 * HALF),
     )(lo, hi, *halves)
 
 
+def pack_kernel(full_ref, mine_ref, other_ref, out_ref, row_ref, sem):
+    row = 0.5 * (mine_ref[0:1, :] + other_ref[0:1, :])
+    rest, rows = jnp.broadcast_to(row, (ROWS, 128)), jnp.zeros((ROWS, 128), F32)
+    place = lax.broadcasted_iota(jnp.int32, (ROWS, 128), 0)
+    for i in range(3):
+        part = rest.astype(BF16).astype(F32)
+        rows = jnp.where(place == i, part, rows)
+        rest = jnp.where(jnp.abs(part) < jnp.inf, rest - part, 0.0)
+    row_ref[...] = rows.astype(BF16)
+    copy = pltpu.make_async_copy(row_ref, out_ref.at[pl.ds(BLOCK * 128, ROWS), :], sem)
+    copy.start()
+    copy.wait()
+
+
+def pack(full, mine, other):
+    vmem = pl.BlockSpec(memory_space=pltpu.VMEM)
+    anywhere = pl.BlockSpec(memory_space=pl.ANY)
+    return pl.pallas_call(
+        pack_kernel,
+        in_specs=[anywhere, vmem, vmem],
+        out_specs=[anywhere, vmem],
+        out_shape=[flat_shape(BLOCK, ROWS), flat_shape(0, ROWS)],
+        scratch_shapes=[pltpu.SemaphoreType.DMA],
+        input_output_aliases={0: 0},
+        compiler_params=params(),
+        cost_estimate=cost(1),
+    )(full, mine, other)
+
+
+def rows_kernel(r0, r2, r1, r3, out_ref):
+    rows = []
+    for ref in (r0, r2, r1, r3):
+        parts = ref[pl.ds(ref.shape[0] - ROWS, ROWS), :].astype(F32)
+        rows.append((parts[0:1, :] + parts[1:2, :]) + parts[2:3, :])
+    total = 2.0 * ((rows[0] + rows[1]) + (rows[2] + rows[3]))
+    out_ref[...] = jnp.broadcast_to(total, (8, 128))
+
+
+def sum_of_rows(*smalls):
+    return pl.pallas_call(
+        rows_kernel,
+        out_shape=jax.ShapeDtypeStruct((8, 128), F32),
+        compiler_params=params(),
+        cost_estimate=cost(1),
+    )(*smalls)
+
+
 def final_kernel(lo_ref, hi_ref, mine_ref, other_ref, m_ref, *refs):
-    blocks, (out_ref, factor_ref, ready_ref, sems) = refs[:8], refs[8:]
+    blocks, (out_ref, factor_ref, ready_ref, sems) = refs[:8], refs[9:]
     shard = lax.axis_index("tensor")
     lo, hi = lo_ref[pl.ds(shard, 1), :], hi_ref[pl.ds(shard, 1), :]
     count = jnp.sum((hi_ref[...] - lo_ref[...]).astype(F32), axis=0, keepdims=True)
@@ -253,18 +321,20 @@
     chosen = jnp.where((lo <= tile) & (tile < hi), clip, 0.0)
     factor_ref[...] = jnp.broadcast_to(jnp.sum(chosen, axis=1, keepdims=True), (128, 128))
 
+    def tiles_of(source, count, first, place):
+        def one_tile(t, carry):
+            value = source[pl.ds(pl.multiple_of(t * 128, 128), 128), :]
+            update = value.astype(F32) * factor_ref[pl.ds(first + t, 1), :]
+            new = MOMENTUM * m_ref[first + t].astype(F32) + update
+            ready_ref[place + t] = new.astype(BF16)
+            return carry
+
+        lax.fori_loop(0, count, one_tile, 0, unroll=4)
+
     copies = []
-    for k, block in enumerate(blocks):
+    for k in range(8):
         first = block_of(k % 2, -RETURNED[k // 2]) * BLOCK
-
-        def one_tile(t, carry):
-            factor = factor_ref[pl.ds(first + t, 1), :]
-            update = block[t].astype(F32) * factor
-            new = MOMENTUM * m_ref[first + t].astype(F32) + update
-            ready_ref[k * BLOCK + t] = new.astype(BF16)
-            return carry
-
-        lax.fori_loop(0, BLOCK, one_tile, 0, unroll=4)
+        tiles_of(blocks[k], BLOCK, first, k * BLOCK)
         copies.append(
             pltpu.make_async_copy(
                 ready_ref.at[pl.ds(k * BLOCK, BLOCK)],
@@ -303,33 +373,34 @@
     residual = pltpu.with_memory_space_constraint(residual, pltpu.HBM)
     bitmap = pltpu.with_memory_space_constraint(bitmap, pltpu.HBM)
     arrays = (bitmap, gradients, residual)
-    swapped = [send(outgoing(1, shifts, *arrays), swap_core()) for shifts in GROUPS]
-    kept = [outgoing(0, shifts, *arrays) for shifts in GROUPS]
-    first = pair_sums(kept[0], swapped[0])
-    by_two = send(first[0], shift_first(2))
-    by_one = send(first[1], shift_first(1))
-    second = pair_sums(kept[1], swapped[1])
-    by_three = send(second[0], shift_first(3))
-    left, token = left_over(second[0], *arrays)
-
-    low, high = block_total(token, second[1], by_one, by_two, by_three)
+    swapped = [send(outgoing(1, shifts, *arrays)[0], swap_core()) for shifts in GROUPS]
+    two, one = pair_sums(outgoing(0, GROUPS[0], *arrays)[0], swapped[0])
+    by_two, by_one = send(two, shift_first(2)), send(one, shift_first(1))
+    three, own = outgoing(0, GROUPS[1], *arrays, swapped[1])
+    by_three = send(three, shift_first(3))
+    left, token = left_over(three, *arrays)
+
+    low, high = block_total(token, own, by_one, by_two, by_three)
     low, high = halves_sum(low, send(low, swap_second(1)), high, send(high, swap_second(3)))
-    full, row = last_sum(lo, hi, low, send(low, swap_second(3)), high, send(high, swap_second(1)))
-
-    returned = {2: send(full, shift_first(2))}
+    plain, full, row = last_sum(
+        lo, hi, low, send(low, swap_second(3)), high, send(high, swap_second(1))
+    )
+
+    by_two = send(plain, shift_first(2))
     row = row + send(row, swap_tensor(1), "tensor")
-    full = after(full, row)
-    returned[1] = send(full, shift_first(1))
-    row = row + send(row, swap_tensor(3), "tensor")
-    full = after(full, row)
-    returned[3] = send(full, shift_first(3))
-    for mask in (1, 3):
-        row = row + send(row, swap_first(mask))
+    full, row = pack(full, row, send(row, swap_tensor(3), "tensor"))
+    by_one, by_three = send(full, shift_first(1)), send(full, shift_first(3))
+    row_two = send(row, shift_first(2))
+    row = sum_of_rows(full, row_two, by_one, by_three)
     other = send(row, swap_core())
-
     blocks = [full, send(full, swap_core())]
-    for k in RETURNED[1:]:
-        blocks += [returned[k], send(after(returned[k], row), swap_core())]
+    for block in (after(by_one, row_two), by_three):
+        blocks += [block, send(block, swap_core())]
+    token = by_two[:ROWS]
+    for _ in range(CHAIN):
+        token = send(token, swap_core())
+    moved, token = lax.optimization_barrier((by_two, token))
+    blocks += [by_two, send(moved, swap_core()), token]
     return (left[None], finish(lo, hi, row, other, momentum, blocks))
 
 

time: 79.7 us -> 74.4 us (0.934)
  waiting for transfers between devices: 30.4 us -> 26.2 us
  starting transfers between devices: 29.4 us -> 28.5 us
    ppermute x21 -> x23, waiting for transfers between devices: 30.4 us -> 26.2 us  [send(): return lax.ppermute(array, axis, pairs)]
    ppermute x21 -> x23, starting transfers between devices: 29.4 us -> 28.5 us  [send(): return lax.ppermute(array, axis, pairs)]
    pallas_call x5 -> x7, Pallas kernels: 7.04 us -> 7.09 us  [the longest x4 6.77 us: outgoing(): pl.pallas_call(functools.partial(outgoing_kernel, side, shifts, len(shape...]
  transfers between devices with their start and end apart: 21 -> 23, of which waited for: 10 -> 13; matrix products, arithmetic and copies ran while one was open for 0% -> 0% of each run, Pallas kernels for 17% -> 18%
where the time goes in v3:
time: 74.4 us; the launch traced here: 74 us
  starting transfers between devices  28.5 us (38%)
  waiting for transfers between devices  26.2 us (35%)
  Pallas kernels  18.5 us (25%)
  between operations  0.76 us (1%)
    ppermute x23, starting transfers between devices, send(): return lax.ppermute(array, axis, pairs)  28.5 us
    ppermute x23, waiting for transfers between devices, send(): return lax.ppermute(array, axis, pairs)  26.2 us
    pallas_call x1, Pallas kernels, left_over(): pl.pallas_call(left_kernel, grid=(8,), in_specs=[pl.BlockSpec(memory_spac...  8.05 us
    pallas_call x4, Pallas kernels, outgoing(): pl.pallas_call(functools.partial(outgoing_kernel, side, shifts, len(shape...  6.77 us
    pallas_call x1, Pallas kernels, finish(): pl.pallas_call(final_kernel, in_specs=[whole] * (5 + len(blocks)), out_sp...  2.7 us
  transfers between devices with their start and end apart: 23, of which 13 were waited for; matrix products, arithmetic and copies ran while one was open for 0% of the time, Pallas kernels for 18%

profile of v3, /device:TPU:1, one launch (start us, length us, event | category | flops | bytes accessed | tf_op | source)
XLA Modules:
  0.0 74.0 jit_solution(8676532975644771816)
XLA Ops:
  0.6 1.7 %shard_map.68 = bf16[32,128,128]{2,1,0:T(8,128)(2,1)S(1)} custom-call(s32[1,128]{1,0:T(1,128)} %bitmap_hbm.7, bf16[128,128,128]{2,1,0:T(8,128)(2,1)} %bitcast.3, bf16[128,128,128]{2,1,0:T(8,128)(2,1)} %bitcast.8), custom_call_target="tpu_custom_call" | custom-call | flops 1572864 | bytes 3145728 | tf_op jit(solution)/shard_map/pallas_call | solution.py:131
  2.3 1.5 %collective-permute-start = (bf16[32,128,128]{2,1,0:T(8,128)(2,1)S(1)}, bf16[32,128,128]{2,1,0:T(8,128)(2,1)S(1)}, u32[]{:S(2)}, u32[]{:S(2)}) collective-permute-start(bf16[32,128,128]{2,1,0:T(8,128)(2,1)S(1)} %shard_map.68), channel_id=1, source_target_pairs={{0,1},{1,0},{2,3},{3,2},{4,5},{5,4},{6,7},{7,6},{8,9},{9,8},{10,11... | collective-permute-start | bytes 3145736 | tf_op jit(solution)/shard_map/ppermute | solution.py:62
  3.8 1.7 %shard_map.72 = bf16[32,128,128]{2,1,0:T(8,128)(2,1)S(1)} custom-call(s32[1,128]{1,0:T(1,128)} %bitmap_hbm.7, bf16[128,128,128]{2,1,0:T(8,128)(2,1)} %bitcast.4, bf16[128,128,128]{2,1,0:T(8,128)(2,1)} %bitcast.9), custom_call_target="tpu_custom_call" | custom-call | flops 1572864 | bytes 3145728 | tf_op jit(solution)/shard_map/pallas_call | solution.py:131
  5.6 1.7 %shard_map.71.a_ref = bf16[32,128,128]{2,1,0:T(8,128)(2,1)S(1)} custom-call(s32[1,128]{1,0:T(1,128)} %bitmap_hbm.7, bf16[128,128,128]{2,1,0:T(8,128)(2,1)} %bitcast.5, bf16[128,128,128]{2,1,0:T(8,128)(2,1)} %bitcast.10), custom_call_target="tpu_custom_call" | custom-call | flops 1572864 | bytes 3145728 | tf_op jit(solution)/shard_map/pallas_call | solution.py:131
  7.3 1.7 %shard_map.69 = (bf16[16,128,128]{2,1,0:T(8,128)(2,1)S(1)}, bf16[16,128,128]{2,1,0:T(8,128)(2,1)S(1)}) custom-call(s32[1,128]{1,0:T(1,128)} %bitmap_hbm.7, bf16[128,128,128]{2,1,0:T(8,128)(2,1)} %bitcast.6, bf16[128,128,128]{2,1,0:T(8,128)(2,1)} %bitcast.11, bf16[32,128,128]{2,1,0:T(8,128)(2,1)S(1)} %collective-permute-done.refs_0_), custom_call_target="tpu_custom_call" | custom-call | flops 1572864 | bytes 3145728 | tf_op jit(solution)/shard_map/pallas_call | solution.py:131
  9.1 3.9 %collective-permute-start.4 = (bf16[16,128,128]{2,1,0:T(8,128)(2,1)S(1)}, bf16[16,128,128]{2,1,0:T(8,128)(2,1)S(1)}, u32[]{:S(2)}, u32[]{:S(2)}) collective-permute-start(bf16[16,128,128]{2,1,0:T(8,128)(2,1)S(1)} %get-tuple-element.20.after_ref), channel_id=1, source_target_pairs={{0,6},{1,25},{2,0},{3,27},{4,2},{5,29},{6,4},{7,31},{8,14},{9,1},{... | collective-permute-start | bytes 1572872 | tf_op jit(solution)/shard_map/ppermute | solution.py:62
  13.4 1.3 %collective-permute-start.3 = (bf16[16,128,128]{2,1,0:T(8,128)(2,1)S(1)}, bf16[16,128,128]{2,1,0:T(8,128)(2,1)S(1)}, u32[]{:S(2)}, u32[]{:S(2)}) collective-permute-start(bf16[16,128,128]{2,1,0:T(8,128)(2,1)S(1)} %get-tuple-element.25), channel_id=1, source_target_pairs={{0,4},{1,17},{2,6},{3,19},{4,0},{5,21},{6,2},{7,23},{8,12},{9,25},... | collective-permute-start | bytes 1572872 | tf_op jit(solution)/shard_map/ppermute | solution.py:62
  14.6 8.1 %shard_map.70 = (bf16[128,128,128]{2,1,0:T(8,128)(2,1)}, f32[8,128]{1,0:T(8,128)S(1)}) custom-call(bf16[16,128,128]{2,1,0:T(8,128)(2,1)S(1)} %get-tuple-element.20.after_ref, s32[1,128]{1,0:T(1,128)} %bitmap_hbm.7, bf16[128,128,128]{2,1,0:T(8,128)(2,1)} %bitcast.7, bf16[128,128,128]{2,1,0:T(8,128)(2,1)} %bitcast.12), custom_call_target="tpu_custom_call" | custom-call | flops 6291456 | bytes 12582912 | tf_op jit(solution)/shard_map/pallas_call | solution.py:157
  22.7 2.0 %collective-permute-done.4.r3 = bf16[16,128,128]{2,1,0:T(8,128)(2,1)S(1)} collective-permute-done((bf16[16,128,128]{2,1,0:T(8,128)(2,1)S(1)}, bf16[16,128,128]{2,1,0:T(8,128)(2,1)S(1)}, u32[]{:S(2)}, u32[]{:S(2)}) %collective-permute-start.4) | collective-permute-done | bytes 524320 | tf_op jit(solution)/shard_map/ppermute | solution.py:62
  24.7 3.7 %collective-permute-done.2.r1 = bf16[16,128,128]{2,1,0:T(8,128)(2,1)S(1)} collective-permute-done((bf16[16,128,128]{2,1,0:T(8,128)(2,1)S(1)}, bf16[16,128,128]{2,1,0:T(8,128)(2,1)S(1)}, u32[]{:S(2)}, u32[]{:S(2)}) %collective-permute-start.2) | collective-permute-done | bytes 524320 | tf_op jit(solution)/shard_map/ppermute | solution.py:62
  29.8 1.8 %collective-permute-start.6 = (bf16[8,128,128]{2,1,0:T(8,128)(2,1)S(1)}, bf16[8,128,128]{2,1,0:T(8,128)(2,1)S(1)}, u32[]{:S(2)}, u32[]{:S(2)}) collective-permute-start(bf16[8,128,128]{2,1,0:T(8,128)(2,1)S(1)} %get-tuple-element.27.b0), channel_id=1, source_target_pairs={{0,24},{1,7},{2,26},{3,5},{4,28},{5,3},{6,30},{7,1},{8,16},{9,15},... | collective-permute-start | bytes 786440 | tf_op jit(solution)/shard_map/ppermute | solution.py:62
  31.6 2.7 %collective-permute-done.5.a1 = bf16[8,128,128]{2,1,0:T(8,128)(2,1)S(1)} collective-permute-done((bf16[8,128,128]{2,1,0:T(8,128)(2,1)S(1)}, bf16[8,128,128]{2,1,0:T(8,128)(2,1)S(1)}, u32[]{:S(2)}, u32[]{:S(2)}) %collective-permute-start.5) | collective-permute-done | bytes 262176 | tf_op jit(solution)/shard_map/ppermute | solution.py:62
  34.3 2.2 %collective-permute-done.6.b1 = bf16[8,128,128]{2,1,0:T(8,128)(2,1)S(1)} collective-permute-done((bf16[8,128,128]{2,1,0:T(8,128)(2,1)S(1)}, bf16[8,128,128]{2,1,0:T(8,128)(2,1)S(1)}, u32[]{:S(2)}, u32[]{:S(2)}) %collective-permute-start.6) | collective-permute-done | bytes 262176 | tf_op jit(solution)/shard_map/ppermute | solution.py:62
  36.6 1.6 %collective-permute-start.7 = (bf16[8,128,128]{2,1,0:T(8,128)(2,1)S(1)}, bf16[8,128,128]{2,1,0:T(8,128)(2,1)S(1)}, u32[]{:S(2)}, u32[]{:S(2)}) collective-permute-start(bf16[8,128,128]{2,1,0:T(8,128)(2,1)S(1)} %get-tuple-element.28.a0), channel_id=1, source_target_pairs={{0,24},{1,7},{2,26},{3,5},{4,28},{5,3},{6,30},{7,1},{8,16},{9,15},... | collective-permute-start | bytes 786440 | tf_op jit(solution)/shard_map/ppermute | solution.py:62
  38.3 5.1 %collective-permute-done.7.a1 = bf16[8,128,128]{2,1,0:T(8,128)(2,1)S(1)} collective-permute-done((bf16[8,128,128]{2,1,0:T(8,128)(2,1)S(1)}, bf16[8,128,128]{2,1,0:T(8,128)(2,1)S(1)}, u32[]{:S(2)}, u32[]{:S(2)}) %collective-permute-start.7) | collective-permute-done | bytes 262176 | tf_op jit(solution)/shard_map/ppermute | solution.py:62
  44.0 1.4 %collective-permute-start.9 = (f32[8,128]{1,0:T(8,128)S(1)}, f32[8,128]{1,0:T(8,128)S(1)}, u32[]{:S(2)}, u32[]{:S(2)}) collective-permute-start(f32[8,128]{1,0:T(8,128)S(1)} %get-tuple-element.31), channel_id=1, source_target_pairs={{0,32},{32,0},{64,96},{96,64},{1,33},{33,1},{65,97},{97,65},{2,34}... | collective-permute-start | bytes 12296 | tf_op jit(solution)/shard_map/ppermute | solution.py:62
  46.8 2.7 %collective-permute-start.10 = (f32[8,128]{1,0:T(8,128)S(1)}, f32[8,128]{1,0:T(8,128)S(1)}, u32[]{:S(2)}, u32[]{:S(2)}) collective-permute-start(f32[8,128]{1,0:T(8,128)S(1)} %add.7.mine_ref), channel_id=1, source_target_pairs={{0,96},{32,64},{64,32},{96,0},{1,97},{33,65},{65,33},{97,1},{2,98}... | collective-permute-start | bytes 12296 | tf_op jit(solution)/shard_map/ppermute | solution.py:62
  50.7 2.7 %collective-permute-start.13 = (bf16[2064,128]{1,0:T(8,128)(2,1)S(1)}, bf16[2064,128]{1,0:T(8,128)(2,1)S(1)}, u32[]{:S(2)}, u32[]{:S(2)}) collective-permute-start(bf16[2064,128]{1,0:T(8,128)(2,1)S(1)} %get-tuple-element.32.r0.refs_0_), channel_id=1, source_target_pairs={{0,6},{1,25},{2,0},{3,27},{4,2},{5,29},{6,4},{7,31},{8,14},{9,1},{... | collective-permute-start | bytes 1585160 | tf_op jit(solution)/shard_map/ppermute | solution.py:62
  53.4 1.6 %collective-permute-done.18.refs_6_ = bf16[2048,128]{1,0:T(8,128)(2,1)S(1)} collective-permute-done((bf16[2048,128]{1,0:T(8,128)(2,1)S(1)}, bf16[2048,128]{1,0:T(8,128)(2,1)S(1)}, u32[]{:S(2)}, u32[]{:S(2)}) %collective-permute-start.18) | collective-permute-done | bytes 524320 | tf_op jit(solution)/shard_map/ppermute | solution.py:62
  55.0 6.8 %collective-permute-start.19 = (bf16[16,128]{1,0:T(8,128)(2,1)S(1)}, bf16[16,128]{1,0:T(8,128)(2,1)S(1)}, u32[]{:S(2)}, u32[]{:S(2)}) collective-permute-start(bf16[16,128]{1,0:T(8,128)(2,1)S(1)} %slice.8), channel_id=1, source_target_pairs={{0,1},{1,0},{2,3},{3,2},{4,5},{5,4},{6,7},{7,6},{8,9},{9,8},{10,11... | collective-permute-start | bytes 12296 | tf_op jit(solution)/shard_map/ppermute | solution.py:62
  64.1 2.8 %collective-permute-done.11.r2 = bf16[16,128]{1,0:T(8,128)(2,1)S(1)} collective-permute-done((bf16[16,128]{1,0:T(8,128)(2,1)S(1)}, bf16[16,128]{1,0:T(8,128)(2,1)S(1)}, u32[]{:S(2)}, u32[]{:S(2)}) %collective-permute-start.11) | collective-permute-done | bytes 4128 | tf_op jit(solution)/shard_map/ppermute | solution.py:62
  66.9 1.3 %collective-permute-start.17 = (bf16[2064,128]{1,0:T(8,128)(2,1)S(1)}, bf16[2064,128]{1,0:T(8,128)(2,1)S(1)}, u32[]{:S(2)}, u32[]{:S(2)}) collective-permute-start(bf16[2064,128]{1,0:T(8,128)(2,1)S(1)} %collective-permute-done.13.r3.refs_4_), channel_id=1, source_target_pairs={{0,1},{1,0},{2,3},{3,2},{4,5},{5,4},{6,7},{7,6},{8,9},{9,8},{10,11... | collective-permute-start | bytes 1585160 | tf_op jit(solution)/shard_map/ppermute | solution.py:62
  68.9 2.4 %collective-permute-done.14.other_ref = f32[8,128]{1,0:T(8,128)S(1)} collective-permute-done((f32[8,128]{1,0:T(8,128)S(1)}, f32[8,128]{1,0:T(8,128)S(1)}, u32[]{:S(2)}, u32[]{:S(2)}) %collective-permute-start.14) | collective-permute-done | bytes 4128 | tf_op jit(solution)/shard_map/ppermute | solution.py:62
  71.3 2.7 %shard_map.79 = bf16[128,128,128]{2,1,0:T(8,128)(2,1)} custom-call(s32[4,128]{1,0:T(4,128)S(1)} %pad.8.lo_ref, s32[4,128]{1,0:T(4,128)S(1)} %pad.9.hi_ref, f32[8,128]{1,0:T(8,128)S(1)} %shard_map.78.mine_ref, f32[8,128]{1,0:T(8,128)S(1)} %collective-permute-done.14.other_ref, bf16[128,128,128]{2,1,0:T(8,128)(2,1)S(1)} %copy-done, ...), custom_call_target="tpu_custom_call" | custom-call | flops 6291456 | bytes 12582912 | tf_op jit(solution)/shard_map/pallas_call | solution.py:352
  (43 shorter events, 8.2 us)
Async XLA Ops:
  2.3 5.0 %collective-permute-start = (bf16[32,128,128]{2,1,0:T(8,128)(2,1)S(1)}, bf16[32,128,128]{2,1,0:T(8,128)(2,1)S(1)}, u32[]{:S(2)}, u32[]{:S(2)}) collective-permute-start(bf16[32,128,128]{2,1,0:T(8,128)(2,1)S(1)} %shard_map.68), channel_id=1, source_target_pairs={{0,1},{1,0},{2,3},{3,2},{4,5},{5,4},{6,7},{7,6},{8,9},{9,8},{10,11... | collective-permute-start | bytes 3145736 | tf_op jit(solution)/shard_map/ppermute | solution.py:62
  5.5 7.5 %collective-permute-start.1 = (bf16[32,128,128]{2,1,0:T(8,128)(2,1)S(1)}, bf16[32,128,128]{2,1,0:T(8,128)(2,1)S(1)}, u32[]{:S(2)}, u32[]{:S(2)}) collective-permute-start(bf16[32,128,128]{2,1,0:T(8,128)(2,1)S(1)} %shard_map.72), channel_id=1, source_target_pairs={{0,1},{1,0},{2,3},{3,2},{4,5},{5,4},{6,7},{7,6},{8,9},{9,8},{10,11... | collective-permute-start | bytes 3145736 | tf_op jit(solution)/shard_map/ppermute | solution.py:62
  9.1 15.7 %collective-permute-start.4 = (bf16[16,128,128]{2,1,0:T(8,128)(2,1)S(1)}, bf16[16,128,128]{2,1,0:T(8,128)(2,1)S(1)}, u32[]{:S(2)}, u32[]{:S(2)}) collective-permute-start(bf16[16,128,128]{2,1,0:T(8,128)(2,1)S(1)} %get-tuple-element.20.after_ref), channel_id=1, source_target_pairs={{0,6},{1,25},{2,0},{3,27},{4,2},{5,29},{6,4},{7,31},{8,14},{9,1},{... | collective-permute-start | bytes 1572872 | tf_op jit(solution)/shard_map/ppermute | solution.py:62
  13.3 15.1 %collective-permute-start.2 = (bf16[16,128,128]{2,1,0:T(8,128)(2,1)S(1)}, bf16[16,128,128]{2,1,0:T(8,128)(2,1)S(1)}, u32[]{:S(2)}, u32[]{:S(2)}) collective-permute-start(bf16[16,128,128]{2,1,0:T(8,128)(2,1)S(1)} %get-tuple-element.24), channel_id=1, source_target_pairs={{0,2},{1,9},{2,4},{3,11},{4,6},{5,13},{6,0},{7,15},{8,10},{9,17},{... | collective-permute-start | bytes 1572872 | tf_op jit(solution)/shard_map/ppermute | solution.py:62
  13.4 15.0 %collective-permute-start.3 = (bf16[16,128,128]{2,1,0:T(8,128)(2,1)S(1)}, bf16[16,128,128]{2,1,0:T(8,128)(2,1)S(1)}, u32[]{:S(2)}, u32[]{:S(2)}) collective-permute-start(bf16[16,128,128]{2,1,0:T(8,128)(2,1)S(1)} %get-tuple-element.25), channel_id=1, source_target_pairs={{0,4},{1,17},{2,6},{3,19},{4,0},{5,21},{6,2},{7,23},{8,12},{9,25},... | collective-permute-start | bytes 1572872 | tf_op jit(solution)/shard_map/ppermute | solution.py:62
  22.7 48.6 %copy-start = (bf16[128,128,128]{2,1,0:T(8,128)(2,1)S(1)}, bf16[128,128,128]{2,1,0:T(8,128)(2,1)}, u32[]{:S(2)}) copy-start(bf16[128,128,128]{2,1,0:T(8,128)(2,1)} %m_ref.1) | copy-start | bytes 12582916
  28.7 5.6 %collective-permute-start.5 = (bf16[8,128,128]{2,1,0:T(8,128)(2,1)S(1)}, bf16[8,128,128]{2,1,0:T(8,128)(2,1)S(1)}, u32[]{:S(2)}, u32[]{:S(2)}) collective-permute-start(bf16[8,128,128]{2,1,0:T(8,128)(2,1)S(1)} %get-tuple-element.26.a0), channel_id=1, source_target_pairs={{0,8},{1,3},{2,10},{3,1},{4,12},{5,7},{6,14},{7,5},{8,0},{9,11},{1... | collective-permute-start | bytes 786440 | tf_op jit(solution)/shard_map/ppermute | solution.py:62
  29.8 6.7 %collective-permute-start.6 = (bf16[8,128,128]{2,1,0:T(8,128)(2,1)S(1)}, bf16[8,128,128]{2,1,0:T(8,128)(2,1)S(1)}, u32[]{:S(2)}, u32[]{:S(2)}) collective-permute-start(bf16[8,128,128]{2,1,0:T(8,128)(2,1)S(1)} %get-tuple-element.27.b0), channel_id=1, source_target_pairs={{0,24},{1,7},{2,26},{3,5},{4,28},{5,3},{6,30},{7,1},{8,16},{9,15},... | collective-permute-start | bytes 786440 | tf_op jit(solution)/shard_map/ppermute | solution.py:62
  36.6 6.8 %collective-permute-start.7 = (bf16[8,128,128]{2,1,0:T(8,128)(2,1)S(1)}, bf16[8,128,128]{2,1,0:T(8,128)(2,1)S(1)}, u32[]{:S(2)}, u32[]{:S(2)}) collective-permute-start(bf16[8,128,128]{2,1,0:T(8,128)(2,1)S(1)} %get-tuple-element.28.a0), channel_id=1, source_target_pairs={{0,24},{1,7},{2,26},{3,5},{4,28},{5,3},{6,30},{7,1},{8,16},{9,15},... | collective-permute-start | bytes 786440 | tf_op jit(solution)/shard_map/ppermute | solution.py:62
  38.2 5.5 %collective-permute-start.8 = (bf16[8,128,128]{2,1,0:T(8,128)(2,1)S(1)}, bf16[8,128,128]{2,1,0:T(8,128)(2,1)S(1)}, u32[]{:S(2)}, u32[]{:S(2)}) collective-permute-start(bf16[8,128,128]{2,1,0:T(8,128)(2,1)S(1)} %get-tuple-element.29.b0), channel_id=1, source_target_pairs={{0,8},{1,3},{2,10},{3,1},{4,12},{5,7},{6,14},{7,5},{8,0},{9,11},{1... | collective-permute-start | bytes 786440 | tf_op jit(solution)/shard_map/ppermute | solution.py:62
  44.0 2.8 %collective-permute-start.9 = (f32[8,128]{1,0:T(8,128)S(1)}, f32[8,128]{1,0:T(8,128)S(1)}, u32[]{:S(2)}, u32[]{:S(2)}) collective-permute-start(f32[8,128]{1,0:T(8,128)S(1)} %get-tuple-element.31), channel_id=1, source_target_pairs={{0,32},{32,0},{64,96},{96,64},{1,33},{33,1},{65,97},{97,65},{2,34}... | collective-permute-start | bytes 12296 | tf_op jit(solution)/shard_map/ppermute | solution.py:62
  45.4 9.6 %collective-permute-start.18 = (bf16[2048,128]{1,0:T(8,128)(2,1)S(1)}, bf16[2048,128]{1,0:T(8,128)(2,1)S(1)}, u32[]{:S(2)}, u32[]{:S(2)}) collective-permute-start(bf16[2048,128]{1,0:T(8,128)(2,1)S(1)} %get-tuple-element.35), channel_id=1, source_target_pairs={{0,4},{1,17},{2,6},{3,19},{4,0},{5,21},{6,2},{7,23},{8,12},{9,25},... | collective-permute-start | bytes 1572872 | tf_op jit(solution)/shard_map/ppermute | solution.py:62
  46.8 3.7 %collective-permute-start.10 = (f32[8,128]{1,0:T(8,128)S(1)}, f32[8,128]{1,0:T(8,128)S(1)}, u32[]{:S(2)}, u32[]{:S(2)}) collective-permute-start(f32[8,128]{1,0:T(8,128)S(1)} %add.7.mine_ref), channel_id=1, source_target_pairs={{0,96},{32,64},{64,32},{96,0},{1,97},{33,65},{65,33},{97,1},{2,98}... | collective-permute-start | bytes 12296 | tf_op jit(solution)/shard_map/ppermute | solution.py:62
  50.6 16.3 %collective-permute-start.12 = (bf16[2064,128]{1,0:T(8,128)(2,1)S(1)}, bf16[2064,128]{1,0:T(8,128)(2,1)S(1)}, u32[]{:S(2)}, u32[]{:S(2)}) collective-permute-start(bf16[2064,128]{1,0:T(8,128)(2,1)S(1)} %get-tuple-element.32.r0.refs_0_), channel_id=1, source_target_pairs={{0,2},{1,9},{2,4},{3,11},{4,6},{5,13},{6,0},{7,15},{8,10},{9,17},{... | collective-permute-start | bytes 1585160 | tf_op jit(solution)/shard_map/ppermute | solution.py:62
  50.7 16.2 %collective-permute-start.13 = (bf16[2064,128]{1,0:T(8,128)(2,1)S(1)}, bf16[2064,128]{1,0:T(8,128)(2,1)S(1)}, u32[]{:S(2)}, u32[]{:S(2)}) collective-permute-start(bf16[2064,128]{1,0:T(8,128)(2,1)S(1)} %get-tuple-element.32.r0.refs_0_), channel_id=1, source_target_pairs={{0,6},{1,25},{2,0},{3,27},{4,2},{5,29},{6,4},{7,31},{8,14},{9,1},{... | collective-permute-start | bytes 1585160 | tf_op jit(solution)/shard_map/ppermute | solution.py:62
  55.0 7.6 %collective-permute-start.19 = (bf16[16,128]{1,0:T(8,128)(2,1)S(1)}, bf16[16,128]{1,0:T(8,128)(2,1)S(1)}, u32[]{:S(2)}, u32[]{:S(2)}) collective-permute-start(bf16[16,128]{1,0:T(8,128)(2,1)S(1)} %slice.8), channel_id=1, source_target_pairs={{0,1},{1,0},{2,3},{3,2},{4,5},{5,4},{6,7},{7,6},{8,9},{9,8},{10,11... | collective-permute-start | bytes 12296 | tf_op jit(solution)/shard_map/ppermute | solution.py:62
  62.6 1.2 %collective-permute-start.20 = (bf16[16,128]{1,0:T(8,128)(2,1)S(1)}, bf16[16,128]{1,0:T(8,128)(2,1)S(1)}, u32[]{:S(2)}, u32[]{:S(2)}) collective-permute-start(bf16[16,128]{1,0:T(8,128)(2,1)S(1)} %collective-permute-done.19), channel_id=1, source_target_pairs={{0,1},{1,0},{2,3},{3,2},{4,5},{5,4},{6,7},{7,6},{8,9},{9,8},{10,11... | collective-permute-start | bytes 12296 | tf_op jit(solution)/shard_map/ppermute | solution.py:62
  63.0 4.0 %collective-permute-start.11 = (bf16[16,128]{1,0:T(8,128)(2,1)S(1)}, bf16[16,128]{1,0:T(8,128)(2,1)S(1)}, u32[]{:S(2)}, u32[]{:S(2)}) collective-permute-start(bf16[16,128]{1,0:T(8,128)(2,1)S(1)} %get-tuple-element.33), channel_id=1, source_target_pairs={{0,4},{1,17},{2,6},{3,19},{4,0},{5,21},{6,2},{7,23},{8,12},{9,25},... | collective-permute-start | bytes 12296 | tf_op jit(solution)/shard_map/ppermute | solution.py:62
  63.0 6.0 %collective-permute-start.15 = (bf16[2064,128]{1,0:T(8,128)(2,1)S(1)}, bf16[2064,128]{1,0:T(8,128)(2,1)S(1)}, u32[]{:S(2)}, u32[]{:S(2)}) collective-permute-start(bf16[2064,128]{1,0:T(8,128)(2,1)S(1)} %get-tuple-element.32.r0.refs_0_), channel_id=1, source_target_pairs={{0,1},{1,0},{2,3},{3,2},{4,5},{5,4},{6,7},{7,6},{8,9},{9,8},{10,11... | collective-permute-start | bytes 1585160 | tf_op jit(solution)/shard_map/ppermute | solution.py:62
  63.8 4.6 %collective-permute-start.21 = (bf16[16,128]{1,0:T(8,128)(2,1)S(1)}, bf16[16,128]{1,0:T(8,128)(2,1)S(1)}, u32[]{:S(2)}, u32[]{:S(2)}) collective-permute-start(bf16[16,128]{1,0:T(8,128)(2,1)S(1)} %collective-permute-done.20), channel_id=1, source_target_pairs={{0,1},{1,0},{2,3},{3,2},{4,5},{5,4},{6,7},{7,6},{8,9},{9,8},{10,11... | collective-permute-start | bytes 12296 | tf_op jit(solution)/shard_map/ppermute | solution.py:62
  66.9 4.4 %collective-permute-start.17 = (bf16[2064,128]{1,0:T(8,128)(2,1)S(1)}, bf16[2064,128]{1,0:T(8,128)(2,1)S(1)}, u32[]{:S(2)}, u32[]{:S(2)}) collective-permute-start(bf16[2064,128]{1,0:T(8,128)(2,1)S(1)} %collective-permute-done.13.r3.refs_4_), channel_id=1, source_target_pairs={{0,1},{1,0},{2,3},{3,2},{4,5},{5,4},{6,7},{7,6},{8,9},{9,8},{10,11... | collective-permute-start | bytes 1585160 | tf_op jit(solution)/shard_map/ppermute | solution.py:62
  68.2 3.1 %collective-permute-start.16 = (bf16[2064,128]{1,0:T(8,128)(2,1)S(1)}, bf16[2064,128]{1,0:T(8,128)(2,1)S(1)}, u32[]{:S(2)}, u32[]{:S(2)}) collective-permute-start(bf16[2064,128]{1,0:T(8,128)(2,1)S(1)} %collective-permute-done.12.r1.refs_2_), channel_id=1, source_target_pairs={{0,1},{1,0},{2,3},{3,2},{4,5},{5,4},{6,7},{7,6},{8,9},{9,8},{10,11... | collective-permute-start | bytes 1585160 | tf_op jit(solution)/shard_map/ppermute | solution.py:62
  68.3 3.0 %collective-permute-start.22 = (bf16[2048,128]{1,0:T(8,128)(2,1)S(1)}, bf16[2048,128]{1,0:T(8,128)(2,1)S(1)}, u32[]{:S(2)}, u32[]{:S(2)}) collective-permute-start(bf16[2048,128]{1,0:T(8,128)(2,1)S(1)} %collective-permute-done.18.refs_6_), channel_id=1, source_target_pairs={{0,1},{1,0},{2,3},{3,2},{4,5},{5,4},{6,7},{7,6},{8,9},{9,8},{10,11... | collective-permute-start | bytes 1572872 | tf_op jit(solution)/shard_map/ppermute | solution.py:62
  68.8 2.5 %collective-permute-start.14 = (f32[8,128]{1,0:T(8,128)S(1)}, f32[8,128]{1,0:T(8,128)S(1)}, u32[]{:S(2)}, u32[]{:S(2)}) collective-permute-start(f32[8,128]{1,0:T(8,128)S(1)} %shard_map.78.mine_ref), channel_id=1, source_target_pairs={{0,1},{1,0},{2,3},{3,2},{4,5},{5,4},{6,7},{7,6},{8,9},{9,8},{10,11... | collective-permute-start | bytes 12296 | tf_op jit(solution)/shard_map/ppermute | solution.py:62
  (1 other events, 24.9 us)

commit v4 on v3

--- a/solution.py
+++ b/solution.py
@@ -95,10 +95,9 @@
     )
 
 
-def outgoing_kernel(side, shifts, outs_count, bitmap_hbm, g_hbm, r_hbm, *refs):
-    given, outs, (bitmap, g_ref, r_ref, sems) = refs[:-5], refs[-5:-4], refs[-4:]
-    if outs_count > 1:
-        given, outs = refs[:1], refs[1:-4]
+def outgoing_kernel(side, bitmap_hbm, g_hbm, r_hbm, *refs):
+    outs, (bitmap, g_ref, r_ref, sems) = refs[:2], refs[2:]
+    shifts = [k for group in GROUPS for k in group]
     firsts = [block_of(side, k) * BLOCK + h * HALF for k in shifts for h in range(2)]
     chosen = pltpu.make_async_copy(bitmap_hbm, bitmap, sems.at[0, 0])
     chosen.start()
@@ -117,31 +116,25 @@
             place = i * HALF + t
             value = g_ref[place] + r_ref[place]
             value = jnp.where(bitmap[0, first + t] > 0, value, jnp.zeros_like(value))
-            if given:
-                value = value + given[0][place]
-                outs[place // BLOCK][place % BLOCK] = value
-            else:
-                outs[0][place] = value
-
-
-def outgoing(side, shifts, bitmap, gradients, residual, *swapped):
-    tiles = len(shifts) * BLOCK
+            outs[place // (2 * BLOCK)][place % (2 * BLOCK)] = value
+
+
+def outgoing(side, bitmap, gradients, residual):
     vmem = pl.BlockSpec(memory_space=pltpu.VMEM)
-    shapes = [tiles_shape(BLOCK)] * len(shifts) if swapped else [tiles_shape(tiles)]
-    return pl.pallas_call(
-        functools.partial(outgoing_kernel, side, shifts, len(shapes)),
-        in_specs=[pl.BlockSpec(memory_space=pl.ANY)] * 3 + [vmem] * len(swapped),
-        out_specs=[vmem] * len(shapes),
-        out_shape=shapes,
+    return pl.pallas_call(
+        functools.partial(outgoing_kernel, side),
+        in_specs=[pl.BlockSpec(memory_space=pl.ANY)] * 3,
+        out_specs=[vmem] * 2,
+        out_shape=[tiles_shape(2 * BLOCK)] * 2,
         scratch_shapes=[
             pltpu.SMEM((1, 128), jnp.int32),
-            pltpu.VMEM((tiles, 128, 128), BF16),
-            pltpu.VMEM((tiles, 128, 128), BF16),
-            pltpu.SemaphoreType.DMA((2 * len(shifts) + 1, 2)),
+            pltpu.VMEM((4 * BLOCK, 128, 128), BF16),
+            pltpu.VMEM((4 * BLOCK, 128, 128), BF16),
+            pltpu.SemaphoreType.DMA((9, 2)),
         ],
         compiler_params=params(),
-        cost_estimate=cost(3 * tiles),
-    )(bitmap, gradients, residual, *swapped)
+        cost_estimate=cost(12 * BLOCK),
+    )(bitmap, gradients, residual)
 
 
 def left_kernel(after_ref, bitmap_ref, g_ref, r_ref, out_ref, token_ref):
@@ -373,10 +366,11 @@
     residual = pltpu.with_memory_space_constraint(residual, pltpu.HBM)
     bitmap = pltpu.with_memory_space_constraint(bitmap, pltpu.HBM)
     arrays = (bitmap, gradients, residual)
-    swapped = [send(outgoing(1, shifts, *arrays)[0], swap_core()) for shifts in GROUPS]
-    two, one = pair_sums(outgoing(0, GROUPS[0], *arrays)[0], swapped[0])
+    swapped = [send(part, swap_core()) for part in outgoing(1, *arrays)]
+    kept = outgoing(0, *arrays)
+    two, one = pair_sums(kept[0], swapped[0])
     by_two, by_one = send(two, shift_first(2)), send(one, shift_first(1))
-    three, own = outgoing(0, GROUPS[1], *arrays, swapped[1])
+    three, own = pair_sums(kept[1], swapped[1])
     by_three = send(three, shift_first(3))
     left, token = left_over(three, *arrays)
 

time: 74.4 us -> 71.4 us (0.960)
  waiting for transfers between devices: 26.2 us -> 20.8 us
  starting transfers between devices: 28.5 us -> 32.6 us
  Pallas kernels: 18.5 us -> 16.9 us
    ppermute x23, waiting for transfers between devices: 26.2 us -> 20.8 us  [send(): return lax.ppermute(array, axis, pairs)]
    ppermute x23, starting transfers between devices: 28.5 us -> 32.6 us  [send(): return lax.ppermute(array, axis, pairs)]
    pallas_call x4 -> x2, Pallas kernels: 6.77 us -> 4.87 us  [outgoing(): pl.pallas_call(functools.partial(outgoing_kernel, side), in_specs=[pl.Blo...]
  transfers between devices with their start and end apart: 23 -> 23, of which waited for: 13 -> 10; matrix products, arithmetic and copies ran while one was open for 0% -> 0% of each run, Pallas kernels for 18% -> 16%
where the time goes in v4:
time: 71.4 us; the launch traced here: 71.1 us
  starting transfers between devices  32.6 us (46%)
  waiting for transfers between devices  20.8 us (29%)
  Pallas kernels  16.9 us (24%)
  between operations  0.74 us (1%)
    ppermute x23, starting transfers between devices, send(): return lax.ppermute(array, axis, pairs)  32.6 us
    ppermute x23, waiting for transfers between devices, send(): return lax.ppermute(array, axis, pairs)  20.8 us
    pallas_call x1, Pallas kernels, left_over(): pl.pallas_call(left_kernel, grid=(8,), in_specs=[pl.BlockSpec(memory_spac...  8.05 us
    pallas_call x2, Pallas kernels, outgoing(): pl.pallas_call(functools.partial(outgoing_kernel, side), in_specs=[pl.Blo...  4.87 us
    pallas_call x1, Pallas kernels, finish(): pl.pallas_call(final_kernel, in_specs=[whole] * (5 + len(blocks)), out_sp...  2.7 us
  transfers between devices with their start and end apart: 23, of which 10 were waited for; matrix products, arithmetic and copies ran while one was open for 0% of the time, Pallas kernels for 16%

profile of v4, /device:TPU:1, one launch (start us, length us, event | category | flops | bytes accessed | tf_op | source)
XLA Modules:
  0.0 71.1 jit_solution(5165822250171518335)
XLA Ops:
  0.6 2.4 %shard_map.69 = (bf16[32,128,128]{2,1,0:T(8,128)(2,1)S(1)}, bf16[32,128,128]{2,1,0:T(8,128)(2,1)S(1)}) custom-call(s32[1,128]{1,0:T(1,128)} %bitmap_ref.1, bf16[128,128,128]{2,1,0:T(8,128)(2,1)} %bitcast.3, bf16[128,128,128]{2,1,0:T(8,128)(2,1)} %bitcast.6), custom_call_target="tpu_custom_call" | custom-call | flops 3145728 | bytes 6291456 | tf_op jit(solution)/shard_map/pallas_call | solution.py:124
  3.0 1.6 %collective-permute-start.1 = (bf16[32,128,128]{2,1,0:T(8,128)(2,1)S(1)}, bf16[32,128,128]{2,1,0:T(8,128)(2,1)S(1)}, u32[]{:S(2)}, u32[]{:S(2)}) collective-permute-start(bf16[32,128,128]{2,1,0:T(8,128)(2,1)S(1)} %get-tuple-element.31), channel_id=1, source_target_pairs={{0,1},{1,0},{2,3},{3,2},{4,5},{5,4},{6,7},{7,6},{8,9},{9,8},{10,11... | collective-permute-start | bytes 3145736 | tf_op jit(solution)/shard_map/ppermute | solution.py:62
  4.7 2.5 %shard_map.68 = (bf16[32,128,128]{2,1,0:T(8,128)(2,1)S(1)}, bf16[32,128,128]{2,1,0:T(8,128)(2,1)S(1)}) custom-call(s32[1,128]{1,0:T(1,128)} %bitmap_ref.1, bf16[128,128,128]{2,1,0:T(8,128)(2,1)} %bitcast.4, bf16[128,128,128]{2,1,0:T(8,128)(2,1)} %bitcast.7), custom_call_target="tpu_custom_call" | custom-call | flops 3145728 | bytes 6291456 | tf_op jit(solution)/shard_map/pallas_call | solution.py:124
  7.5 1.8 %collective-permute-start.2 = (bf16[16,128,128]{2,1,0:T(8,128)(2,1)S(1)}, bf16[16,128,128]{2,1,0:T(8,128)(2,1)S(1)}, u32[]{:S(2)}, u32[]{:S(2)}) collective-permute-start(bf16[16,128,128]{2,1,0:T(8,128)(2,1)S(1)} %get-tuple-element.32), channel_id=1, source_target_pairs={{0,2},{1,9},{2,4},{3,11},{4,6},{5,13},{6,0},{7,15},{8,10},{9,17},{... | collective-permute-start | bytes 1572872 | tf_op jit(solution)/shard_map/ppermute | solution.py:62
  9.3 3.3 %collective-permute-start.3 = (bf16[16,128,128]{2,1,0:T(8,128)(2,1)S(1)}, bf16[16,128,128]{2,1,0:T(8,128)(2,1)S(1)}, u32[]{:S(2)}, u32[]{:S(2)}) collective-permute-start(bf16[16,128,128]{2,1,0:T(8,128)(2,1)S(1)} %get-tuple-element.33), channel_id=1, source_target_pairs={{0,4},{1,17},{2,6},{3,19},{4,0},{5,21},{6,2},{7,23},{8,12},{9,25},... | collective-permute-start | bytes 1572872 | tf_op jit(solution)/shard_map/ppermute | solution.py:62
  13.7 8.1 %shard_map.71 = (bf16[128,128,128]{2,1,0:T(8,128)(2,1)}, f32[8,128]{1,0:T(8,128)S(1)}) custom-call(bf16[16,128,128]{2,1,0:T(8,128)(2,1)S(1)} %get-tuple-element.26.after_ref, s32[1,128]{1,0:T(1,128)} %bitmap_ref.1, bf16[128,128,128]{2,1,0:T(8,128)(2,1)} %bitcast.5, bf16[128,128,128]{2,1,0:T(8,128)(2,1)} %bitcast.8), custom_call_target="tpu_custom_call" | custom-call | flops 6291456 | bytes 12582912 | tf_op jit(solution)/shard_map/pallas_call | solution.py:150
  21.7 3.0 %collective-permute-done.3.r2 = bf16[16,128,128]{2,1,0:T(8,128)(2,1)S(1)} collective-permute-done((bf16[16,128,128]{2,1,0:T(8,128)(2,1)S(1)}, bf16[16,128,128]{2,1,0:T(8,128)(2,1)S(1)}, u32[]{:S(2)}, u32[]{:S(2)}) %collective-permute-start.3) | collective-permute-done | bytes 524320 | tf_op jit(solution)/shard_map/ppermute | solution.py:62
  25.0 1.3 %collective-permute-start.5 = (bf16[8,128,128]{2,1,0:T(8,128)(2,1)S(1)}, bf16[8,128,128]{2,1,0:T(8,128)(2,1)S(1)}, u32[]{:S(2)}, u32[]{:S(2)}) collective-permute-start(bf16[8,128,128]{2,1,0:T(8,128)(2,1)S(1)} %get-tuple-element.34.a0), channel_id=1, source_target_pairs={{0,8},{1,3},{2,10},{3,1},{4,12},{5,7},{6,14},{7,5},{8,0},{9,11},{1... | collective-permute-start | bytes 786440 | tf_op jit(solution)/shard_map/ppermute | solution.py:62
  26.3 1.8 %collective-permute-start.6 = (bf16[8,128,128]{2,1,0:T(8,128)(2,1)S(1)}, bf16[8,128,128]{2,1,0:T(8,128)(2,1)S(1)}, u32[]{:S(2)}, u32[]{:S(2)}) collective-permute-start(bf16[8,128,128]{2,1,0:T(8,128)(2,1)S(1)} %get-tuple-element.35.b0), channel_id=1, source_target_pairs={{0,24},{1,7},{2,26},{3,5},{4,28},{5,3},{6,30},{7,1},{8,16},{9,15},... | collective-permute-start | bytes 786440 | tf_op jit(solution)/shard_map/ppermute | solution.py:62
  28.2 2.5 %collective-permute-done.5.a1 = bf16[8,128,128]{2,1,0:T(8,128)(2,1)S(1)} collective-permute-done((bf16[8,128,128]{2,1,0:T(8,128)(2,1)S(1)}, bf16[8,128,128]{2,1,0:T(8,128)(2,1)S(1)}, u32[]{:S(2)}, u32[]{:S(2)}) %collective-permute-start.5) | collective-permute-done | bytes 262176 | tf_op jit(solution)/shard_map/ppermute | solution.py:62
  30.6 2.4 %collective-permute-done.6.b1 = bf16[8,128,128]{2,1,0:T(8,128)(2,1)S(1)} collective-permute-done((bf16[8,128,128]{2,1,0:T(8,128)(2,1)S(1)}, bf16[8,128,128]{2,1,0:T(8,128)(2,1)S(1)}, u32[]{:S(2)}, u32[]{:S(2)}) %collective-permute-start.6) | collective-permute-done | bytes 262176 | tf_op jit(solution)/shard_map/ppermute | solution.py:62
  33.2 1.9 %collective-permute-start.7 = (bf16[8,128,128]{2,1,0:T(8,128)(2,1)S(1)}, bf16[8,128,128]{2,1,0:T(8,128)(2,1)S(1)}, u32[]{:S(2)}, u32[]{:S(2)}) collective-permute-start(bf16[8,128,128]{2,1,0:T(8,128)(2,1)S(1)} %get-tuple-element.36.a0), channel_id=1, source_target_pairs={{0,24},{1,7},{2,26},{3,5},{4,28},{5,3},{6,30},{7,1},{8,16},{9,15},... | collective-permute-start | bytes 786440 | tf_op jit(solution)/shard_map/ppermute | solution.py:62
  35.2 4.8 %collective-permute-done.7.a1 = bf16[8,128,128]{2,1,0:T(8,128)(2,1)S(1)} collective-permute-done((bf16[8,128,128]{2,1,0:T(8,128)(2,1)S(1)}, bf16[8,128,128]{2,1,0:T(8,128)(2,1)S(1)}, u32[]{:S(2)}, u32[]{:S(2)}) %collective-permute-start.7) | collective-permute-done | bytes 262176 | tf_op jit(solution)/shard_map/ppermute | solution.py:62
  40.9 1.4 %collective-permute-start.9 = (f32[8,128]{1,0:T(8,128)S(1)}, f32[8,128]{1,0:T(8,128)S(1)}, u32[]{:S(2)}, u32[]{:S(2)}) collective-permute-start(f32[8,128]{1,0:T(8,128)S(1)} %get-tuple-element.39), channel_id=1, source_target_pairs={{0,32},{32,0},{64,96},{96,64},{1,33},{33,1},{65,97},{97,65},{2,34}... | collective-permute-start | bytes 12296 | tf_op jit(solution)/shard_map/ppermute | solution.py:62
  42.3 2.0 %collective-permute-start.18 = (bf16[2048,128]{1,0:T(8,128)(2,1)S(1)}, bf16[2048,128]{1,0:T(8,128)(2,1)S(1)}, u32[]{:S(2)}, u32[]{:S(2)}) collective-permute-start(bf16[2048,128]{1,0:T(8,128)(2,1)S(1)} %get-tuple-element.43), channel_id=1, source_target_pairs={{0,4},{1,17},{2,6},{3,19},{4,0},{5,21},{6,2},{7,23},{8,12},{9,25},... | collective-permute-start | bytes 1572872 | tf_op jit(solution)/shard_map/ppermute | solution.py:62
  44.2 2.1 %collective-permute-start.10 = (f32[8,128]{1,0:T(8,128)S(1)}, f32[8,128]{1,0:T(8,128)S(1)}, u32[]{:S(2)}, u32[]{:S(2)}) collective-permute-start(f32[8,128]{1,0:T(8,128)S(1)} %add.7.mine_ref), channel_id=1, source_target_pairs={{0,96},{32,64},{64,32},{96,0},{1,97},{33,65},{65,33},{97,1},{2,98}... | collective-permute-start | bytes 12296 | tf_op jit(solution)/shard_map/ppermute | solution.py:62
  46.3 1.6 %collective-permute-done.10.other_ref = f32[8,128]{1,0:T(8,128)S(1)} collective-permute-done((f32[8,128]{1,0:T(8,128)S(1)}, f32[8,128]{1,0:T(8,128)S(1)}, u32[]{:S(2)}, u32[]{:S(2)}) %collective-permute-start.10) | collective-permute-done | bytes 4128 | tf_op jit(solution)/shard_map/ppermute | solution.py:62
  48.5 2.2 %collective-permute-start.13 = (bf16[2064,128]{1,0:T(8,128)(2,1)S(1)}, bf16[2064,128]{1,0:T(8,128)(2,1)S(1)}, u32[]{:S(2)}, u32[]{:S(2)}) collective-permute-start(bf16[2064,128]{1,0:T(8,128)(2,1)S(1)} %get-tuple-element.40.r0.refs_0_), channel_id=1, source_target_pairs={{0,6},{1,25},{2,0},{3,27},{4,2},{5,29},{6,4},{7,31},{8,14},{9,1},{... | collective-permute-start | bytes 1585160 | tf_op jit(solution)/shard_map/ppermute | solution.py:62
  50.7 1.4 %collective-permute-done.18.refs_6_ = bf16[2048,128]{1,0:T(8,128)(2,1)S(1)} collective-permute-done((bf16[2048,128]{1,0:T(8,128)(2,1)S(1)}, bf16[2048,128]{1,0:T(8,128)(2,1)S(1)}, u32[]{:S(2)}, u32[]{:S(2)}) %collective-permute-start.18) | collective-permute-done | bytes 524320 | tf_op jit(solution)/shard_map/ppermute | solution.py:62
  52.1 5.9 %collective-permute-start.19 = (bf16[16,128]{1,0:T(8,128)(2,1)S(1)}, bf16[16,128]{1,0:T(8,128)(2,1)S(1)}, u32[]{:S(2)}, u32[]{:S(2)}) collective-permute-start(bf16[16,128]{1,0:T(8,128)(2,1)S(1)} %slice.8), channel_id=1, source_target_pairs={{0,1},{1,0},{2,3},{3,2},{4,5},{5,4},{6,7},{7,6},{8,9},{9,8},{10,11... | collective-permute-start | bytes 12296 | tf_op jit(solution)/shard_map/ppermute | solution.py:62
  59.2 2.7 %collective-permute-start.15 = (bf16[2064,128]{1,0:T(8,128)(2,1)S(1)}, bf16[2064,128]{1,0:T(8,128)(2,1)S(1)}, u32[]{:S(2)}, u32[]{:S(2)}) collective-permute-start(bf16[2064,128]{1,0:T(8,128)(2,1)S(1)} %get-tuple-element.40.r0.refs_0_), channel_id=1, source_target_pairs={{0,1},{1,0},{2,3},{3,2},{4,5},{5,4},{6,7},{7,6},{8,9},{9,8},{10,11... | collective-permute-start | bytes 1585160 | tf_op jit(solution)/shard_map/ppermute | solution.py:62
  63.2 2.2 %collective-permute-start.17 = (bf16[2064,128]{1,0:T(8,128)(2,1)S(1)}, bf16[2064,128]{1,0:T(8,128)(2,1)S(1)}, u32[]{:S(2)}, u32[]{:S(2)}) collective-permute-start(bf16[2064,128]{1,0:T(8,128)(2,1)S(1)} %collective-permute-done.13.r3.refs_4_), channel_id=1, source_target_pairs={{0,1},{1,0},{2,3},{3,2},{4,5},{5,4},{6,7},{7,6},{8,9},{9,8},{10,11... | collective-permute-start | bytes 1585160 | tf_op jit(solution)/shard_map/ppermute | solution.py:62
  66.1 2.4 %collective-permute-done.14.other_ref = f32[8,128]{1,0:T(8,128)S(1)} collective-permute-done((f32[8,128]{1,0:T(8,128)S(1)}, f32[8,128]{1,0:T(8,128)S(1)}, u32[]{:S(2)}, u32[]{:S(2)}) %collective-permute-start.14) | collective-permute-done | bytes 4128 | tf_op jit(solution)/shard_map/ppermute | solution.py:62
  68.4 2.7 %shard_map.78 = bf16[128,128,128]{2,1,0:T(8,128)(2,1)} custom-call(s32[4,128]{1,0:T(4,128)S(1)} %pad.8.lo_ref, s32[4,128]{1,0:T(4,128)S(1)} %pad.9.hi_ref, f32[8,128]{1,0:T(8,128)S(1)} %shard_map.77.mine_ref, f32[8,128]{1,0:T(8,128)S(1)} %collective-permute-done.14.other_ref, bf16[128,128,128]{2,1,0:T(8,128)(2,1)S(1)} %copy-done, ...), custom_call_target="tpu_custom_call" | custom-call | flops 6291456 | bytes 12582912 | tf_op jit(solution)/shard_map/pallas_call | solution.py:345
  (42 shorter events, 6.5 us)
Async XLA Ops:
  3.0 4.2 %collective-permute-start.1 = (bf16[32,128,128]{2,1,0:T(8,128)(2,1)S(1)}, bf16[32,128,128]{2,1,0:T(8,128)(2,1)S(1)}, u32[]{:S(2)}, u32[]{:S(2)}) collective-permute-start(bf16[32,128,128]{2,1,0:T(8,128)(2,1)S(1)} %get-tuple-element.31), channel_id=1, source_target_pairs={{0,1},{1,0},{2,3},{3,2},{4,5},{5,4},{6,7},{7,6},{8,9},{9,8},{10,11... | collective-permute-start | bytes 3145736 | tf_op jit(solution)/shard_map/ppermute | solution.py:62
  4.6 8.0 %collective-permute-start = (bf16[32,128,128]{2,1,0:T(8,128)(2,1)S(1)}, bf16[32,128,128]{2,1,0:T(8,128)(2,1)S(1)}, u32[]{:S(2)}, u32[]{:S(2)}) collective-permute-start(bf16[32,128,128]{2,1,0:T(8,128)(2,1)S(1)} %get-tuple-element.25), channel_id=1, source_target_pairs={{0,1},{1,0},{2,3},{3,2},{4,5},{5,4},{6,7},{7,6},{8,9},{9,8},{10,11... | collective-permute-start | bytes 3145736 | tf_op jit(solution)/shard_map/ppermute | solution.py:62
  7.5 14.2 %collective-permute-start.2 = (bf16[16,128,128]{2,1,0:T(8,128)(2,1)S(1)}, bf16[16,128,128]{2,1,0:T(8,128)(2,1)S(1)}, u32[]{:S(2)}, u32[]{:S(2)}) collective-permute-start(bf16[16,128,128]{2,1,0:T(8,128)(2,1)S(1)} %get-tuple-element.32), channel_id=1, source_target_pairs={{0,2},{1,9},{2,4},{3,11},{4,6},{5,13},{6,0},{7,15},{8,10},{9,17},{... | collective-permute-start | bytes 1572872 | tf_op jit(solution)/shard_map/ppermute | solution.py:62
  9.3 15.5 %collective-permute-start.3 = (bf16[16,128,128]{2,1,0:T(8,128)(2,1)S(1)}, bf16[16,128,128]{2,1,0:T(8,128)(2,1)S(1)}, u32[]{:S(2)}, u32[]{:S(2)}) collective-permute-start(bf16[16,128,128]{2,1,0:T(8,128)(2,1)S(1)} %get-tuple-element.33), channel_id=1, source_target_pairs={{0,4},{1,17},{2,6},{3,19},{4,0},{5,21},{6,2},{7,23},{8,12},{9,25},... | collective-permute-start | bytes 1572872 | tf_op jit(solution)/shard_map/ppermute | solution.py:62
  12.9 11.9 %collective-permute-start.4 = (bf16[16,128,128]{2,1,0:T(8,128)(2,1)S(1)}, bf16[16,128,128]{2,1,0:T(8,128)(2,1)S(1)}, u32[]{:S(2)}, u32[]{:S(2)}) collective-permute-start(bf16[16,128,128]{2,1,0:T(8,128)(2,1)S(1)} %get-tuple-element.26.after_ref), channel_id=1, source_target_pairs={{0,6},{1,25},{2,0},{3,27},{4,2},{5,29},{6,4},{7,31},{8,14},{9,1},{... | collective-permute-start | bytes 1572872 | tf_op jit(solution)/shard_map/ppermute | solution.py:62
  21.7 46.7 %copy-start = (bf16[128,128,128]{2,1,0:T(8,128)(2,1)S(1)}, bf16[128,128,128]{2,1,0:T(8,128)(2,1)}, u32[]{:S(2)}) copy-start(bf16[128,128,128]{2,1,0:T(8,128)(2,1)} %m_ref.1) | copy-start | bytes 12582916
  25.0 5.6 %collective-permute-start.5 = (bf16[8,128,128]{2,1,0:T(8,128)(2,1)S(1)}, bf16[8,128,128]{2,1,0:T(8,128)(2,1)S(1)}, u32[]{:S(2)}, u32[]{:S(2)}) collective-permute-start(bf16[8,128,128]{2,1,0:T(8,128)(2,1)S(1)} %get-tuple-element.34.a0), channel_id=1, source_target_pairs={{0,8},{1,3},{2,10},{3,1},{4,12},{5,7},{6,14},{7,5},{8,0},{9,11},{1... | collective-permute-start | bytes 786440 | tf_op jit(solution)/shard_map/ppermute | solution.py:62
  26.3 6.7 %collective-permute-start.6 = (bf16[8,128,128]{2,1,0:T(8,128)(2,1)S(1)}, bf16[8,128,128]{2,1,0:T(8,128)(2,1)S(1)}, u32[]{:S(2)}, u32[]{:S(2)}) collective-permute-start(bf16[8,128,128]{2,1,0:T(8,128)(2,1)S(1)} %get-tuple-element.35.b0), channel_id=1, source_target_pairs={{0,24},{1,7},{2,26},{3,5},{4,28},{5,3},{6,30},{7,1},{8,16},{9,15},... | collective-permute-start | bytes 786440 | tf_op jit(solution)/shard_map/ppermute | solution.py:62
  33.2 6.8 %collective-permute-start.7 = (bf16[8,128,128]{2,1,0:T(8,128)(2,1)S(1)}, bf16[8,128,128]{2,1,0:T(8,128)(2,1)S(1)}, u32[]{:S(2)}, u32[]{:S(2)}) collective-permute-start(bf16[8,128,128]{2,1,0:T(8,128)(2,1)S(1)} %get-tuple-element.36.a0), channel_id=1, source_target_pairs={{0,24},{1,7},{2,26},{3,5},{4,28},{5,3},{6,30},{7,1},{8,16},{9,15},... | collective-permute-start | bytes 786440 | tf_op jit(solution)/shard_map/ppermute | solution.py:62
  35.1 5.5 %collective-permute-start.8 = (bf16[8,128,128]{2,1,0:T(8,128)(2,1)S(1)}, bf16[8,128,128]{2,1,0:T(8,128)(2,1)S(1)}, u32[]{:S(2)}, u32[]{:S(2)}) collective-permute-start(bf16[8,128,128]{2,1,0:T(8,128)(2,1)S(1)} %get-tuple-element.37.b0), channel_id=1, source_target_pairs={{0,8},{1,3},{2,10},{3,1},{4,12},{5,7},{6,14},{7,5},{8,0},{9,11},{1... | collective-permute-start | bytes 786440 | tf_op jit(solution)/shard_map/ppermute | solution.py:62
  40.9 3.3 %collective-permute-start.9 = (f32[8,128]{1,0:T(8,128)S(1)}, f32[8,128]{1,0:T(8,128)S(1)}, u32[]{:S(2)}, u32[]{:S(2)}) collective-permute-start(f32[8,128]{1,0:T(8,128)S(1)} %get-tuple-element.39), channel_id=1, source_target_pairs={{0,32},{32,0},{64,96},{96,64},{1,33},{33,1},{65,97},{97,65},{2,34}... | collective-permute-start | bytes 12296 | tf_op jit(solution)/shard_map/ppermute | solution.py:62
  42.3 9.8 %collective-permute-start.18 = (bf16[2048,128]{1,0:T(8,128)(2,1)S(1)}, bf16[2048,128]{1,0:T(8,128)(2,1)S(1)}, u32[]{:S(2)}, u32[]{:S(2)}) collective-permute-start(bf16[2048,128]{1,0:T(8,128)(2,1)S(1)} %get-tuple-element.43), channel_id=1, source_target_pairs={{0,4},{1,17},{2,6},{3,19},{4,0},{5,21},{6,2},{7,23},{8,12},{9,25},... | collective-permute-start | bytes 1572872 | tf_op jit(solution)/shard_map/ppermute | solution.py:62
  44.2 3.7 %collective-permute-start.10 = (f32[8,128]{1,0:T(8,128)S(1)}, f32[8,128]{1,0:T(8,128)S(1)}, u32[]{:S(2)}, u32[]{:S(2)}) collective-permute-start(f32[8,128]{1,0:T(8,128)S(1)} %add.7.mine_ref), channel_id=1, source_target_pairs={{0,96},{32,64},{64,32},{96,0},{1,97},{33,65},{65,33},{97,1},{2,98}... | collective-permute-start | bytes 12296 | tf_op jit(solution)/shard_map/ppermute | solution.py:62
  48.0 15.2 %collective-permute-start.12 = (bf16[2064,128]{1,0:T(8,128)(2,1)S(1)}, bf16[2064,128]{1,0:T(8,128)(2,1)S(1)}, u32[]{:S(2)}, u32[]{:S(2)}) collective-permute-start(bf16[2064,128]{1,0:T(8,128)(2,1)S(1)} %get-tuple-element.40.r0.refs_0_), channel_id=1, source_target_pairs={{0,2},{1,9},{2,4},{3,11},{4,6},{5,13},{6,0},{7,15},{8,10},{9,17},{... | collective-permute-start | bytes 1585160 | tf_op jit(solution)/shard_map/ppermute | solution.py:62
  48.5 14.6 %collective-permute-start.13 = (bf16[2064,128]{1,0:T(8,128)(2,1)S(1)}, bf16[2064,128]{1,0:T(8,128)(2,1)S(1)}, u32[]{:S(2)}, u32[]{:S(2)}) collective-permute-start(bf16[2064,128]{1,0:T(8,128)(2,1)S(1)} %get-tuple-element.40.r0.refs_0_), channel_id=1, source_target_pairs={{0,6},{1,25},{2,0},{3,27},{4,2},{5,29},{6,4},{7,31},{8,14},{9,1},{... | collective-permute-start | bytes 1585160 | tf_op jit(solution)/shard_map/ppermute | solution.py:62
  52.1 6.7 %collective-permute-start.19 = (bf16[16,128]{1,0:T(8,128)(2,1)S(1)}, bf16[16,128]{1,0:T(8,128)(2,1)S(1)}, u32[]{:S(2)}, u32[]{:S(2)}) collective-permute-start(bf16[16,128]{1,0:T(8,128)(2,1)S(1)} %slice.8), channel_id=1, source_target_pairs={{0,1},{1,0},{2,3},{3,2},{4,5},{5,4},{6,7},{7,6},{8,9},{9,8},{10,11... | collective-permute-start | bytes 12296 | tf_op jit(solution)/shard_map/ppermute | solution.py:62
  58.8 3.1 %collective-permute-start.20 = (bf16[16,128]{1,0:T(8,128)(2,1)S(1)}, bf16[16,128]{1,0:T(8,128)(2,1)S(1)}, u32[]{:S(2)}, u32[]{:S(2)}) collective-permute-start(bf16[16,128]{1,0:T(8,128)(2,1)S(1)} %collective-permute-done.19), channel_id=1, source_target_pairs={{0,1},{1,0},{2,3},{3,2},{4,5},{5,4},{6,7},{7,6},{8,9},{9,8},{10,11... | collective-permute-start | bytes 12296 | tf_op jit(solution)/shard_map/ppermute | solution.py:62
  59.2 4.0 %collective-permute-start.11 = (bf16[16,128]{1,0:T(8,128)(2,1)S(1)}, bf16[16,128]{1,0:T(8,128)(2,1)S(1)}, u32[]{:S(2)}, u32[]{:S(2)}) collective-permute-start(bf16[16,128]{1,0:T(8,128)(2,1)S(1)} %get-tuple-element.41), channel_id=1, source_target_pairs={{0,4},{1,17},{2,6},{3,19},{4,0},{5,21},{6,2},{7,23},{8,12},{9,25},... | collective-permute-start | bytes 12296 | tf_op jit(solution)/shard_map/ppermute | solution.py:62
  59.2 6.9 %collective-permute-start.15 = (bf16[2064,128]{1,0:T(8,128)(2,1)S(1)}, bf16[2064,128]{1,0:T(8,128)(2,1)S(1)}, u32[]{:S(2)}, u32[]{:S(2)}) collective-permute-start(bf16[2064,128]{1,0:T(8,128)(2,1)S(1)} %get-tuple-element.40.r0.refs_0_), channel_id=1, source_target_pairs={{0,1},{1,0},{2,3},{3,2},{4,5},{5,4},{6,7},{7,6},{8,9},{9,8},{10,11... | collective-permute-start | bytes 1585160 | tf_op jit(solution)/shard_map/ppermute | solution.py:62
  61.9 3.5 %collective-permute-start.21 = (bf16[16,128]{1,0:T(8,128)(2,1)S(1)}, bf16[16,128]{1,0:T(8,128)(2,1)S(1)}, u32[]{:S(2)}, u32[]{:S(2)}) collective-permute-start(bf16[16,128]{1,0:T(8,128)(2,1)S(1)} %collective-permute-done.20), channel_id=1, source_target_pairs={{0,1},{1,0},{2,3},{3,2},{4,5},{5,4},{6,7},{7,6},{8,9},{9,8},{10,11... | collective-permute-start | bytes 12296 | tf_op jit(solution)/shard_map/ppermute | solution.py:62
  63.2 5.3 %collective-permute-start.17 = (bf16[2064,128]{1,0:T(8,128)(2,1)S(1)}, bf16[2064,128]{1,0:T(8,128)(2,1)S(1)}, u32[]{:S(2)}, u32[]{:S(2)}) collective-permute-start(bf16[2064,128]{1,0:T(8,128)(2,1)S(1)} %collective-permute-done.13.r3.refs_4_), channel_id=1, source_target_pairs={{0,1},{1,0},{2,3},{3,2},{4,5},{5,4},{6,7},{7,6},{8,9},{9,8},{10,11... | collective-permute-start | bytes 1585160 | tf_op jit(solution)/shard_map/ppermute | solution.py:62
  65.4 3.1 %collective-permute-start.16 = (bf16[2064,128]{1,0:T(8,128)(2,1)S(1)}, bf16[2064,128]{1,0:T(8,128)(2,1)S(1)}, u32[]{:S(2)}, u32[]{:S(2)}) collective-permute-start(bf16[2064,128]{1,0:T(8,128)(2,1)S(1)} %collective-permute-done.12.r1.refs_2_), channel_id=1, source_target_pairs={{0,1},{1,0},{2,3},{3,2},{4,5},{5,4},{6,7},{7,6},{8,9},{9,8},{10,11... | collective-permute-start | bytes 1585160 | tf_op jit(solution)/shard_map/ppermute | solution.py:62
  65.4 3.0 %collective-permute-start.22 = (bf16[2048,128]{1,0:T(8,128)(2,1)S(1)}, bf16[2048,128]{1,0:T(8,128)(2,1)S(1)}, u32[]{:S(2)}, u32[]{:S(2)}) collective-permute-start(bf16[2048,128]{1,0:T(8,128)(2,1)S(1)} %collective-permute-done.18.refs_6_), channel_id=1, source_target_pairs={{0,1},{1,0},{2,3},{3,2},{4,5},{5,4},{6,7},{7,6},{8,9},{9,8},{10,11... | collective-permute-start | bytes 1572872 | tf_op jit(solution)/shard_map/ppermute | solution.py:62
  65.9 2.5 %collective-permute-start.14 = (f32[8,128]{1,0:T(8,128)S(1)}, f32[8,128]{1,0:T(8,128)S(1)}, u32[]{:S(2)}, u32[]{:S(2)}) collective-permute-start(f32[8,128]{1,0:T(8,128)S(1)} %shard_map.77.mine_ref), channel_id=1, source_target_pairs={{0,1},{1,0},{2,3},{3,2},{4,5},{5,4},{6,7},{7,6},{8,9},{9,8},{10,11... | collective-permute-start | bytes 12296 | tf_op jit(solution)/shard_map/ppermute | solution.py:62
  (1 other events, 22.3 us)

commit v5 on v4

--- a/solution.py
+++ b/solution.py
@@ -16,7 +16,7 @@
 BLOCK = 16
 ROWS = 16
 CHAIN = 3
-GROUPS = ((2, 1), (3, 0))
+GROUPS = ((1, 3), (2, 0))
 RETURNED = (0, 1, 3, 2)
 MIB = 2**20
 
@@ -368,11 +368,12 @@
     arrays = (bitmap, gradients, residual)
     swapped = [send(part, swap_core()) for part in outgoing(1, *arrays)]
     kept = outgoing(0, *arrays)
-    two, one = pair_sums(kept[0], swapped[0])
-    by_two, by_one = send(two, shift_first(2)), send(one, shift_first(1))
-    three, own = pair_sums(kept[1], swapped[1])
+    one, three = pair_sums(kept[0], swapped[0])
+    by_one = send(one, shift_first(1))
     by_three = send(three, shift_first(3))
-    left, token = left_over(three, *arrays)
+    two, own = pair_sums(kept[1], swapped[1])
+    by_two = send(two, shift_first(2))
+    left, token = left_over(two, *arrays)
 
     low, high = block_total(token, own, by_one, by_two, by_three)
     low, high = halves_sum(low, send(low, swap_second(1)), high, send(high, swap_second(3)))

time: 71.4 us -> 70.1 us (0.982)
  starting transfers between devices: 32.6 us -> 27.9 us
  waiting for transfers between devices: 20.8 us -> 24.1 us
    ppermute x23, starting transfers between devices: 32.6 us -> 27.9 us  [send(): return lax.ppermute(array, axis, pairs)]
    ppermute x23, waiting for transfers between devices: 20.8 us -> 24.1 us  [send(): return lax.ppermute(array, axis, pairs)]
  transfers between devices with their start and end apart: 23 -> 23, of which waited for: 10 -> 12; matrix products, arithmetic and copies ran while one was open for 0% -> 0% of each run, Pallas kernels for 16% -> 16%
where the time goes in v5:
time: 70.1 us; the launch traced here: 69.7 us
  starting transfers between devices  27.9 us (40%)
  waiting for transfers between devices  24.1 us (34%)
  Pallas kernels  16.9 us (24%)
  between operations  0.73 us (1%)
    ppermute x23, starting transfers between devices, send(): return lax.ppermute(array, axis, pairs)  27.9 us
    ppermute x23, waiting for transfers between devices, send(): return lax.ppermute(array, axis, pairs)  24.1 us
    pallas_call x1, Pallas kernels, left_over(): pl.pallas_call(left_kernel, grid=(8,), in_specs=[pl.BlockSpec(memory_spac...  8.05 us
    pallas_call x2, Pallas kernels, outgoing(): pl.pallas_call(functools.partial(outgoing_kernel, side), in_specs=[pl.Blo...  4.87 us
    pallas_call x1, Pallas kernels, finish(): pl.pallas_call(final_kernel, in_specs=[whole] * (5 + len(blocks)), out_sp...  2.7 us
  transfers between devices with their start and end apart: 23, of which 12 were waited for; matrix products, arithmetic and copies ran while one was open for 0% of the time, Pallas kernels for 16%

profile of v5, /device:TPU:1, one launch (start us, length us, event | category | flops | bytes accessed | tf_op | source)
XLA Modules:
  0.0 69.7 jit_solution(9112856818745187915)
XLA Ops:
  0.6 2.4 %shard_map.69 = (bf16[32,128,128]{2,1,0:T(8,128)(2,1)S(1)}, bf16[32,128,128]{2,1,0:T(8,128)(2,1)S(1)}) custom-call(s32[1,128]{1,0:T(1,128)} %bitmap_ref.1, bf16[128,128,128]{2,1,0:T(8,128)(2,1)} %bitcast.3, bf16[128,128,128]{2,1,0:T(8,128)(2,1)} %bitcast.6), custom_call_target="tpu_custom_call" | custom-call | flops 3145728 | bytes 6291456 | tf_op jit(solution)/shard_map/pallas_call | solution.py:124
  3.0 1.6 %collective-permute-start.1 = (bf16[32,128,128]{2,1,0:T(8,128)(2,1)S(1)}, bf16[32,128,128]{2,1,0:T(8,128)(2,1)S(1)}, u32[]{:S(2)}, u32[]{:S(2)}) collective-permute-start(bf16[32,128,128]{2,1,0:T(8,128)(2,1)S(1)} %get-tuple-element.31), channel_id=1, source_target_pairs={{0,1},{1,0},{2,3},{3,2},{4,5},{5,4},{6,7},{7,6},{8,9},{9,8},{10,11... | collective-permute-start | bytes 3145736 | tf_op jit(solution)/shard_map/ppermute | solution.py:62
  4.7 2.5 %shard_map.68 = (bf16[32,128,128]{2,1,0:T(8,128)(2,1)S(1)}, bf16[32,128,128]{2,1,0:T(8,128)(2,1)S(1)}) custom-call(s32[1,128]{1,0:T(1,128)} %bitmap_ref.1, bf16[128,128,128]{2,1,0:T(8,128)(2,1)} %bitcast.4, bf16[128,128,128]{2,1,0:T(8,128)(2,1)} %bitcast.7), custom_call_target="tpu_custom_call" | custom-call | flops 3145728 | bytes 6291456 | tf_op jit(solution)/shard_map/pallas_call | solution.py:124
  7.5 1.8 %collective-permute-start.2 = (bf16[16,128,128]{2,1,0:T(8,128)(2,1)S(1)}, bf16[16,128,128]{2,1,0:T(8,128)(2,1)S(1)}, u32[]{:S(2)}, u32[]{:S(2)}) collective-permute-start(bf16[16,128,128]{2,1,0:T(8,128)(2,1)S(1)} %get-tuple-element.32), channel_id=1, source_target_pairs={{0,2},{1,9},{2,4},{3,11},{4,6},{5,13},{6,0},{7,15},{8,10},{9,17},{... | collective-permute-start | bytes 1572872 | tf_op jit(solution)/shard_map/ppermute | solution.py:62
  9.3 2.2 %collective-permute-start.4 = (bf16[16,128,128]{2,1,0:T(8,128)(2,1)S(1)}, bf16[16,128,128]{2,1,0:T(8,128)(2,1)S(1)}, u32[]{:S(2)}, u32[]{:S(2)}) collective-permute-start(bf16[16,128,128]{2,1,0:T(8,128)(2,1)S(1)} %get-tuple-element.33), channel_id=1, source_target_pairs={{0,6},{1,25},{2,0},{3,27},{4,2},{5,29},{6,4},{7,31},{8,14},{9,1},{... | collective-permute-start | bytes 1572872 | tf_op jit(solution)/shard_map/ppermute | solution.py:62
  11.8 1.3 %collective-permute-start.3 = (bf16[16,128,128]{2,1,0:T(8,128)(2,1)S(1)}, bf16[16,128,128]{2,1,0:T(8,128)(2,1)S(1)}, u32[]{:S(2)}, u32[]{:S(2)}) collective-permute-start(bf16[16,128,128]{2,1,0:T(8,128)(2,1)S(1)} %get-tuple-element.26.after_ref), channel_id=1, source_target_pairs={{0,4},{1,17},{2,6},{3,19},{4,0},{5,21},{6,2},{7,23},{8,12},{9,25},... | collective-permute-start | bytes 1572872 | tf_op jit(solution)/shard_map/ppermute | solution.py:62
  13.1 8.1 %shard_map.71 = (bf16[128,128,128]{2,1,0:T(8,128)(2,1)}, f32[8,128]{1,0:T(8,128)S(1)}) custom-call(bf16[16,128,128]{2,1,0:T(8,128)(2,1)S(1)} %get-tuple-element.26.after_ref, s32[1,128]{1,0:T(1,128)} %bitmap_ref.1, bf16[128,128,128]{2,1,0:T(8,128)(2,1)} %bitcast.5, bf16[128,128,128]{2,1,0:T(8,128)(2,1)} %bitcast.8), custom_call_target="tpu_custom_call" | custom-call | flops 6291456 | bytes 12582912 | tf_op jit(solution)/shard_map/pallas_call | solution.py:150
  21.1 2.1 %collective-permute-done.4.r3 = bf16[16,128,128]{2,1,0:T(8,128)(2,1)S(1)} collective-permute-done((bf16[16,128,128]{2,1,0:T(8,128)(2,1)S(1)}, bf16[16,128,128]{2,1,0:T(8,128)(2,1)S(1)}, u32[]{:S(2)}, u32[]{:S(2)}) %collective-permute-start.4) | collective-permute-done | bytes 524320 | tf_op jit(solution)/shard_map/ppermute | solution.py:62
  23.2 1.5 %collective-permute-done.3.r2 = bf16[16,128,128]{2,1,0:T(8,128)(2,1)S(1)} collective-permute-done((bf16[16,128,128]{2,1,0:T(8,128)(2,1)S(1)}, bf16[16,128,128]{2,1,0:T(8,128)(2,1)S(1)}, u32[]{:S(2)}, u32[]{:S(2)}) %collective-permute-start.3) | collective-permute-done | bytes 524320 | tf_op jit(solution)/shard_map/ppermute | solution.py:62
  25.0 1.3 %collective-permute-start.5 = (bf16[8,128,128]{2,1,0:T(8,128)(2,1)S(1)}, bf16[8,128,128]{2,1,0:T(8,128)(2,1)S(1)}, u32[]{:S(2)}, u32[]{:S(2)}) collective-permute-start(bf16[8,128,128]{2,1,0:T(8,128)(2,1)S(1)} %get-tuple-element.34.a0), channel_id=1, source_target_pairs={{0,8},{1,3},{2,10},{3,1},{4,12},{5,7},{6,14},{7,5},{8,0},{9,11},{1... | collective-permute-start | bytes 786440 | tf_op jit(solution)/shard_map/ppermute | solution.py:62
  26.3 1.8 %collective-permute-start.6 = (bf16[8,128,128]{2,1,0:T(8,128)(2,1)S(1)}, bf16[8,128,128]{2,1,0:T(8,128)(2,1)S(1)}, u32[]{:S(2)}, u32[]{:S(2)}) collective-permute-start(bf16[8,128,128]{2,1,0:T(8,128)(2,1)S(1)} %get-tuple-element.35.b0), channel_id=1, source_target_pairs={{0,24},{1,7},{2,26},{3,5},{4,28},{5,3},{6,30},{7,1},{8,16},{9,15},... | collective-permute-start | bytes 786440 | tf_op jit(solution)/shard_map/ppermute | solution.py:62
  28.2 2.5 %collective-permute-done.5.a1 = bf16[8,128,128]{2,1,0:T(8,128)(2,1)S(1)} collective-permute-done((bf16[8,128,128]{2,1,0:T(8,128)(2,1)S(1)}, bf16[8,128,128]{2,1,0:T(8,128)(2,1)S(1)}, u32[]{:S(2)}, u32[]{:S(2)}) %collective-permute-start.5) | collective-permute-done | bytes 262176 | tf_op jit(solution)/shard_map/ppermute | solution.py:62
  30.6 2.4 %collective-permute-done.6.b1 = bf16[8,128,128]{2,1,0:T(8,128)(2,1)S(1)} collective-permute-done((bf16[8,128,128]{2,1,0:T(8,128)(2,1)S(1)}, bf16[8,128,128]{2,1,0:T(8,128)(2,1)S(1)}, u32[]{:S(2)}, u32[]{:S(2)}) %collective-permute-start.6) | collective-permute-done | bytes 262176 | tf_op jit(solution)/shard_map/ppermute | solution.py:62
  33.2 1.9 %collective-permute-start.7 = (bf16[8,128,128]{2,1,0:T(8,128)(2,1)S(1)}, bf16[8,128,128]{2,1,0:T(8,128)(2,1)S(1)}, u32[]{:S(2)}, u32[]{:S(2)}) collective-permute-start(bf16[8,128,128]{2,1,0:T(8,128)(2,1)S(1)} %get-tuple-element.36.a0), channel_id=1, source_target_pairs={{0,24},{1,7},{2,26},{3,5},{4,28},{5,3},{6,30},{7,1},{8,16},{9,15},... | collective-permute-start | bytes 786440 | tf_op jit(solution)/shard_map/ppermute | solution.py:62
  35.2 4.8 %collective-permute-done.7.a1 = bf16[8,128,128]{2,1,0:T(8,128)(2,1)S(1)} collective-permute-done((bf16[8,128,128]{2,1,0:T(8,128)(2,1)S(1)}, bf16[8,128,128]{2,1,0:T(8,128)(2,1)S(1)}, u32[]{:S(2)}, u32[]{:S(2)}) %collective-permute-start.7) | collective-permute-done | bytes 262176 | tf_op jit(solution)/shard_map/ppermute | solution.py:62
  40.9 1.4 %collective-permute-start.9 = (f32[8,128]{1,0:T(8,128)S(1)}, f32[8,128]{1,0:T(8,128)S(1)}, u32[]{:S(2)}, u32[]{:S(2)}) collective-permute-start(f32[8,128]{1,0:T(8,128)S(1)} %get-tuple-element.39), channel_id=1, source_target_pairs={{0,32},{32,0},{64,96},{96,64},{1,33},{33,1},{65,97},{97,65},{2,34}... | collective-permute-start | bytes 12296 | tf_op jit(solution)/shard_map/ppermute | solution.py:62
  43.5 2.7 %collective-permute-start.10 = (f32[8,128]{1,0:T(8,128)S(1)}, f32[8,128]{1,0:T(8,128)S(1)}, u32[]{:S(2)}, u32[]{:S(2)}) collective-permute-start(f32[8,128]{1,0:T(8,128)S(1)} %add.7.mine_ref), channel_id=1, source_target_pairs={{0,96},{32,64},{64,32},{96,0},{1,97},{33,65},{65,33},{97,1},{2,98}... | collective-permute-start | bytes 12296 | tf_op jit(solution)/shard_map/ppermute | solution.py:62
  48.2 1.9 %collective-permute-start.13 = (bf16[2064,128]{1,0:T(8,128)(2,1)S(1)}, bf16[2064,128]{1,0:T(8,128)(2,1)S(1)}, u32[]{:S(2)}, u32[]{:S(2)}) collective-permute-start(bf16[2064,128]{1,0:T(8,128)(2,1)S(1)} %get-tuple-element.40.r0.refs_0_), channel_id=1, source_target_pairs={{0,6},{1,25},{2,0},{3,27},{4,2},{5,29},{6,4},{7,31},{8,14},{9,1},{... | collective-permute-start | bytes 1585160 | tf_op jit(solution)/shard_map/ppermute | solution.py:62
  50.0 2.0 %collective-permute-done.18.refs_6_ = bf16[2048,128]{1,0:T(8,128)(2,1)S(1)} collective-permute-done((bf16[2048,128]{1,0:T(8,128)(2,1)S(1)}, bf16[2048,128]{1,0:T(8,128)(2,1)S(1)}, u32[]{:S(2)}, u32[]{:S(2)}) %collective-permute-start.18) | collective-permute-done | bytes 524320 | tf_op jit(solution)/shard_map/ppermute | solution.py:62
  52.1 4.5 %collective-permute-start.19 = (bf16[16,128]{1,0:T(8,128)(2,1)S(1)}, bf16[16,128]{1,0:T(8,128)(2,1)S(1)}, u32[]{:S(2)}, u32[]{:S(2)}) collective-permute-start(bf16[16,128]{1,0:T(8,128)(2,1)S(1)} %slice.8), channel_id=1, source_target_pairs={{0,1},{1,0},{2,3},{3,2},{4,5},{5,4},{6,7},{7,6},{8,9},{9,8},{10,11... | collective-permute-start | bytes 12296 | tf_op jit(solution)/shard_map/ppermute | solution.py:62
  58.9 2.8 %collective-permute-done.11.r2 = bf16[16,128]{1,0:T(8,128)(2,1)S(1)} collective-permute-done((bf16[16,128]{1,0:T(8,128)(2,1)S(1)}, bf16[16,128]{1,0:T(8,128)(2,1)S(1)}, u32[]{:S(2)}, u32[]{:S(2)}) %collective-permute-start.11) | collective-permute-done | bytes 4128 | tf_op jit(solution)/shard_map/ppermute | solution.py:62
  61.7 2.3 %collective-permute-start.17 = (bf16[2064,128]{1,0:T(8,128)(2,1)S(1)}, bf16[2064,128]{1,0:T(8,128)(2,1)S(1)}, u32[]{:S(2)}, u32[]{:S(2)}) collective-permute-start(bf16[2064,128]{1,0:T(8,128)(2,1)S(1)} %collective-permute-done.13.r3.refs_4_), channel_id=1, source_target_pairs={{0,1},{1,0},{2,3},{3,2},{4,5},{5,4},{6,7},{7,6},{8,9},{9,8},{10,11... | collective-permute-start | bytes 1585160 | tf_op jit(solution)/shard_map/ppermute | solution.py:62
  64.7 2.4 %collective-permute-done.14.other_ref = f32[8,128]{1,0:T(8,128)S(1)} collective-permute-done((f32[8,128]{1,0:T(8,128)S(1)}, f32[8,128]{1,0:T(8,128)S(1)}, u32[]{:S(2)}, u32[]{:S(2)}) %collective-permute-start.14) | collective-permute-done | bytes 4128 | tf_op jit(solution)/shard_map/ppermute | solution.py:62
  67.0 2.7 %shard_map.78 = bf16[128,128,128]{2,1,0:T(8,128)(2,1)} custom-call(s32[4,128]{1,0:T(4,128)S(1)} %pad.8.lo_ref, s32[4,128]{1,0:T(4,128)S(1)} %pad.9.hi_ref, f32[8,128]{1,0:T(8,128)S(1)} %shard_map.77.mine_ref, f32[8,128]{1,0:T(8,128)S(1)} %collective-permute-done.14.other_ref, bf16[128,128,128]{2,1,0:T(8,128)(2,1)S(1)} %copy-done, ...), custom_call_target="tpu_custom_call" | custom-call | flops 6291456 | bytes 12582912 | tf_op jit(solution)/shard_map/pallas_call | solution.py:345
  (42 shorter events, 8.2 us)
Async XLA Ops:
  3.0 4.2 %collective-permute-start.1 = (bf16[32,128,128]{2,1,0:T(8,128)(2,1)S(1)}, bf16[32,128,128]{2,1,0:T(8,128)(2,1)S(1)}, u32[]{:S(2)}, u32[]{:S(2)}) collective-permute-start(bf16[32,128,128]{2,1,0:T(8,128)(2,1)S(1)} %get-tuple-element.31), channel_id=1, source_target_pairs={{0,1},{1,0},{2,3},{3,2},{4,5},{5,4},{6,7},{7,6},{8,9},{9,8},{10,11... | collective-permute-start | bytes 3145736 | tf_op jit(solution)/shard_map/ppermute | solution.py:62
  4.6 6.9 %collective-permute-start = (bf16[32,128,128]{2,1,0:T(8,128)(2,1)S(1)}, bf16[32,128,128]{2,1,0:T(8,128)(2,1)S(1)}, u32[]{:S(2)}, u32[]{:S(2)}) collective-permute-start(bf16[32,128,128]{2,1,0:T(8,128)(2,1)S(1)} %get-tuple-element.25), channel_id=1, source_target_pairs={{0,1},{1,0},{2,3},{3,2},{4,5},{5,4},{6,7},{7,6},{8,9},{9,8},{10,11... | collective-permute-start | bytes 3145736 | tf_op jit(solution)/shard_map/ppermute | solution.py:62
  7.5 13.6 %collective-permute-start.2 = (bf16[16,128,128]{2,1,0:T(8,128)(2,1)S(1)}, bf16[16,128,128]{2,1,0:T(8,128)(2,1)S(1)}, u32[]{:S(2)}, u32[]{:S(2)}) collective-permute-start(bf16[16,128,128]{2,1,0:T(8,128)(2,1)S(1)} %get-tuple-element.32), channel_id=1, source_target_pairs={{0,2},{1,9},{2,4},{3,11},{4,6},{5,13},{6,0},{7,15},{8,10},{9,17},{... | collective-permute-start | bytes 1572872 | tf_op jit(solution)/shard_map/ppermute | solution.py:62
  9.3 13.9 %collective-permute-start.4 = (bf16[16,128,128]{2,1,0:T(8,128)(2,1)S(1)}, bf16[16,128,128]{2,1,0:T(8,128)(2,1)S(1)}, u32[]{:S(2)}, u32[]{:S(2)}) collective-permute-start(bf16[16,128,128]{2,1,0:T(8,128)(2,1)S(1)} %get-tuple-element.33), channel_id=1, source_target_pairs={{0,6},{1,25},{2,0},{3,27},{4,2},{5,29},{6,4},{7,31},{8,14},{9,1},{... | collective-permute-start | bytes 1572872 | tf_op jit(solution)/shard_map/ppermute | solution.py:62
  11.8 13.0 %collective-permute-start.3 = (bf16[16,128,128]{2,1,0:T(8,128)(2,1)S(1)}, bf16[16,128,128]{2,1,0:T(8,128)(2,1)S(1)}, u32[]{:S(2)}, u32[]{:S(2)}) collective-permute-start(bf16[16,128,128]{2,1,0:T(8,128)(2,1)S(1)} %get-tuple-element.26.after_ref), channel_id=1, source_target_pairs={{0,4},{1,17},{2,6},{3,19},{4,0},{5,21},{6,2},{7,23},{8,12},{9,25},... | collective-permute-start | bytes 1572872 | tf_op jit(solution)/shard_map/ppermute | solution.py:62
  21.1 45.9 %copy-start = (bf16[128,128,128]{2,1,0:T(8,128)(2,1)S(1)}, bf16[128,128,128]{2,1,0:T(8,128)(2,1)}, u32[]{:S(2)}) copy-start(bf16[128,128,128]{2,1,0:T(8,128)(2,1)} %m_ref.1) | copy-start | bytes 12582916
  25.0 5.6 %collective-permute-start.5 = (bf16[8,128,128]{2,1,0:T(8,128)(2,1)S(1)}, bf16[8,128,128]{2,1,0:T(8,128)(2,1)S(1)}, u32[]{:S(2)}, u32[]{:S(2)}) collective-permute-start(bf16[8,128,128]{2,1,0:T(8,128)(2,1)S(1)} %get-tuple-element.34.a0), channel_id=1, source_target_pairs={{0,8},{1,3},{2,10},{3,1},{4,12},{5,7},{6,14},{7,5},{8,0},{9,11},{1... | collective-permute-start | bytes 786440 | tf_op jit(solution)/shard_map/ppermute | solution.py:62
  26.3 6.7 %collective-permute-start.6 = (bf16[8,128,128]{2,1,0:T(8,128)(2,1)S(1)}, bf16[8,128,128]{2,1,0:T(8,128)(2,1)S(1)}, u32[]{:S(2)}, u32[]{:S(2)}) collective-permute-start(bf16[8,128,128]{2,1,0:T(8,128)(2,1)S(1)} %get-tuple-element.35.b0), channel_id=1, source_target_pairs={{0,24},{1,7},{2,26},{3,5},{4,28},{5,3},{6,30},{7,1},{8,16},{9,15},... | collective-permute-start | bytes 786440 | tf_op jit(solution)/shard_map/ppermute | solution.py:62
  33.2 6.8 %collective-permute-start.7 = (bf16[8,128,128]{2,1,0:T(8,128)(2,1)S(1)}, bf16[8,128,128]{2,1,0:T(8,128)(2,1)S(1)}, u32[]{:S(2)}, u32[]{:S(2)}) collective-permute-start(bf16[8,128,128]{2,1,0:T(8,128)(2,1)S(1)} %get-tuple-element.36.a0), channel_id=1, source_target_pairs={{0,24},{1,7},{2,26},{3,5},{4,28},{5,3},{6,30},{7,1},{8,16},{9,15},... | collective-permute-start | bytes 786440 | tf_op jit(solution)/shard_map/ppermute | solution.py:62
  35.1 5.5 %collective-permute-start.8 = (bf16[8,128,128]{2,1,0:T(8,128)(2,1)S(1)}, bf16[8,128,128]{2,1,0:T(8,128)(2,1)S(1)}, u32[]{:S(2)}, u32[]{:S(2)}) collective-permute-start(bf16[8,128,128]{2,1,0:T(8,128)(2,1)S(1)} %get-tuple-element.37.b0), channel_id=1, source_target_pairs={{0,8},{1,3},{2,10},{3,1},{4,12},{5,7},{6,14},{7,5},{8,0},{9,11},{1... | collective-permute-start | bytes 786440 | tf_op jit(solution)/shard_map/ppermute | solution.py:62
  40.9 2.6 %collective-permute-start.9 = (f32[8,128]{1,0:T(8,128)S(1)}, f32[8,128]{1,0:T(8,128)S(1)}, u32[]{:S(2)}, u32[]{:S(2)}) collective-permute-start(f32[8,128]{1,0:T(8,128)S(1)} %get-tuple-element.39), channel_id=1, source_target_pairs={{0,32},{32,0},{64,96},{96,64},{1,33},{33,1},{65,97},{97,65},{2,34}... | collective-permute-start | bytes 12296 | tf_op jit(solution)/shard_map/ppermute | solution.py:62
  42.2 9.8 %collective-permute-start.18 = (bf16[2048,128]{1,0:T(8,128)(2,1)S(1)}, bf16[2048,128]{1,0:T(8,128)(2,1)S(1)}, u32[]{:S(2)}, u32[]{:S(2)}) collective-permute-start(bf16[2048,128]{1,0:T(8,128)(2,1)S(1)} %get-tuple-element.43), channel_id=1, source_target_pairs={{0,4},{1,17},{2,6},{3,19},{4,0},{5,21},{6,2},{7,23},{8,12},{9,25},... | collective-permute-start | bytes 1572872 | tf_op jit(solution)/shard_map/ppermute | solution.py:62
  43.5 3.7 %collective-permute-start.10 = (f32[8,128]{1,0:T(8,128)S(1)}, f32[8,128]{1,0:T(8,128)S(1)}, u32[]{:S(2)}, u32[]{:S(2)}) collective-permute-start(f32[8,128]{1,0:T(8,128)S(1)} %add.7.mine_ref), channel_id=1, source_target_pairs={{0,96},{32,64},{64,32},{96,0},{1,97},{33,65},{65,33},{97,1},{2,98}... | collective-permute-start | bytes 12296 | tf_op jit(solution)/shard_map/ppermute | solution.py:62
  47.3 14.4 %collective-permute-start.12 = (bf16[2064,128]{1,0:T(8,128)(2,1)S(1)}, bf16[2064,128]{1,0:T(8,128)(2,1)S(1)}, u32[]{:S(2)}, u32[]{:S(2)}) collective-permute-start(bf16[2064,128]{1,0:T(8,128)(2,1)S(1)} %get-tuple-element.40.r0.refs_0_), channel_id=1, source_target_pairs={{0,2},{1,9},{2,4},{3,11},{4,6},{5,13},{6,0},{7,15},{8,10},{9,17},{... | collective-permute-start | bytes 1585160 | tf_op jit(solution)/shard_map/ppermute | solution.py:62
  48.2 13.5 %collective-permute-start.13 = (bf16[2064,128]{1,0:T(8,128)(2,1)S(1)}, bf16[2064,128]{1,0:T(8,128)(2,1)S(1)}, u32[]{:S(2)}, u32[]{:S(2)}) collective-permute-start(bf16[2064,128]{1,0:T(8,128)(2,1)S(1)} %get-tuple-element.40.r0.refs_0_), channel_id=1, source_target_pairs={{0,6},{1,25},{2,0},{3,27},{4,2},{5,29},{6,4},{7,31},{8,14},{9,1},{... | collective-permute-start | bytes 1585160 | tf_op jit(solution)/shard_map/ppermute | solution.py:62
  52.1 5.3 %collective-permute-start.19 = (bf16[16,128]{1,0:T(8,128)(2,1)S(1)}, bf16[16,128]{1,0:T(8,128)(2,1)S(1)}, u32[]{:S(2)}, u32[]{:S(2)}) collective-permute-start(bf16[16,128]{1,0:T(8,128)(2,1)S(1)} %slice.8), channel_id=1, source_target_pairs={{0,1},{1,0},{2,3},{3,2},{4,5},{5,4},{6,7},{7,6},{8,9},{9,8},{10,11... | collective-permute-start | bytes 12296 | tf_op jit(solution)/shard_map/ppermute | solution.py:62
  57.4 1.3 %collective-permute-start.20 = (bf16[16,128]{1,0:T(8,128)(2,1)S(1)}, bf16[16,128]{1,0:T(8,128)(2,1)S(1)}, u32[]{:S(2)}, u32[]{:S(2)}) collective-permute-start(bf16[16,128]{1,0:T(8,128)(2,1)S(1)} %collective-permute-done.19), channel_id=1, source_target_pairs={{0,1},{1,0},{2,3},{3,2},{4,5},{5,4},{6,7},{7,6},{8,9},{9,8},{10,11... | collective-permute-start | bytes 12296 | tf_op jit(solution)/shard_map/ppermute | solution.py:62
  57.7 4.0 %collective-permute-start.11 = (bf16[16,128]{1,0:T(8,128)(2,1)S(1)}, bf16[16,128]{1,0:T(8,128)(2,1)S(1)}, u32[]{:S(2)}, u32[]{:S(2)}) collective-permute-start(bf16[16,128]{1,0:T(8,128)(2,1)S(1)} %get-tuple-element.41), channel_id=1, source_target_pairs={{0,4},{1,17},{2,6},{3,19},{4,0},{5,21},{6,2},{7,23},{8,12},{9,25},... | collective-permute-start | bytes 12296 | tf_op jit(solution)/shard_map/ppermute | solution.py:62
  57.7 7.0 %collective-permute-start.15 = (bf16[2064,128]{1,0:T(8,128)(2,1)S(1)}, bf16[2064,128]{1,0:T(8,128)(2,1)S(1)}, u32[]{:S(2)}, u32[]{:S(2)}) collective-permute-start(bf16[2064,128]{1,0:T(8,128)(2,1)S(1)} %get-tuple-element.40.r0.refs_0_), channel_id=1, source_target_pairs={{0,1},{1,0},{2,3},{3,2},{4,5},{5,4},{6,7},{7,6},{8,9},{9,8},{10,11... | collective-permute-start | bytes 1585160 | tf_op jit(solution)/shard_map/ppermute | solution.py:62
  58.7 5.3 %collective-permute-start.21 = (bf16[16,128]{1,0:T(8,128)(2,1)S(1)}, bf16[16,128]{1,0:T(8,128)(2,1)S(1)}, u32[]{:S(2)}, u32[]{:S(2)}) collective-permute-start(bf16[16,128]{1,0:T(8,128)(2,1)S(1)} %collective-permute-done.20), channel_id=1, source_target_pairs={{0,1},{1,0},{2,3},{3,2},{4,5},{5,4},{6,7},{7,6},{8,9},{9,8},{10,11... | collective-permute-start | bytes 12296 | tf_op jit(solution)/shard_map/ppermute | solution.py:62
  61.7 5.3 %collective-permute-start.17 = (bf16[2064,128]{1,0:T(8,128)(2,1)S(1)}, bf16[2064,128]{1,0:T(8,128)(2,1)S(1)}, u32[]{:S(2)}, u32[]{:S(2)}) collective-permute-start(bf16[2064,128]{1,0:T(8,128)(2,1)S(1)} %collective-permute-done.13.r3.refs_4_), channel_id=1, source_target_pairs={{0,1},{1,0},{2,3},{3,2},{4,5},{5,4},{6,7},{7,6},{8,9},{9,8},{10,11... | collective-permute-start | bytes 1585160 | tf_op jit(solution)/shard_map/ppermute | solution.py:62
  64.0 3.1 %collective-permute-start.16 = (bf16[2064,128]{1,0:T(8,128)(2,1)S(1)}, bf16[2064,128]{1,0:T(8,128)(2,1)S(1)}, u32[]{:S(2)}, u32[]{:S(2)}) collective-permute-start(bf16[2064,128]{1,0:T(8,128)(2,1)S(1)} %collective-permute-done.12.r1.refs_2_), channel_id=1, source_target_pairs={{0,1},{1,0},{2,3},{3,2},{4,5},{5,4},{6,7},{7,6},{8,9},{9,8},{10,11... | collective-permute-start | bytes 1585160 | tf_op jit(solution)/shard_map/ppermute | solution.py:62
  64.1 3.0 %collective-permute-start.22 = (bf16[2048,128]{1,0:T(8,128)(2,1)S(1)}, bf16[2048,128]{1,0:T(8,128)(2,1)S(1)}, u32[]{:S(2)}, u32[]{:S(2)}) collective-permute-start(bf16[2048,128]{1,0:T(8,128)(2,1)S(1)} %collective-permute-done.18.refs_6_), channel_id=1, source_target_pairs={{0,1},{1,0},{2,3},{3,2},{4,5},{5,4},{6,7},{7,6},{8,9},{9,8},{10,11... | collective-permute-start | bytes 1572872 | tf_op jit(solution)/shard_map/ppermute | solution.py:62
  64.5 2.5 %collective-permute-start.14 = (f32[8,128]{1,0:T(8,128)S(1)}, f32[8,128]{1,0:T(8,128)S(1)}, u32[]{:S(2)}, u32[]{:S(2)}) collective-permute-start(f32[8,128]{1,0:T(8,128)S(1)} %shard_map.77.mine_ref), channel_id=1, source_target_pairs={{0,1},{1,0},{2,3},{3,2},{4,5},{5,4},{6,7},{7,6},{8,9},{9,8},{10,11... | collective-permute-start | bytes 12296 | tf_op jit(solution)/shard_map/ppermute | solution.py:62
  (1 other events, 23.3 us)

commit v6 on v5

--- a/solution.py
+++ b/solution.py
@@ -314,7 +314,7 @@
     chosen = jnp.where((lo <= tile) & (tile < hi), clip, 0.0)
     factor_ref[...] = jnp.broadcast_to(jnp.sum(chosen, axis=1, keepdims=True), (128, 128))
 
-    def tiles_of(source, count, first, place):
+    def tiles_of(source, start, first, place):
         def one_tile(t, carry):
             value = source[pl.ds(pl.multiple_of(t * 128, 128), 128), :]
             update = value.astype(F32) * factor_ref[pl.ds(first + t, 1), :]
@@ -322,20 +322,22 @@
             ready_ref[place + t] = new.astype(BF16)
             return carry
 
-        lax.fori_loop(0, count, one_tile, 0, unroll=4)
+        lax.fori_loop(start, start + HALF, one_tile, 0, unroll=HALF)
 
     copies = []
     for k in range(8):
         first = block_of(k % 2, -RETURNED[k // 2]) * BLOCK
-        tiles_of(blocks[k], BLOCK, first, k * BLOCK)
-        copies.append(
-            pltpu.make_async_copy(
-                ready_ref.at[pl.ds(k * BLOCK, BLOCK)],
-                out_ref.at[pl.ds(first, BLOCK)],
-                sems.at[k],
+        for half in range(2):
+            start, place = half * HALF, k * BLOCK + half * HALF
+            tiles_of(blocks[k], start, first, k * BLOCK)
+            copies.append(
+                pltpu.make_async_copy(
+                    ready_ref.at[pl.ds(place, HALF)],
+                    out_ref.at[pl.ds(first + start, HALF)],
+                    sems.at[2 * k + half],
+                )
             )
-        )
-        copies[-1].start()
+            copies[-1].start()
     for copy in copies:
         copy.wait()
 
@@ -349,7 +351,7 @@
         scratch_shapes=[
             pltpu.VMEM((128, 128), F32),
             pltpu.VMEM((128, 128, 128), BF16),
-            pltpu.SemaphoreType.DMA((8,)),
+            pltpu.SemaphoreType.DMA((16,)),
         ],
         out_shape=tiles_shape(128),
         compiler_params=params(20),

time: 70.1 us -> 69.8 us (level)
  no operation moved by 1% of the time
where the time goes in v6:
time: 69.8 us; the launch traced here: 69.5 us
  starting transfers between devices  27.9 us (40%)
  waiting for transfers between devices  24.1 us (35%)
  Pallas kernels  16.7 us (24%)
  between operations  0.73 us (1%)
    ppermute x23, starting transfers between devices, send(): return lax.ppermute(array, axis, pairs)  27.9 us
    ppermute x23, waiting for transfers between devices, send(): return lax.ppermute(array, axis, pairs)  24.1 us
    pallas_call x1, Pallas kernels, left_over(): pl.pallas_call(left_kernel, grid=(8,), in_specs=[pl.BlockSpec(memory_spac...  8.05 us
    pallas_call x2, Pallas kernels, outgoing(): pl.pallas_call(functools.partial(outgoing_kernel, side), in_specs=[pl.Blo...  4.87 us
    pallas_call x1, Pallas kernels, finish(): pl.pallas_call(final_kernel, in_specs=[whole] * (5 + len(blocks)), out_sp...  2.5 us
  transfers between devices with their start and end apart: 23, of which 12 were waited for; matrix products, arithmetic and copies ran while one was open for 0% of the time, Pallas kernels for 16%

profile of v6, /device:TPU:1, one launch (start us, length us, event | category | flops | bytes accessed | tf_op | source)
XLA Modules:
  0.0 69.5 jit_solution(5243409316058464776)
XLA Ops:
  0.6 2.4 %shard_map.69 = (bf16[32,128,128]{2,1,0:T(8,128)(2,1)S(1)}, bf16[32,128,128]{2,1,0:T(8,128)(2,1)S(1)}) custom-call(s32[1,128]{1,0:T(1,128)} %bitmap_ref.1, bf16[128,128,128]{2,1,0:T(8,128)(2,1)} %bitcast.3, bf16[128,128,128]{2,1,0:T(8,128)(2,1)} %bitcast.6), custom_call_target="tpu_custom_call" | custom-call | flops 3145728 | bytes 6291456 | tf_op jit(solution)/shard_map/pallas_call | solution.py:124
  3.0 1.6 %collective-permute-start.1 = (bf16[32,128,128]{2,1,0:T(8,128)(2,1)S(1)}, bf16[32,128,128]{2,1,0:T(8,128)(2,1)S(1)}, u32[]{:S(2)}, u32[]{:S(2)}) collective-permute-start(bf16[32,128,128]{2,1,0:T(8,128)(2,1)S(1)} %get-tuple-element.31), channel_id=1, source_target_pairs={{0,1},{1,0},{2,3},{3,2},{4,5},{5,4},{6,7},{7,6},{8,9},{9,8},{10,11... | collective-permute-start | bytes 3145736 | tf_op jit(solution)/shard_map/ppermute | solution.py:62
  4.7 2.5 %shard_map.68 = (bf16[32,128,128]{2,1,0:T(8,128)(2,1)S(1)}, bf16[32,128,128]{2,1,0:T(8,128)(2,1)S(1)}) custom-call(s32[1,128]{1,0:T(1,128)} %bitmap_ref.1, bf16[128,128,128]{2,1,0:T(8,128)(2,1)} %bitcast.4, bf16[128,128,128]{2,1,0:T(8,128)(2,1)} %bitcast.7), custom_call_target="tpu_custom_call" | custom-call | flops 3145728 | bytes 6291456 | tf_op jit(solution)/shard_map/pallas_call | solution.py:124
  7.5 1.8 %collective-permute-start.2 = (bf16[16,128,128]{2,1,0:T(8,128)(2,1)S(1)}, bf16[16,128,128]{2,1,0:T(8,128)(2,1)S(1)}, u32[]{:S(2)}, u32[]{:S(2)}) collective-permute-start(bf16[16,128,128]{2,1,0:T(8,128)(2,1)S(1)} %get-tuple-element.32), channel_id=1, source_target_pairs={{0,2},{1,9},{2,4},{3,11},{4,6},{5,13},{6,0},{7,15},{8,10},{9,17},{... | collective-permute-start | bytes 1572872 | tf_op jit(solution)/shard_map/ppermute | solution.py:62
  9.3 2.2 %collective-permute-start.4 = (bf16[16,128,128]{2,1,0:T(8,128)(2,1)S(1)}, bf16[16,128,128]{2,1,0:T(8,128)(2,1)S(1)}, u32[]{:S(2)}, u32[]{:S(2)}) collective-permute-start(bf16[16,128,128]{2,1,0:T(8,128)(2,1)S(1)} %get-tuple-element.33), channel_id=1, source_target_pairs={{0,6},{1,25},{2,0},{3,27},{4,2},{5,29},{6,4},{7,31},{8,14},{9,1},{... | collective-permute-start | bytes 1572872 | tf_op jit(solution)/shard_map/ppermute | solution.py:62
  11.8 1.3 %collective-permute-start.3 = (bf16[16,128,128]{2,1,0:T(8,128)(2,1)S(1)}, bf16[16,128,128]{2,1,0:T(8,128)(2,1)S(1)}, u32[]{:S(2)}, u32[]{:S(2)}) collective-permute-start(bf16[16,128,128]{2,1,0:T(8,128)(2,1)S(1)} %get-tuple-element.26.after_ref), channel_id=1, source_target_pairs={{0,4},{1,17},{2,6},{3,19},{4,0},{5,21},{6,2},{7,23},{8,12},{9,25},... | collective-permute-start | bytes 1572872 | tf_op jit(solution)/shard_map/ppermute | solution.py:62
  13.1 8.1 %shard_map.71 = (bf16[128,128,128]{2,1,0:T(8,128)(2,1)}, f32[8,128]{1,0:T(8,128)S(1)}) custom-call(bf16[16,128,128]{2,1,0:T(8,128)(2,1)S(1)} %get-tuple-element.26.after_ref, s32[1,128]{1,0:T(1,128)} %bitmap_ref.1, bf16[128,128,128]{2,1,0:T(8,128)(2,1)} %bitcast.5, bf16[128,128,128]{2,1,0:T(8,128)(2,1)} %bitcast.8), custom_call_target="tpu_custom_call" | custom-call | flops 6291456 | bytes 12582912 | tf_op jit(solution)/shard_map/pallas_call | solution.py:150
  21.1 2.1 %collective-permute-done.4.r3 = bf16[16,128,128]{2,1,0:T(8,128)(2,1)S(1)} collective-permute-done((bf16[16,128,128]{2,1,0:T(8,128)(2,1)S(1)}, bf16[16,128,128]{2,1,0:T(8,128)(2,1)S(1)}, u32[]{:S(2)}, u32[]{:S(2)}) %collective-permute-start.4) | collective-permute-done | bytes 524320 | tf_op jit(solution)/shard_map/ppermute | solution.py:62
  23.2 1.5 %collective-permute-done.3.r2 = bf16[16,128,128]{2,1,0:T(8,128)(2,1)S(1)} collective-permute-done((bf16[16,128,128]{2,1,0:T(8,128)(2,1)S(1)}, bf16[16,128,128]{2,1,0:T(8,128)(2,1)S(1)}, u32[]{:S(2)}, u32[]{:S(2)}) %collective-permute-start.3) | collective-permute-done | bytes 524320 | tf_op jit(solution)/shard_map/ppermute | solution.py:62
  25.0 1.3 %collective-permute-start.5 = (bf16[8,128,128]{2,1,0:T(8,128)(2,1)S(1)}, bf16[8,128,128]{2,1,0:T(8,128)(2,1)S(1)}, u32[]{:S(2)}, u32[]{:S(2)}) collective-permute-start(bf16[8,128,128]{2,1,0:T(8,128)(2,1)S(1)} %get-tuple-element.34.a0), channel_id=1, source_target_pairs={{0,8},{1,3},{2,10},{3,1},{4,12},{5,7},{6,14},{7,5},{8,0},{9,11},{1... | collective-permute-start | bytes 786440 | tf_op jit(solution)/shard_map/ppermute | solution.py:62
  26.3 1.8 %collective-permute-start.6 = (bf16[8,128,128]{2,1,0:T(8,128)(2,1)S(1)}, bf16[8,128,128]{2,1,0:T(8,128)(2,1)S(1)}, u32[]{:S(2)}, u32[]{:S(2)}) collective-permute-start(bf16[8,128,128]{2,1,0:T(8,128)(2,1)S(1)} %get-tuple-element.35.b0), channel_id=1, source_target_pairs={{0,24},{1,7},{2,26},{3,5},{4,28},{5,3},{6,30},{7,1},{8,16},{9,15},... | collective-permute-start | bytes 786440 | tf_op jit(solution)/shard_map/ppermute | solution.py:62
  28.2 2.5 %collective-permute-done.5.a1 = bf16[8,128,128]{2,1,0:T(8,128)(2,1)S(1)} collective-permute-done((bf16[8,128,128]{2,1,0:T(8,128)(2,1)S(1)}, bf16[8,128,128]{2,1,0:T(8,128)(2,1)S(1)}, u32[]{:S(2)}, u32[]{:S(2)}) %collective-permute-start.5) | collective-permute-done | bytes 262176 | tf_op jit(solution)/shard_map/ppermute | solution.py:62
  30.6 2.4 %collective-permute-done.6.b1 = bf16[8,128,128]{2,1,0:T(8,128)(2,1)S(1)} collective-permute-done((bf16[8,128,128]{2,1,0:T(8,128)(2,1)S(1)}, bf16[8,128,128]{2,1,0:T(8,128)(2,1)S(1)}, u32[]{:S(2)}, u32[]{:S(2)}) %collective-permute-start.6) | collective-permute-done | bytes 262176 | tf_op jit(solution)/shard_map/ppermute | solution.py:62
  33.2 1.9 %collective-permute-start.7 = (bf16[8,128,128]{2,1,0:T(8,128)(2,1)S(1)}, bf16[8,128,128]{2,1,0:T(8,128)(2,1)S(1)}, u32[]{:S(2)}, u32[]{:S(2)}) collective-permute-start(bf16[8,128,128]{2,1,0:T(8,128)(2,1)S(1)} %get-tuple-element.36.a0), channel_id=1, source_target_pairs={{0,24},{1,7},{2,26},{3,5},{4,28},{5,3},{6,30},{7,1},{8,16},{9,15},... | collective-permute-start | bytes 786440 | tf_op jit(solution)/shard_map/ppermute | solution.py:62
  35.2 4.8 %collective-permute-done.7.a1 = bf16[8,128,128]{2,1,0:T(8,128)(2,1)S(1)} collective-permute-done((bf16[8,128,128]{2,1,0:T(8,128)(2,1)S(1)}, bf16[8,128,128]{2,1,0:T(8,128)(2,1)S(1)}, u32[]{:S(2)}, u32[]{:S(2)}) %collective-permute-start.7) | collective-permute-done | bytes 262176 | tf_op jit(solution)/shard_map/ppermute | solution.py:62
  40.9 1.4 %collective-permute-start.9 = (f32[8,128]{1,0:T(8,128)S(1)}, f32[8,128]{1,0:T(8,128)S(1)}, u32[]{:S(2)}, u32[]{:S(2)}) collective-permute-start(f32[8,128]{1,0:T(8,128)S(1)} %get-tuple-element.39), channel_id=1, source_target_pairs={{0,32},{32,0},{64,96},{96,64},{1,33},{33,1},{65,97},{97,65},{2,34}... | collective-permute-start | bytes 12296 | tf_op jit(solution)/shard_map/ppermute | solution.py:62
  43.5 2.7 %collective-permute-start.10 = (f32[8,128]{1,0:T(8,128)S(1)}, f32[8,128]{1,0:T(8,128)S(1)}, u32[]{:S(2)}, u32[]{:S(2)}) collective-permute-start(f32[8,128]{1,0:T(8,128)S(1)} %add.7.mine_ref), channel_id=1, source_target_pairs={{0,96},{32,64},{64,32},{96,0},{1,97},{33,65},{65,33},{97,1},{2,98}... | collective-permute-start | bytes 12296 | tf_op jit(solution)/shard_map/ppermute | solution.py:62
  48.2 1.9 %collective-permute-start.13 = (bf16[2064,128]{1,0:T(8,128)(2,1)S(1)}, bf16[2064,128]{1,0:T(8,128)(2,1)S(1)}, u32[]{:S(2)}, u32[]{:S(2)}) collective-permute-start(bf16[2064,128]{1,0:T(8,128)(2,1)S(1)} %get-tuple-element.40.r0.refs_0_), channel_id=1, source_target_pairs={{0,6},{1,25},{2,0},{3,27},{4,2},{5,29},{6,4},{7,31},{8,14},{9,1},{... | collective-permute-start | bytes 1585160 | tf_op jit(solution)/shard_map/ppermute | solution.py:62
  50.0 2.0 %collective-permute-done.18.refs_6_ = bf16[2048,128]{1,0:T(8,128)(2,1)S(1)} collective-permute-done((bf16[2048,128]{1,0:T(8,128)(2,1)S(1)}, bf16[2048,128]{1,0:T(8,128)(2,1)S(1)}, u32[]{:S(2)}, u32[]{:S(2)}) %collective-permute-start.18) | collective-permute-done | bytes 524320 | tf_op jit(solution)/shard_map/ppermute | solution.py:62
  52.1 4.5 %collective-permute-start.19 = (bf16[16,128]{1,0:T(8,128)(2,1)S(1)}, bf16[16,128]{1,0:T(8,128)(2,1)S(1)}, u32[]{:S(2)}, u32[]{:S(2)}) collective-permute-start(bf16[16,128]{1,0:T(8,128)(2,1)S(1)} %slice.8), channel_id=1, source_target_pairs={{0,1},{1,0},{2,3},{3,2},{4,5},{5,4},{6,7},{7,6},{8,9},{9,8},{10,11... | collective-permute-start | bytes 12296 | tf_op jit(solution)/shard_map/ppermute | solution.py:62
  58.9 2.8 %collective-permute-done.11.r2 = bf16[16,128]{1,0:T(8,128)(2,1)S(1)} collective-permute-done((bf16[16,128]{1,0:T(8,128)(2,1)S(1)}, bf16[16,128]{1,0:T(8,128)(2,1)S(1)}, u32[]{:S(2)}, u32[]{:S(2)}) %collective-permute-start.11) | collective-permute-done | bytes 4128 | tf_op jit(solution)/shard_map/ppermute | solution.py:62
  61.7 2.3 %collective-permute-start.17 = (bf16[2064,128]{1,0:T(8,128)(2,1)S(1)}, bf16[2064,128]{1,0:T(8,128)(2,1)S(1)}, u32[]{:S(2)}, u32[]{:S(2)}) collective-permute-start(bf16[2064,128]{1,0:T(8,128)(2,1)S(1)} %collective-permute-done.13.r3.refs_4_), channel_id=1, source_target_pairs={{0,1},{1,0},{2,3},{3,2},{4,5},{5,4},{6,7},{7,6},{8,9},{9,8},{10,11... | collective-permute-start | bytes 1585160 | tf_op jit(solution)/shard_map/ppermute | solution.py:62
  64.7 2.4 %collective-permute-done.14.other_ref = f32[8,128]{1,0:T(8,128)S(1)} collective-permute-done((f32[8,128]{1,0:T(8,128)S(1)}, f32[8,128]{1,0:T(8,128)S(1)}, u32[]{:S(2)}, u32[]{:S(2)}) %collective-permute-start.14) | collective-permute-done | bytes 4128 | tf_op jit(solution)/shard_map/ppermute | solution.py:62
  67.0 2.5 %shard_map.78 = bf16[128,128,128]{2,1,0:T(8,128)(2,1)} custom-call(s32[4,128]{1,0:T(4,128)S(1)} %pad.8.lo_ref, s32[4,128]{1,0:T(4,128)S(1)} %pad.9.hi_ref, f32[8,128]{1,0:T(8,128)S(1)} %shard_map.77.mine_ref, f32[8,128]{1,0:T(8,128)S(1)} %collective-permute-done.14.other_ref, bf16[128,128,128]{2,1,0:T(8,128)(2,1)S(1)} %copy-done, ...), custom_call_target="tpu_custom_call" | custom-call | flops 6291456 | bytes 12582912 | tf_op jit(solution)/shard_map/pallas_call | solution.py:347
  (42 shorter events, 8.2 us)
Async XLA Ops:
  3.0 4.2 %collective-permute-start.1 = (bf16[32,128,128]{2,1,0:T(8,128)(2,1)S(1)}, bf16[32,128,128]{2,1,0:T(8,128)(2,1)S(1)}, u32[]{:S(2)}, u32[]{:S(2)}) collective-permute-start(bf16[32,128,128]{2,1,0:T(8,128)(2,1)S(1)} %get-tuple-element.31), channel_id=1, source_target_pairs={{0,1},{1,0},{2,3},{3,2},{4,5},{5,4},{6,7},{7,6},{8,9},{9,8},{10,11... | collective-permute-start | bytes 3145736 | tf_op jit(solution)/shard_map/ppermute | solution.py:62
  4.6 6.9 %collective-permute-start = (bf16[32,128,128]{2,1,0:T(8,128)(2,1)S(1)}, bf16[32,128,128]{2,1,0:T(8,128)(2,1)S(1)}, u32[]{:S(2)}, u32[]{:S(2)}) collective-permute-start(bf16[32,128,128]{2,1,0:T(8,128)(2,1)S(1)} %get-tuple-element.25), channel_id=1, source_target_pairs={{0,1},{1,0},{2,3},{3,2},{4,5},{5,4},{6,7},{7,6},{8,9},{9,8},{10,11... | collective-permute-start | bytes 3145736 | tf_op jit(solution)/shard_map/ppermute | solution.py:62
  7.5 13.6 %collective-permute-start.2 = (bf16[16,128,128]{2,1,0:T(8,128)(2,1)S(1)}, bf16[16,128,128]{2,1,0:T(8,128)(2,1)S(1)}, u32[]{:S(2)}, u32[]{:S(2)}) collective-permute-start(bf16[16,128,128]{2,1,0:T(8,128)(2,1)S(1)} %get-tuple-element.32), channel_id=1, source_target_pairs={{0,2},{1,9},{2,4},{3,11},{4,6},{5,13},{6,0},{7,15},{8,10},{9,17},{... | collective-permute-start | bytes 1572872 | tf_op jit(solution)/shard_map/ppermute | solution.py:62
  9.3 13.9 %collective-permute-start.4 = (bf16[16,128,128]{2,1,0:T(8,128)(2,1)S(1)}, bf16[16,128,128]{2,1,0:T(8,128)(2,1)S(1)}, u32[]{:S(2)}, u32[]{:S(2)}) collective-permute-start(bf16[16,128,128]{2,1,0:T(8,128)(2,1)S(1)} %get-tuple-element.33), channel_id=1, source_target_pairs={{0,6},{1,25},{2,0},{3,27},{4,2},{5,29},{6,4},{7,31},{8,14},{9,1},{... | collective-permute-start | bytes 1572872 | tf_op jit(solution)/shard_map/ppermute | solution.py:62
  11.8 13.0 %collective-permute-start.3 = (bf16[16,128,128]{2,1,0:T(8,128)(2,1)S(1)}, bf16[16,128,128]{2,1,0:T(8,128)(2,1)S(1)}, u32[]{:S(2)}, u32[]{:S(2)}) collective-permute-start(bf16[16,128,128]{2,1,0:T(8,128)(2,1)S(1)} %get-tuple-element.26.after_ref), channel_id=1, source_target_pairs={{0,4},{1,17},{2,6},{3,19},{4,0},{5,21},{6,2},{7,23},{8,12},{9,25},... | collective-permute-start | bytes 1572872 | tf_op jit(solution)/shard_map/ppermute | solution.py:62
  21.1 45.9 %copy-start = (bf16[128,128,128]{2,1,0:T(8,128)(2,1)S(1)}, bf16[128,128,128]{2,1,0:T(8,128)(2,1)}, u32[]{:S(2)}) copy-start(bf16[128,128,128]{2,1,0:T(8,128)(2,1)} %m_ref.1) | copy-start | bytes 12582916
  25.0 5.6 %collective-permute-start.5 = (bf16[8,128,128]{2,1,0:T(8,128)(2,1)S(1)}, bf16[8,128,128]{2,1,0:T(8,128)(2,1)S(1)}, u32[]{:S(2)}, u32[]{:S(2)}) collective-permute-start(bf16[8,128,128]{2,1,0:T(8,128)(2,1)S(1)} %get-tuple-element.34.a0), channel_id=1, source_target_pairs={{0,8},{1,3},{2,10},{3,1},{4,12},{5,7},{6,14},{7,5},{8,0},{9,11},{1... | collective-permute-start | bytes 786440 | tf_op jit(solution)/shard_map/ppermute | solution.py:62
  26.3 6.7 %collective-permute-start.6 = (bf16[8,128,128]{2,1,0:T(8,128)(2,1)S(1)}, bf16[8,128,128]{2,1,0:T(8,128)(2,1)S(1)}, u32[]{:S(2)}, u32[]{:S(2)}) collective-permute-start(bf16[8,128,128]{2,1,0:T(8,128)(2,1)S(1)} %get-tuple-element.35.b0), channel_id=1, source_target_pairs={{0,24},{1,7},{2,26},{3,5},{4,28},{5,3},{6,30},{7,1},{8,16},{9,15},... | collective-permute-start | bytes 786440 | tf_op jit(solution)/shard_map/ppermute | solution.py:62
  33.2 6.8 %collective-permute-start.7 = (bf16[8,128,128]{2,1,0:T(8,128)(2,1)S(1)}, bf16[8,128,128]{2,1,0:T(8,128)(2,1)S(1)}, u32[]{:S(2)}, u32[]{:S(2)}) collective-permute-start(bf16[8,128,128]{2,1,0:T(8,128)(2,1)S(1)} %get-tuple-element.36.a0), channel_id=1, source_target_pairs={{0,24},{1,7},{2,26},{3,5},{4,28},{5,3},{6,30},{7,1},{8,16},{9,15},... | collective-permute-start | bytes 786440 | tf_op jit(solution)/shard_map/ppermute | solution.py:62
  35.1 5.5 %collective-permute-start.8 = (bf16[8,128,128]{2,1,0:T(8,128)(2,1)S(1)}, bf16[8,128,128]{2,1,0:T(8,128)(2,1)S(1)}, u32[]{:S(2)}, u32[]{:S(2)}) collective-permute-start(bf16[8,128,128]{2,1,0:T(8,128)(2,1)S(1)} %get-tuple-element.37.b0), channel_id=1, source_target_pairs={{0,8},{1,3},{2,10},{3,1},{4,12},{5,7},{6,14},{7,5},{8,0},{9,11},{1... | collective-permute-start | bytes 786440 | tf_op jit(solution)/shard_map/ppermute | solution.py:62
  40.9 2.6 %collective-permute-start.9 = (f32[8,128]{1,0:T(8,128)S(1)}, f32[8,128]{1,0:T(8,128)S(1)}, u32[]{:S(2)}, u32[]{:S(2)}) collective-permute-start(f32[8,128]{1,0:T(8,128)S(1)} %get-tuple-element.39), channel_id=1, source_target_pairs={{0,32},{32,0},{64,96},{96,64},{1,33},{33,1},{65,97},{97,65},{2,34}... | collective-permute-start | bytes 12296 | tf_op jit(solution)/shard_map/ppermute | solution.py:62
  42.2 9.8 %collective-permute-start.18 = (bf16[2048,128]{1,0:T(8,128)(2,1)S(1)}, bf16[2048,128]{1,0:T(8,128)(2,1)S(1)}, u32[]{:S(2)}, u32[]{:S(2)}) collective-permute-start(bf16[2048,128]{1,0:T(8,128)(2,1)S(1)} %get-tuple-element.43), channel_id=1, source_target_pairs={{0,4},{1,17},{2,6},{3,19},{4,0},{5,21},{6,2},{7,23},{8,12},{9,25},... | collective-permute-start | bytes 1572872 | tf_op jit(solution)/shard_map/ppermute | solution.py:62
  43.5 3.7 %collective-permute-start.10 = (f32[8,128]{1,0:T(8,128)S(1)}, f32[8,128]{1,0:T(8,128)S(1)}, u32[]{:S(2)}, u32[]{:S(2)}) collective-permute-start(f32[8,128]{1,0:T(8,128)S(1)} %add.7.mine_ref), channel_id=1, source_target_pairs={{0,96},{32,64},{64,32},{96,0},{1,97},{33,65},{65,33},{97,1},{2,98}... | collective-permute-start | bytes 12296 | tf_op jit(solution)/shard_map/ppermute | solution.py:62
  47.3 14.4 %collective-permute-start.12 = (bf16[2064,128]{1,0:T(8,128)(2,1)S(1)}, bf16[2064,128]{1,0:T(8,128)(2,1)S(1)}, u32[]{:S(2)}, u32[]{:S(2)}) collective-permute-start(bf16[2064,128]{1,0:T(8,128)(2,1)S(1)} %get-tuple-element.40.r0.refs_0_), channel_id=1, source_target_pairs={{0,2},{1,9},{2,4},{3,11},{4,6},{5,13},{6,0},{7,15},{8,10},{9,17},{... | collective-permute-start | bytes 1585160 | tf_op jit(solution)/shard_map/ppermute | solution.py:62
  48.2 13.5 %collective-permute-start.13 = (bf16[2064,128]{1,0:T(8,128)(2,1)S(1)}, bf16[2064,128]{1,0:T(8,128)(2,1)S(1)}, u32[]{:S(2)}, u32[]{:S(2)}) collective-permute-start(bf16[2064,128]{1,0:T(8,128)(2,1)S(1)} %get-tuple-element.40.r0.refs_0_), channel_id=1, source_target_pairs={{0,6},{1,25},{2,0},{3,27},{4,2},{5,29},{6,4},{7,31},{8,14},{9,1},{... | collective-permute-start | bytes 1585160 | tf_op jit(solution)/shard_map/ppermute | solution.py:62
  52.1 5.3 %collective-permute-start.19 = (bf16[16,128]{1,0:T(8,128)(2,1)S(1)}, bf16[16,128]{1,0:T(8,128)(2,1)S(1)}, u32[]{:S(2)}, u32[]{:S(2)}) collective-permute-start(bf16[16,128]{1,0:T(8,128)(2,1)S(1)} %slice.8), channel_id=1, source_target_pairs={{0,1},{1,0},{2,3},{3,2},{4,5},{5,4},{6,7},{7,6},{8,9},{9,8},{10,11... | collective-permute-start | bytes 12296 | tf_op jit(solution)/shard_map/ppermute | solution.py:62
  57.4 1.3 %collective-permute-start.20 = (bf16[16,128]{1,0:T(8,128)(2,1)S(1)}, bf16[16,128]{1,0:T(8,128)(2,1)S(1)}, u32[]{:S(2)}, u32[]{:S(2)}) collective-permute-start(bf16[16,128]{1,0:T(8,128)(2,1)S(1)} %collective-permute-done.19), channel_id=1, source_target_pairs={{0,1},{1,0},{2,3},{3,2},{4,5},{5,4},{6,7},{7,6},{8,9},{9,8},{10,11... | collective-permute-start | bytes 12296 | tf_op jit(solution)/shard_map/ppermute | solution.py:62
  57.7 4.0 %collective-permute-start.11 = (bf16[16,128]{1,0:T(8,128)(2,1)S(1)}, bf16[16,128]{1,0:T(8,128)(2,1)S(1)}, u32[]{:S(2)}, u32[]{:S(2)}) collective-permute-start(bf16[16,128]{1,0:T(8,128)(2,1)S(1)} %get-tuple-element.41), channel_id=1, source_target_pairs={{0,4},{1,17},{2,6},{3,19},{4,0},{5,21},{6,2},{7,23},{8,12},{9,25},... | collective-permute-start | bytes 12296 | tf_op jit(solution)/shard_map/ppermute | solution.py:62
  57.7 7.0 %collective-permute-start.15 = (bf16[2064,128]{1,0:T(8,128)(2,1)S(1)}, bf16[2064,128]{1,0:T(8,128)(2,1)S(1)}, u32[]{:S(2)}, u32[]{:S(2)}) collective-permute-start(bf16[2064,128]{1,0:T(8,128)(2,1)S(1)} %get-tuple-element.40.r0.refs_0_), channel_id=1, source_target_pairs={{0,1},{1,0},{2,3},{3,2},{4,5},{5,4},{6,7},{7,6},{8,9},{9,8},{10,11... | collective-permute-start | bytes 1585160 | tf_op jit(solution)/shard_map/ppermute | solution.py:62
  58.7 5.3 %collective-permute-start.21 = (bf16[16,128]{1,0:T(8,128)(2,1)S(1)}, bf16[16,128]{1,0:T(8,128)(2,1)S(1)}, u32[]{:S(2)}, u32[]{:S(2)}) collective-permute-start(bf16[16,128]{1,0:T(8,128)(2,1)S(1)} %collective-permute-done.20), channel_id=1, source_target_pairs={{0,1},{1,0},{2,3},{3,2},{4,5},{5,4},{6,7},{7,6},{8,9},{9,8},{10,11... | collective-permute-start | bytes 12296 | tf_op jit(solution)/shard_map/ppermute | solution.py:62
  61.7 5.3 %collective-permute-start.17 = (bf16[2064,128]{1,0:T(8,128)(2,1)S(1)}, bf16[2064,128]{1,0:T(8,128)(2,1)S(1)}, u32[]{:S(2)}, u32[]{:S(2)}) collective-permute-start(bf16[2064,128]{1,0:T(8,128)(2,1)S(1)} %collective-permute-done.13.r3.refs_4_), channel_id=1, source_target_pairs={{0,1},{1,0},{2,3},{3,2},{4,5},{5,4},{6,7},{7,6},{8,9},{9,8},{10,11... | collective-permute-start | bytes 1585160 | tf_op jit(solution)/shard_map/ppermute | solution.py:62
  64.0 3.1 %collective-permute-start.16 = (bf16[2064,128]{1,0:T(8,128)(2,1)S(1)}, bf16[2064,128]{1,0:T(8,128)(2,1)S(1)}, u32[]{:S(2)}, u32[]{:S(2)}) collective-permute-start(bf16[2064,128]{1,0:T(8,128)(2,1)S(1)} %collective-permute-done.12.r1.refs_2_), channel_id=1, source_target_pairs={{0,1},{1,0},{2,3},{3,2},{4,5},{5,4},{6,7},{7,6},{8,9},{9,8},{10,11... | collective-permute-start | bytes 1585160 | tf_op jit(solution)/shard_map/ppermute | solution.py:62
  64.1 3.0 %collective-permute-start.22 = (bf16[2048,128]{1,0:T(8,128)(2,1)S(1)}, bf16[2048,128]{1,0:T(8,128)(2,1)S(1)}, u32[]{:S(2)}, u32[]{:S(2)}) collective-permute-start(bf16[2048,128]{1,0:T(8,128)(2,1)S(1)} %collective-permute-done.18.refs_6_), channel_id=1, source_target_pairs={{0,1},{1,0},{2,3},{3,2},{4,5},{5,4},{6,7},{7,6},{8,9},{9,8},{10,11... | collective-permute-start | bytes 1572872 | tf_op jit(solution)/shard_map/ppermute | solution.py:62
  64.5 2.5 %collective-permute-start.14 = (f32[8,128]{1,0:T(8,128)S(1)}, f32[8,128]{1,0:T(8,128)S(1)}, u32[]{:S(2)}, u32[]{:S(2)}) collective-permute-start(f32[8,128]{1,0:T(8,128)S(1)} %shard_map.77.mine_ref), channel_id=1, source_target_pairs={{0,1},{1,0},{2,3},{3,2},{4,5},{5,4},{6,7},{7,6},{8,9},{9,8},{10,11... | collective-permute-start | bytes 12296 | tf_op jit(solution)/shard_map/ppermute | solution.py:62
  (1 other events, 23.3 us)

commit v7 on v6

--- a/solution.py
+++ b/solution.py
@@ -15,7 +15,6 @@
 HALF = 8
 BLOCK = 16
 ROWS = 16
-CHAIN = 3
 GROUPS = ((1, 3), (2, 0))
 RETURNED = (0, 1, 3, 2)
 MIB = 2**20
@@ -390,14 +389,14 @@
     row_two = send(row, shift_first(2))
     row = sum_of_rows(full, row_two, by_one, by_three)
     other = send(row, swap_core())
-    blocks = [full, send(full, swap_core())]
-    for block in (after(by_one, row_two), by_three):
-        blocks += [block, send(block, swap_core())]
     token = by_two[:ROWS]
-    for _ in range(CHAIN):
+    for _ in range(2):
         token = send(token, swap_core())
     moved, token = lax.optimization_barrier((by_two, token))
-    blocks += [by_two, send(moved, swap_core()), token]
+    two = send(moved, swap_core())
+    moved, token, row_two = lax.optimization_barrier((by_one, token, row_two))
+    blocks = [full, send(full, swap_core()), by_one, send(moved, swap_core())]
+    blocks += [by_three, send(by_three, swap_core()), by_two, two, token]
     return (left[None], finish(lo, hi, row, other, momentum, blocks))
 
 

time: 69.8 us -> 69.8 us (level)
    ppermute x23 -> x22, waiting for transfers between devices: 24.1 us -> 24.3 us  [send(): return lax.ppermute(array, axis, pairs)]
    ppermute x23 -> x22, starting transfers between devices: 27.9 us -> 27.7 us  [send(): return lax.ppermute(array, axis, pairs)]
  transfers between devices with their start and end apart: 23 -> 22, of which waited for: 12 -> 12; matrix products, arithmetic and copies ran while one was open for 0% -> 0% of each run, Pallas kernels for 16% -> 16%
where the time goes in v7:
time: 69.8 us; the launch traced here: 69.5 us
  starting transfers between devices  27.7 us (40%)
  waiting for transfers between devices  24.3 us (35%)
  Pallas kernels  16.7 us (24%)
  between operations  0.73 us (1%)
    ppermute x22, starting transfers between devices, send(): return lax.ppermute(array, axis, pairs)  27.7 us
    ppermute x22, waiting for transfers between devices, send(): return lax.ppermute(array, axis, pairs)  24.3 us
    pallas_call x1, Pallas kernels, left_over(): pl.pallas_call(left_kernel, grid=(8,), in_specs=[pl.BlockSpec(memory_spac...  8.05 us
    pallas_call x2, Pallas kernels, outgoing(): pl.pallas_call(functools.partial(outgoing_kernel, side), in_specs=[pl.Blo...  4.87 us
    pallas_call x1, Pallas kernels, finish(): pl.pallas_call(final_kernel, in_specs=[whole] * (5 + len(blocks)), out_sp...  2.5 us
  transfers between devices with their start and end apart: 22, of which 12 were waited for; matrix products, arithmetic and copies ran while one was open for 0% of the time, Pallas kernels for 16%

profile of v7, /device:TPU:1, one launch (start us, length us, event | category | flops | bytes accessed | tf_op | source)
XLA Modules:
  0.0 69.5 jit_solution(2534357891707738517)
XLA Ops:
  0.6 2.4 %shard_map.69 = (bf16[32,128,128]{2,1,0:T(8,128)(2,1)S(1)}, bf16[32,128,128]{2,1,0:T(8,128)(2,1)S(1)}) custom-call(s32[1,128]{1,0:T(1,128)} %bitmap_ref.1, bf16[128,128,128]{2,1,0:T(8,128)(2,1)} %bitcast.3, bf16[128,128,128]{2,1,0:T(8,128)(2,1)} %bitcast.6), custom_call_target="tpu_custom_call" | custom-call | flops 3145728 | bytes 6291456 | tf_op jit(solution)/shard_map/pallas_call | solution.py:123
  3.0 1.6 %collective-permute-start.1 = (bf16[32,128,128]{2,1,0:T(8,128)(2,1)S(1)}, bf16[32,128,128]{2,1,0:T(8,128)(2,1)S(1)}, u32[]{:S(2)}, u32[]{:S(2)}) collective-permute-start(bf16[32,128,128]{2,1,0:T(8,128)(2,1)S(1)} %get-tuple-element.32), channel_id=1, source_target_pairs={{0,1},{1,0},{2,3},{3,2},{4,5},{5,4},{6,7},{7,6},{8,9},{9,8},{10,11... | collective-permute-start | bytes 3145736 | tf_op jit(solution)/shard_map/ppermute | solution.py:61
  4.7 2.5 %shard_map.68 = (bf16[32,128,128]{2,1,0:T(8,128)(2,1)S(1)}, bf16[32,128,128]{2,1,0:T(8,128)(2,1)S(1)}) custom-call(s32[1,128]{1,0:T(1,128)} %bitmap_ref.1, bf16[128,128,128]{2,1,0:T(8,128)(2,1)} %bitcast.4, bf16[128,128,128]{2,1,0:T(8,128)(2,1)} %bitcast.7), custom_call_target="tpu_custom_call" | custom-call | flops 3145728 | bytes 6291456 | tf_op jit(solution)/shard_map/pallas_call | solution.py:123
  7.5 1.8 %collective-permute-start.2 = (bf16[16,128,128]{2,1,0:T(8,128)(2,1)S(1)}, bf16[16,128,128]{2,1,0:T(8,128)(2,1)S(1)}, u32[]{:S(2)}, u32[]{:S(2)}) collective-permute-start(bf16[16,128,128]{2,1,0:T(8,128)(2,1)S(1)} %get-tuple-element.33), channel_id=1, source_target_pairs={{0,2},{1,9},{2,4},{3,11},{4,6},{5,13},{6,0},{7,15},{8,10},{9,17},{... | collective-permute-start | bytes 1572872 | tf_op jit(solution)/shard_map/ppermute | solution.py:61
  9.3 2.2 %collective-permute-start.4 = (bf16[16,128,128]{2,1,0:T(8,128)(2,1)S(1)}, bf16[16,128,128]{2,1,0:T(8,128)(2,1)S(1)}, u32[]{:S(2)}, u32[]{:S(2)}) collective-permute-start(bf16[16,128,128]{2,1,0:T(8,128)(2,1)S(1)} %get-tuple-element.34), channel_id=1, source_target_pairs={{0,6},{1,25},{2,0},{3,27},{4,2},{5,29},{6,4},{7,31},{8,14},{9,1},{... | collective-permute-start | bytes 1572872 | tf_op jit(solution)/shard_map/ppermute | solution.py:61
  11.8 1.3 %collective-permute-start.3 = (bf16[16,128,128]{2,1,0:T(8,128)(2,1)S(1)}, bf16[16,128,128]{2,1,0:T(8,128)(2,1)S(1)}, u32[]{:S(2)}, u32[]{:S(2)}) collective-permute-start(bf16[16,128,128]{2,1,0:T(8,128)(2,1)S(1)} %get-tuple-element.27.after_ref), channel_id=1, source_target_pairs={{0,4},{1,17},{2,6},{3,19},{4,0},{5,21},{6,2},{7,23},{8,12},{9,25},... | collective-permute-start | bytes 1572872 | tf_op jit(solution)/shard_map/ppermute | solution.py:61
  13.1 8.1 %shard_map.71 = (bf16[128,128,128]{2,1,0:T(8,128)(2,1)}, f32[8,128]{1,0:T(8,128)S(1)}) custom-call(bf16[16,128,128]{2,1,0:T(8,128)(2,1)S(1)} %get-tuple-element.27.after_ref, s32[1,128]{1,0:T(1,128)} %bitmap_ref.1, bf16[128,128,128]{2,1,0:T(8,128)(2,1)} %bitcast.5, bf16[128,128,128]{2,1,0:T(8,128)(2,1)} %bitcast.8), custom_call_target="tpu_custom_call" | custom-call | flops 6291456 | bytes 12582912 | tf_op jit(solution)/shard_map/pallas_call | solution.py:149
  21.1 2.1 %collective-permute-done.4.r3 = bf16[16,128,128]{2,1,0:T(8,128)(2,1)S(1)} collective-permute-done((bf16[16,128,128]{2,1,0:T(8,128)(2,1)S(1)}, bf16[16,128,128]{2,1,0:T(8,128)(2,1)S(1)}, u32[]{:S(2)}, u32[]{:S(2)}) %collective-permute-start.4) | collective-permute-done | bytes 524320 | tf_op jit(solution)/shard_map/ppermute | solution.py:61
  23.2 1.5 %collective-permute-done.3.r2 = bf16[16,128,128]{2,1,0:T(8,128)(2,1)S(1)} collective-permute-done((bf16[16,128,128]{2,1,0:T(8,128)(2,1)S(1)}, bf16[16,128,128]{2,1,0:T(8,128)(2,1)S(1)}, u32[]{:S(2)}, u32[]{:S(2)}) %collective-permute-start.3) | collective-permute-done | bytes 524320 | tf_op jit(solution)/shard_map/ppermute | solution.py:61
  25.0 1.3 %collective-permute-start.5 = (bf16[8,128,128]{2,1,0:T(8,128)(2,1)S(1)}, bf16[8,128,128]{2,1,0:T(8,128)(2,1)S(1)}, u32[]{:S(2)}, u32[]{:S(2)}) collective-permute-start(bf16[8,128,128]{2,1,0:T(8,128)(2,1)S(1)} %get-tuple-element.35.a0), channel_id=1, source_target_pairs={{0,8},{1,3},{2,10},{3,1},{4,12},{5,7},{6,14},{7,5},{8,0},{9,11},{1... | collective-permute-start | bytes 786440 | tf_op jit(solution)/shard_map/ppermute | solution.py:61
  26.3 1.8 %collective-permute-start.6 = (bf16[8,128,128]{2,1,0:T(8,128)(2,1)S(1)}, bf16[8,128,128]{2,1,0:T(8,128)(2,1)S(1)}, u32[]{:S(2)}, u32[]{:S(2)}) collective-permute-start(bf16[8,128,128]{2,1,0:T(8,128)(2,1)S(1)} %get-tuple-element.36.b0), channel_id=1, source_target_pairs={{0,24},{1,7},{2,26},{3,5},{4,28},{5,3},{6,30},{7,1},{8,16},{9,15},... | collective-permute-start | bytes 786440 | tf_op jit(solution)/shard_map/ppermute | solution.py:61
  28.2 2.5 %collective-permute-done.5.a1 = bf16[8,128,128]{2,1,0:T(8,128)(2,1)S(1)} collective-permute-done((bf16[8,128,128]{2,1,0:T(8,128)(2,1)S(1)}, bf16[8,128,128]{2,1,0:T(8,128)(2,1)S(1)}, u32[]{:S(2)}, u32[]{:S(2)}) %collective-permute-start.5) | collective-permute-done | bytes 262176 | tf_op jit(solution)/shard_map/ppermute | solution.py:61
  30.6 2.4 %collective-permute-done.6.b1 = bf16[8,128,128]{2,1,0:T(8,128)(2,1)S(1)} collective-permute-done((bf16[8,128,128]{2,1,0:T(8,128)(2,1)S(1)}, bf16[8,128,128]{2,1,0:T(8,128)(2,1)S(1)}, u32[]{:S(2)}, u32[]{:S(2)}) %collective-permute-start.6) | collective-permute-done | bytes 262176 | tf_op jit(solution)/shard_map/ppermute | solution.py:61
  33.2 1.9 %collective-permute-start.7 = (bf16[8,128,128]{2,1,0:T(8,128)(2,1)S(1)}, bf16[8,128,128]{2,1,0:T(8,128)(2,1)S(1)}, u32[]{:S(2)}, u32[]{:S(2)}) collective-permute-start(bf16[8,128,128]{2,1,0:T(8,128)(2,1)S(1)} %get-tuple-element.37.a0), channel_id=1, source_target_pairs={{0,24},{1,7},{2,26},{3,5},{4,28},{5,3},{6,30},{7,1},{8,16},{9,15},... | collective-permute-start | bytes 786440 | tf_op jit(solution)/shard_map/ppermute | solution.py:61
  35.2 4.8 %collective-permute-done.7.a1 = bf16[8,128,128]{2,1,0:T(8,128)(2,1)S(1)} collective-permute-done((bf16[8,128,128]{2,1,0:T(8,128)(2,1)S(1)}, bf16[8,128,128]{2,1,0:T(8,128)(2,1)S(1)}, u32[]{:S(2)}, u32[]{:S(2)}) %collective-permute-start.7) | collective-permute-done | bytes 262176 | tf_op jit(solution)/shard_map/ppermute | solution.py:61
  40.9 1.4 %collective-permute-start.9 = (f32[8,128]{1,0:T(8,128)S(1)}, f32[8,128]{1,0:T(8,128)S(1)}, u32[]{:S(2)}, u32[]{:S(2)}) collective-permute-start(f32[8,128]{1,0:T(8,128)S(1)} %get-tuple-element.40), channel_id=1, source_target_pairs={{0,32},{32,0},{64,96},{96,64},{1,33},{33,1},{65,97},{97,65},{2,34}... | collective-permute-start | bytes 12296 | tf_op jit(solution)/shard_map/ppermute | solution.py:61
  43.5 2.7 %collective-permute-start.10 = (f32[8,128]{1,0:T(8,128)S(1)}, f32[8,128]{1,0:T(8,128)S(1)}, u32[]{:S(2)}, u32[]{:S(2)}) collective-permute-start(f32[8,128]{1,0:T(8,128)S(1)} %add.7.mine_ref), channel_id=1, source_target_pairs={{0,96},{32,64},{64,32},{96,0},{1,97},{33,65},{65,33},{97,1},{2,98}... | collective-permute-start | bytes 12296 | tf_op jit(solution)/shard_map/ppermute | solution.py:61
  48.2 1.9 %collective-permute-start.13 = (bf16[2064,128]{1,0:T(8,128)(2,1)S(1)}, bf16[2064,128]{1,0:T(8,128)(2,1)S(1)}, u32[]{:S(2)}, u32[]{:S(2)}) collective-permute-start(bf16[2064,128]{1,0:T(8,128)(2,1)S(1)} %get-tuple-element.41.r0.refs_0_), channel_id=1, source_target_pairs={{0,6},{1,25},{2,0},{3,27},{4,2},{5,29},{6,4},{7,31},{8,14},{9,1},{... | collective-permute-start | bytes 1585160 | tf_op jit(solution)/shard_map/ppermute | solution.py:61
  50.0 2.0 %collective-permute-done.16.refs_6_ = bf16[2048,128]{1,0:T(8,128)(2,1)S(1)} collective-permute-done((bf16[2048,128]{1,0:T(8,128)(2,1)S(1)}, bf16[2048,128]{1,0:T(8,128)(2,1)S(1)}, u32[]{:S(2)}, u32[]{:S(2)}) %collective-permute-start.16) | collective-permute-done | bytes 524320 | tf_op jit(solution)/shard_map/ppermute | solution.py:61
  52.1 4.5 %collective-permute-start.17 = (bf16[16,128]{1,0:T(8,128)(2,1)S(1)}, bf16[16,128]{1,0:T(8,128)(2,1)S(1)}, u32[]{:S(2)}, u32[]{:S(2)}) collective-permute-start(bf16[16,128]{1,0:T(8,128)(2,1)S(1)} %slice.8), channel_id=1, source_target_pairs={{0,1},{1,0},{2,3},{3,2},{4,5},{5,4},{6,7},{7,6},{8,9},{9,8},{10,11... | collective-permute-start | bytes 12296 | tf_op jit(solution)/shard_map/ppermute | solution.py:61
  58.7 3.0 %collective-permute-done.11.r2 = bf16[16,128]{1,0:T(8,128)(2,1)S(1)} collective-permute-done((bf16[16,128]{1,0:T(8,128)(2,1)S(1)}, bf16[16,128]{1,0:T(8,128)(2,1)S(1)}, u32[]{:S(2)}, u32[]{:S(2)}) %collective-permute-start.11) | collective-permute-done | bytes 4128 | tf_op jit(solution)/shard_map/ppermute | solution.py:61
  61.7 2.3 %collective-permute-start.20 = (bf16[2064,128]{1,0:T(8,128)(2,1)S(1)}, bf16[2064,128]{1,0:T(8,128)(2,1)S(1)}, u32[]{:S(2)}, u32[]{:S(2)}) collective-permute-start(bf16[2064,128]{1,0:T(8,128)(2,1)S(1)} %collective-permute-done.13.r3.refs_4_), channel_id=1, source_target_pairs={{0,1},{1,0},{2,3},{3,2},{4,5},{5,4},{6,7},{7,6},{8,9},{9,8},{10,11... | collective-permute-start | bytes 1585160 | tf_op jit(solution)/shard_map/ppermute | solution.py:61
  64.7 2.4 %collective-permute-done.14.other_ref = f32[8,128]{1,0:T(8,128)S(1)} collective-permute-done((f32[8,128]{1,0:T(8,128)S(1)}, f32[8,128]{1,0:T(8,128)S(1)}, u32[]{:S(2)}, u32[]{:S(2)}) %collective-permute-start.14) | collective-permute-done | bytes 4128 | tf_op jit(solution)/shard_map/ppermute | solution.py:61
  67.0 2.5 %shard_map.78 = bf16[128,128,128]{2,1,0:T(8,128)(2,1)} custom-call(s32[4,128]{1,0:T(4,128)S(1)} %pad.8.lo_ref, s32[4,128]{1,0:T(4,128)S(1)} %pad.9.hi_ref, f32[8,128]{1,0:T(8,128)S(1)} %shard_map.77.mine_ref, f32[8,128]{1,0:T(8,128)S(1)} %collective-permute-done.14.other_ref, bf16[128,128,128]{2,1,0:T(8,128)(2,1)S(1)} %copy-done, ...), custom_call_target="tpu_custom_call" | custom-call | flops 6291456 | bytes 12582912 | tf_op jit(solution)/shard_map/pallas_call | solution.py:346
  (40 shorter events, 8.1 us)
Async XLA Ops:
  3.0 4.2 %collective-permute-start.1 = (bf16[32,128,128]{2,1,0:T(8,128)(2,1)S(1)}, bf16[32,128,128]{2,1,0:T(8,128)(2,1)S(1)}, u32[]{:S(2)}, u32[]{:S(2)}) collective-permute-start(bf16[32,128,128]{2,1,0:T(8,128)(2,1)S(1)} %get-tuple-element.32), channel_id=1, source_target_pairs={{0,1},{1,0},{2,3},{3,2},{4,5},{5,4},{6,7},{7,6},{8,9},{9,8},{10,11... | collective-permute-start | bytes 3145736 | tf_op jit(solution)/shard_map/ppermute | solution.py:61
  4.6 6.9 %collective-permute-start = (bf16[32,128,128]{2,1,0:T(8,128)(2,1)S(1)}, bf16[32,128,128]{2,1,0:T(8,128)(2,1)S(1)}, u32[]{:S(2)}, u32[]{:S(2)}) collective-permute-start(bf16[32,128,128]{2,1,0:T(8,128)(2,1)S(1)} %get-tuple-element.26), channel_id=1, source_target_pairs={{0,1},{1,0},{2,3},{3,2},{4,5},{5,4},{6,7},{7,6},{8,9},{9,8},{10,11... | collective-permute-start | bytes 3145736 | tf_op jit(solution)/shard_map/ppermute | solution.py:61
  7.5 13.6 %collective-permute-start.2 = (bf16[16,128,128]{2,1,0:T(8,128)(2,1)S(1)}, bf16[16,128,128]{2,1,0:T(8,128)(2,1)S(1)}, u32[]{:S(2)}, u32[]{:S(2)}) collective-permute-start(bf16[16,128,128]{2,1,0:T(8,128)(2,1)S(1)} %get-tuple-element.33), channel_id=1, source_target_pairs={{0,2},{1,9},{2,4},{3,11},{4,6},{5,13},{6,0},{7,15},{8,10},{9,17},{... | collective-permute-start | bytes 1572872 | tf_op jit(solution)/shard_map/ppermute | solution.py:61
  9.3 13.9 %collective-permute-start.4 = (bf16[16,128,128]{2,1,0:T(8,128)(2,1)S(1)}, bf16[16,128,128]{2,1,0:T(8,128)(2,1)S(1)}, u32[]{:S(2)}, u32[]{:S(2)}) collective-permute-start(bf16[16,128,128]{2,1,0:T(8,128)(2,1)S(1)} %get-tuple-element.34), channel_id=1, source_target_pairs={{0,6},{1,25},{2,0},{3,27},{4,2},{5,29},{6,4},{7,31},{8,14},{9,1},{... | collective-permute-start | bytes 1572872 | tf_op jit(solution)/shard_map/ppermute | solution.py:61
  11.8 23.3 %copy-start.1 = (s32[4,32]{1,0:T(4,128)S(1)}, s32[4,32]{1,0:T(4,128)}, u32[]{:S(2)}) copy-start(s32[4,32]{1,0:T(4,128)} %param.9) | copy-start | bytes 1540
  11.8 13.0 %collective-permute-start.3 = (bf16[16,128,128]{2,1,0:T(8,128)(2,1)S(1)}, bf16[16,128,128]{2,1,0:T(8,128)(2,1)S(1)}, u32[]{:S(2)}, u32[]{:S(2)}) collective-permute-start(bf16[16,128,128]{2,1,0:T(8,128)(2,1)S(1)} %get-tuple-element.27.after_ref), channel_id=1, source_target_pairs={{0,4},{1,17},{2,6},{3,19},{4,0},{5,21},{6,2},{7,23},{8,12},{9,25},... | collective-permute-start | bytes 1572872 | tf_op jit(solution)/shard_map/ppermute | solution.py:61
  21.1 45.9 %copy-start = (bf16[128,128,128]{2,1,0:T(8,128)(2,1)S(1)}, bf16[128,128,128]{2,1,0:T(8,128)(2,1)}, u32[]{:S(2)}) copy-start(bf16[128,128,128]{2,1,0:T(8,128)(2,1)} %m_ref.1) | copy-start | bytes 12582916
  25.0 5.6 %collective-permute-start.5 = (bf16[8,128,128]{2,1,0:T(8,128)(2,1)S(1)}, bf16[8,128,128]{2,1,0:T(8,128)(2,1)S(1)}, u32[]{:S(2)}, u32[]{:S(2)}) collective-permute-start(bf16[8,128,128]{2,1,0:T(8,128)(2,1)S(1)} %get-tuple-element.35.a0), channel_id=1, source_target_pairs={{0,8},{1,3},{2,10},{3,1},{4,12},{5,7},{6,14},{7,5},{8,0},{9,11},{1... | collective-permute-start | bytes 786440 | tf_op jit(solution)/shard_map/ppermute | solution.py:61
  26.3 6.7 %collective-permute-start.6 = (bf16[8,128,128]{2,1,0:T(8,128)(2,1)S(1)}, bf16[8,128,128]{2,1,0:T(8,128)(2,1)S(1)}, u32[]{:S(2)}, u32[]{:S(2)}) collective-permute-start(bf16[8,128,128]{2,1,0:T(8,128)(2,1)S(1)} %get-tuple-element.36.b0), channel_id=1, source_target_pairs={{0,24},{1,7},{2,26},{3,5},{4,28},{5,3},{6,30},{7,1},{8,16},{9,15},... | collective-permute-start | bytes 786440 | tf_op jit(solution)/shard_map/ppermute | solution.py:61
  33.2 6.8 %collective-permute-start.7 = (bf16[8,128,128]{2,1,0:T(8,128)(2,1)S(1)}, bf16[8,128,128]{2,1,0:T(8,128)(2,1)S(1)}, u32[]{:S(2)}, u32[]{:S(2)}) collective-permute-start(bf16[8,128,128]{2,1,0:T(8,128)(2,1)S(1)} %get-tuple-element.37.a0), channel_id=1, source_target_pairs={{0,24},{1,7},{2,26},{3,5},{4,28},{5,3},{6,30},{7,1},{8,16},{9,15},... | collective-permute-start | bytes 786440 | tf_op jit(solution)/shard_map/ppermute | solution.py:61
  35.1 5.5 %collective-permute-start.8 = (bf16[8,128,128]{2,1,0:T(8,128)(2,1)S(1)}, bf16[8,128,128]{2,1,0:T(8,128)(2,1)S(1)}, u32[]{:S(2)}, u32[]{:S(2)}) collective-permute-start(bf16[8,128,128]{2,1,0:T(8,128)(2,1)S(1)} %get-tuple-element.38.b0), channel_id=1, source_target_pairs={{0,8},{1,3},{2,10},{3,1},{4,12},{5,7},{6,14},{7,5},{8,0},{9,11},{1... | collective-permute-start | bytes 786440 | tf_op jit(solution)/shard_map/ppermute | solution.py:61
  40.9 2.6 %collective-permute-start.9 = (f32[8,128]{1,0:T(8,128)S(1)}, f32[8,128]{1,0:T(8,128)S(1)}, u32[]{:S(2)}, u32[]{:S(2)}) collective-permute-start(f32[8,128]{1,0:T(8,128)S(1)} %get-tuple-element.40), channel_id=1, source_target_pairs={{0,32},{32,0},{64,96},{96,64},{1,33},{33,1},{65,97},{97,65},{2,34}... | collective-permute-start | bytes 12296 | tf_op jit(solution)/shard_map/ppermute | solution.py:61
  42.2 9.8 %collective-permute-start.16 = (bf16[2048,128]{1,0:T(8,128)(2,1)S(1)}, bf16[2048,128]{1,0:T(8,128)(2,1)S(1)}, u32[]{:S(2)}, u32[]{:S(2)}) collective-permute-start(bf16[2048,128]{1,0:T(8,128)(2,1)S(1)} %get-tuple-element.43), channel_id=1, source_target_pairs={{0,4},{1,17},{2,6},{3,19},{4,0},{5,21},{6,2},{7,23},{8,12},{9,25},... | collective-permute-start | bytes 1572872 | tf_op jit(solution)/shard_map/ppermute | solution.py:61
  43.5 3.7 %collective-permute-start.10 = (f32[8,128]{1,0:T(8,128)S(1)}, f32[8,128]{1,0:T(8,128)S(1)}, u32[]{:S(2)}, u32[]{:S(2)}) collective-permute-start(f32[8,128]{1,0:T(8,128)S(1)} %add.7.mine_ref), channel_id=1, source_target_pairs={{0,96},{32,64},{64,32},{96,0},{1,97},{33,65},{65,33},{97,1},{2,98}... | collective-permute-start | bytes 12296 | tf_op jit(solution)/shard_map/ppermute | solution.py:61
  47.3 14.4 %collective-permute-start.12 = (bf16[2064,128]{1,0:T(8,128)(2,1)S(1)}, bf16[2064,128]{1,0:T(8,128)(2,1)S(1)}, u32[]{:S(2)}, u32[]{:S(2)}) collective-permute-start(bf16[2064,128]{1,0:T(8,128)(2,1)S(1)} %get-tuple-element.41.r0.refs_0_), channel_id=1, source_target_pairs={{0,2},{1,9},{2,4},{3,11},{4,6},{5,13},{6,0},{7,15},{8,10},{9,17},{... | collective-permute-start | bytes 1585160 | tf_op jit(solution)/shard_map/ppermute | solution.py:61
  48.2 13.5 %collective-permute-start.13 = (bf16[2064,128]{1,0:T(8,128)(2,1)S(1)}, bf16[2064,128]{1,0:T(8,128)(2,1)S(1)}, u32[]{:S(2)}, u32[]{:S(2)}) collective-permute-start(bf16[2064,128]{1,0:T(8,128)(2,1)S(1)} %get-tuple-element.41.r0.refs_0_), channel_id=1, source_target_pairs={{0,6},{1,25},{2,0},{3,27},{4,2},{5,29},{6,4},{7,31},{8,14},{9,1},{... | collective-permute-start | bytes 1585160 | tf_op jit(solution)/shard_map/ppermute | solution.py:61
  52.1 5.3 %collective-permute-start.17 = (bf16[16,128]{1,0:T(8,128)(2,1)S(1)}, bf16[16,128]{1,0:T(8,128)(2,1)S(1)}, u32[]{:S(2)}, u32[]{:S(2)}) collective-permute-start(bf16[16,128]{1,0:T(8,128)(2,1)S(1)} %slice.8), channel_id=1, source_target_pairs={{0,1},{1,0},{2,3},{3,2},{4,5},{5,4},{6,7},{7,6},{8,9},{9,8},{10,11... | collective-permute-start | bytes 12296 | tf_op jit(solution)/shard_map/ppermute | solution.py:61
  57.4 1.3 %collective-permute-start.18 = (bf16[16,128]{1,0:T(8,128)(2,1)S(1)}, bf16[16,128]{1,0:T(8,128)(2,1)S(1)}, u32[]{:S(2)}, u32[]{:S(2)}) collective-permute-start(bf16[16,128]{1,0:T(8,128)(2,1)S(1)} %collective-permute-done.17), channel_id=1, source_target_pairs={{0,1},{1,0},{2,3},{3,2},{4,5},{5,4},{6,7},{7,6},{8,9},{9,8},{10,11... | collective-permute-start | bytes 12296 | tf_op jit(solution)/shard_map/ppermute | solution.py:61
  57.7 4.0 %collective-permute-start.11 = (bf16[16,128]{1,0:T(8,128)(2,1)S(1)}, bf16[16,128]{1,0:T(8,128)(2,1)S(1)}, u32[]{:S(2)}, u32[]{:S(2)}) collective-permute-start(bf16[16,128]{1,0:T(8,128)(2,1)S(1)} %get-tuple-element.42), channel_id=1, source_target_pairs={{0,4},{1,17},{2,6},{3,19},{4,0},{5,21},{6,2},{7,23},{8,12},{9,25},... | collective-permute-start | bytes 12296 | tf_op jit(solution)/shard_map/ppermute | solution.py:61
  57.7 6.9 %collective-permute-start.15 = (bf16[2064,128]{1,0:T(8,128)(2,1)S(1)}, bf16[2064,128]{1,0:T(8,128)(2,1)S(1)}, u32[]{:S(2)}, u32[]{:S(2)}) collective-permute-start(bf16[2064,128]{1,0:T(8,128)(2,1)S(1)} %get-tuple-element.41.r0.refs_0_), channel_id=1, source_target_pairs={{0,1},{1,0},{2,3},{3,2},{4,5},{5,4},{6,7},{7,6},{8,9},{9,8},{10,11... | collective-permute-start | bytes 1585160 | tf_op jit(solution)/shard_map/ppermute | solution.py:61
  61.7 5.3 %collective-permute-start.20 = (bf16[2064,128]{1,0:T(8,128)(2,1)S(1)}, bf16[2064,128]{1,0:T(8,128)(2,1)S(1)}, u32[]{:S(2)}, u32[]{:S(2)}) collective-permute-start(bf16[2064,128]{1,0:T(8,128)(2,1)S(1)} %collective-permute-done.13.r3.refs_4_), channel_id=1, source_target_pairs={{0,1},{1,0},{2,3},{3,2},{4,5},{5,4},{6,7},{7,6},{8,9},{9,8},{10,11... | collective-permute-start | bytes 1585160 | tf_op jit(solution)/shard_map/ppermute | solution.py:61
  64.0 3.1 %collective-permute-start.19 = (bf16[2064,128]{1,0:T(8,128)(2,1)S(1)}, bf16[2064,128]{1,0:T(8,128)(2,1)S(1)}, u32[]{:S(2)}, u32[]{:S(2)}) collective-permute-start(bf16[2064,128]{1,0:T(8,128)(2,1)S(1)} %collective-permute-done.12.r1.refs_2_), channel_id=1, source_target_pairs={{0,1},{1,0},{2,3},{3,2},{4,5},{5,4},{6,7},{7,6},{8,9},{9,8},{10,11... | collective-permute-start | bytes 1585160 | tf_op jit(solution)/shard_map/ppermute | solution.py:61
  64.1 3.0 %collective-permute-start.21 = (bf16[2048,128]{1,0:T(8,128)(2,1)S(1)}, bf16[2048,128]{1,0:T(8,128)(2,1)S(1)}, u32[]{:S(2)}, u32[]{:S(2)}) collective-permute-start(bf16[2048,128]{1,0:T(8,128)(2,1)S(1)} %collective-permute-done.16.refs_6_), channel_id=1, source_target_pairs={{0,1},{1,0},{2,3},{3,2},{4,5},{5,4},{6,7},{7,6},{8,9},{9,8},{10,11... | collective-permute-start | bytes 1572872 | tf_op jit(solution)/shard_map/ppermute | solution.py:61
  64.5 2.5 %collective-permute-start.14 = (f32[8,128]{1,0:T(8,128)S(1)}, f32[8,128]{1,0:T(8,128)S(1)}, u32[]{:S(2)}, u32[]{:S(2)}) collective-permute-start(f32[8,128]{1,0:T(8,128)S(1)} %shard_map.77.mine_ref), channel_id=1, source_target_pairs={{0,1},{1,0},{2,3},{3,2},{4,5},{5,4},{6,7},{7,6},{8,9},{9,8},{10,11... | collective-permute-start | bytes 12296 | tf_op jit(solution)/shard_map/ppermute | solution.py:61
